TPU v7x, 32 devices: a whole 2x2x4 slice. The times are simulated.
32 devices in a mesh: groups: 2 (over y), atoms: 4 (over z), states: 2 (over x), sub: 2 (over core).
Axes of the slice: x: 2, y: 2, z: 4, core: 2. Of those that a mesh axis runs over, the one named last changes fastest.
Arguments:
- coeffs: float32 [16384, 2048], P(('groups', 'atoms', 'sub'), 'states'), parts along dimension 0, may hold values from -0.15 to 0.15
- occup: float32 [4096], P(('groups', 'states')), parts along dimension 0, may hold values from 0.1 to 2
- energies: float32 [4096], P(('groups', 'states')), parts along dimension 0, may hold values from -1.5 to 0.5
- nbr: int32 [16, 4096], P(None, ('groups', 'atoms', 'sub')), parts along dimension 1, may hold values from -1 to 2047, as said below
- dham: float32 [48, 16, 4096], P(None, None, ('groups', 'atoms', 'sub')), parts along dimension 2, may hold values from -6 to 6
- dovl: float32 [48, 16, 4096], P(None, None, ('groups', 'atoms', 'sub')), parts along dimension 2, may hold values from -6 to 6
Outputs:
- forces: float32 [3, 4096], P(None, ('groups', 'atoms', 'sub')), parts along dimension 1
There are 2 independent parts, one for each index of `groups`. A program takes and returns all parts, laid end to end along the dimension named above; each array names one. Nothing has to cross between parts.
Inputs may be any that keep to these rules, and one draw needn't show every extreme that they name: Each live nbr[n, i] lies in i+1 .. i+128, and the live entries of an atom are distinct. Each atom has from half of 16 to 16 live slots, which come first; near the end of the slab a target past the last atom is dropped to -1 in whatever slot it stands, which can leave -1 between live slots. Atom 0 has all 16 slots live and its neighbour i+128.
All inputs are finite; a program needn't handle non-finite values.
Results may differ from a plain program's by a relative error of at most 0.0001.
Values sent between devices are 32-bit elements; how exact they have to be, the bound alone decides.
No kernel may reach another device: no remote copies, remote signals or barrier semaphores. Data moves between devices by JAX's collectives and lax.ppermute only.
A program may use at most 64 MiB of HBM per device.

v0:
```python
import jax
import jax.numpy as jnp
from jax import lax
from jax.sharding import PartitionSpec as P


def shifted(value, axis, steps):
    count = lax.axis_size(axis)
    first, last = (max(0, -steps), min(count, count - steps))
    return lax.ppermute(value, axis, [(source, source + steps) for source in range(first, last)])


def pair_forces(
    window, weights, deriv_h, deriv_s, neighbours, window_start, atom_count, block_atoms, halo_atoms
):
    states_local = window.shape[1]
    accum = jnp.zeros((3, atom_count + halo_atoms), jnp.float32)
    span = block_atoms + halo_atoms

    def step(block_index, accum):
        first_atom = block_index * block_atoms
        own_rows = lax.dynamic_slice_in_dim(window, first_atom * 4, block_atoms * 4, 0)
        near_rows = lax.dynamic_slice_in_dim(window, first_atom * 4, span * 4, 0)
        near_rows = (
            near_rows.reshape(span, 4, states_local)
            .transpose(1, 0, 2)
            .reshape(4 * span, states_local)
        )
        scaled = own_rows[None] * weights[:, None, :]
        gram_blocks = jnp.einsum("xrs,cs->xrc", scaled, near_rows, precision=lax.Precision.HIGHEST)
        gram_blocks = gram_blocks.reshape(2, block_atoms, 4, 4, span)
        listed = lax.dynamic_slice_in_dim(neighbours, first_atom, block_atoms, 1)
        alive = listed >= 0
        relative = jnp.where(alive, listed - window_start - first_atom, 0)
        onehot = (
            (relative[:, :, None] == jnp.arange(span, dtype=jnp.int32)[None, None, :])
            & alive[:, :, None]
        ).astype(jnp.float32)
        picked = jnp.einsum(
            "xiabj,nij->xabni", gram_blocks, onehot, precision=lax.Precision.HIGHEST
        )
        block_h = lax.dynamic_slice_in_dim(deriv_h, first_atom, block_atoms, 4)
        block_s = lax.dynamic_slice_in_dim(deriv_s, first_atom, block_atoms, 4)
        pair_terms = jnp.einsum(
            "abni,kabni->kni", picked[0], block_h, precision=lax.Precision.HIGHEST
        )
        pair_terms = pair_terms - jnp.einsum(
            "abni,kabni->kni", picked[1], block_s, precision=lax.Precision.HIGHEST
        )
        pair_terms = jnp.where(alive[None], pair_terms, 0.0)
        self_part = -2.0 * jnp.sum(pair_terms, axis=1)
        spread_terms = 2.0 * jnp.einsum(
            "kni,nij->kj", pair_terms, onehot, precision=lax.Precision.HIGHEST
        )
        window_part = lax.dynamic_slice_in_dim(accum, first_atom, span, 1) + spread_terms
        window_part = window_part.at[:, :block_atoms].add(self_part)
        return lax.dynamic_update_slice_in_dim(accum, window_part, first_atom, 1)

    return lax.fori_loop(0, atom_count // block_atoms, step, accum)


def local(coeffs, occup, energies, nbr, dham, dovl):
    atom_count = nbr.shape[1]
    slot_count = nbr.shape[0]
    halo_atoms = atom_count // 2
    block_atoms = min(atom_count, 128)
    weights = jnp.stack([occup, occup * energies])
    atom_start = lax.axis_index(("atoms", "sub")) * atom_count
    upper_rows = shifted(coeffs[: 4 * halo_atoms], ("atoms", "sub"), -1)
    window = jnp.concatenate([coeffs, upper_rows], 0)
    deriv_h = dham.reshape(3, 4, 4, slot_count, atom_count)
    deriv_s = dovl.reshape(3, 4, 4, slot_count, atom_count)
    accum = pair_forces(
        window, weights, deriv_h, deriv_s, nbr, atom_start, atom_count, block_atoms, halo_atoms
    )
    returned = shifted(accum[:, atom_count:], ("atoms", "sub"), 1)
    own_force = accum[:, :atom_count] + jnp.pad(returned, ((0, 0), (0, atom_count - halo_atoms)))
    return lax.psum(own_force, "states")


def solution(mesh):
    in_specs = (
        P(("groups", "atoms", "sub"), "states"),
        P(("groups", "states")),
        P(("groups", "states")),
        P(None, ("groups", "atoms", "sub")),
        P(None, None, ("groups", "atoms", "sub")),
        P(None, None, ("groups", "atoms", "sub")),
    )
    out_specs = P(None, ("groups", "atoms", "sub"))
    return jax.shard_map(local, mesh=mesh, in_specs=in_specs, out_specs=out_specs, check_vma=False)
```

profile of v0, /device:TPU:1, one launch (start us, length us, event | category | flops | bytes accessed | tf_op | source)
XLA Modules:
  0.0 135.2 jit_solution(1883645513082138528)
XLA Ops:
  0.0 1.8 %slice.64 = f32[512,1024]{1,0:T(8,128)S(1)} slice(f32[1024,1024]{1,0:T(8,128)} %param.10), slice={[0:512], [0:1024]} | slice | bytes 4194304 | tf_op jit(solution)/shard_map/slice | solution.py:69
  1.8 2.0 %collective-permute-start = (f32[512,1024]{1,0:T(8,128)S(1)}, f32[512,1024]{1,0:T(8,128)}, u32[]{:S(2)}, u32[]{:S(2)}) collective-permute-start(f32[512,1024]{1,0:T(8,128)S(1)} %slice.64), channel_id=1, source_target_pairs={{1,0},{4,1},{5,4},{8,5},{9,8},{12,9},{13,12},{3,2},{6,3},{7,6},{10... | collective-permute-start | bytes 6291464 | tf_op jit(solution)/shard_map/ppermute | solution.py:10
  3.8 26.4 %collective-permute-done = f32[512,1024]{1,0:T(8,128)} collective-permute-done((f32[512,1024]{1,0:T(8,128)S(1)}, f32[512,1024]{1,0:T(8,128)}, u32[]{:S(2)}, u32[]{:S(2)}) %collective-permute-start) | collective-permute-done | bytes 2097184 | tf_op jit(solution)/shard_map/ppermute | solution.py:10
  30.2 6.6 %pad_maximum_fusion = f32[1536,1024]{1,0:T(8,128)} fusion(f32[512,1024]{1,0:T(8,128)} %collective-permute-done, f32[1024,1024]{1,0:T(8,128)} %param.10), kind=kLoop, calls=%fused_computation.34 | loop fusion | flops 1572864 | bytes 12582912 | tf_op jit(solution)/shard_map/concatenate | solution.py:70
  36.8 91.0 %while.16 = (s32[]{:T(128)}, f32[3,384]{1,0:T(4,128)S(1)}, s32[16,256]{1,0:T(8,128)S(1)}, f32[3,4,4,16,256]{4,3,2,1,0:T(8,128)S(1)}, s32[]{:T(128)}, /*index=5*/...) while((s32[]{:T(128)}, f32[3,384]{1,0:T(4,128)S(1)}, ...), condition=%wide.region_3.4_spmd, body=%wide.region_0.3_spmd.sunk | while | flops 13108671488 | bytes 68641600 | solution.py:59
  36.8 4.9 %constant_dynamic-slice_fusion.4 = f32[1024,1024]{1,0:T(8,128)} fusion(f32[1536,1024]{1,0:T(8,128)} %get-tuple-element.345, s32[]{:T(128)S(6)} %select_n.76), kind=kLoop, calls=%fused_computation.30.clone.1 | loop fusion | bytes 8388612 | tf_op jit(solution)/shard_map/while/body/eval_jaxpr/dynamic_slice | solution.py:23
  41.7 5.2 %reshape.97 = f32[256,4,1024]{2,1,0:T(4,128)} reshape(f32[1024,1024]{1,0:T(8,128)} %constant_dynamic-slice_fusion.4) | data formatting | bytes 8388608 | tf_op jit(solution)/shard_map/while/body/eval_jaxpr/reshape | solution.py:25
  46.9 1.7 %constant_dynamic-slice_fusion.5 = f32[512,1024]{1,0:T(8,128)S(1)} fusion(f32[1536,1024]{1,0:T(8,128)} %get-tuple-element.345, s32[]{:T(128)S(6)} %select_n.76), kind=kLoop, calls=%fused_computation.31.clone.1 | loop fusion | bytes 4194308 | tf_op jit(solution)/shard_map/while/body/eval_jaxpr/dynamic_slice | solution.py:22
  48.6 1.6 %mul.110 = f32[128,4,1024]{2,1,0:T(4,128)} reshape(f32[512,1024]{1,0:T(8,128)S(1)} %constant_dynamic-slice_fusion.5) | data formatting | bytes 4194304 | tf_op jit(solution)/shard_map/while/body/eval_jaxpr/mul | solution.py:29
  50.3 2.8 %multiply_bitcast_fusion.2 = f32[2,128,4,1024,1]{3,2,1,0,4:T(4,128)S(1)} fusion(f32[2,1024]{1,0:T(2,128)S(1)} %get-tuple-element.346, f32[128,4,1024]{2,1,0:T(4,128)} %mul.110), kind=kLoop, calls=%fused_computation.5.clone.1 | loop fusion | flops 1048576 | bytes 6299648 | tf_op jit(solution)/shard_map/while/body/eval_jaxpr/mul | solution.py:29
  53.1 17.6 %fusion.48 = f32[2,128,4,4,256]{4,1,3,2,0:T(8,128)S(1)} fusion(f32[4,256,1024,1,1]{2,0,1,3,4:T(4,128)S(1)} %bitcast.53, f32[2,128,4,1024,1]{3,2,1,0,4:T(4,128)S(1)} %multiply_bitcast_fusion.2), kind=kOutput, calls=%fused_computation.2.clone.1 | convolution fusion | flops 12884901888 | bytes 12582912 | tf_op jit(solution)/shard_map/while/body/eval_jaxpr/xrs,cs->xrc/dot_general | solution.py:30
  70.7 0.7 fusion.49
  71.5 6.0 %fusion.50 = f32[2,4,4,16,128]{3,2,1,0,4:T(4,128)S(1)} fusion(f32[2,128,4,4,256]{4,1,3,2,0:T(8,128)S(1)} %fusion.48, pred[16,128,256,1,1]{2,1,0,4,3:T(32,128)(4,1)S(1)} %fusion.49), kind=kOutput, calls=%fused_computation.11.clone.1 | convolution fusion | flops 201326592 | bytes 4980736 | tf_op jit(solution)/shard_map/while/body/eval_jaxpr/xiabj,nij->xabni/dot_general | solution.py:39
  78.9 1.1 multiply_reduce_fusion.3
  80.0 1.0 fusion.51
  81.0 0.6 compare_reduce_fusion.2
  81.7 0.6 fusion.52
  82.3 4.9 %constant_dynamic-slice_fusion.4 = f32[1024,1024]{1,0:T(8,128)} fusion(f32[1536,1024]{1,0:T(8,128)} %get-tuple-element.345, s32[]{:T(128)S(6)} %select_n.76), kind=kLoop, calls=%fused_computation.30.clone.1 | loop fusion | bytes 8388612 | tf_op jit(solution)/shard_map/while/body/eval_jaxpr/dynamic_slice | solution.py:23
  87.2 5.2 %reshape.97 = f32[256,4,1024]{2,1,0:T(4,128)} reshape(f32[1024,1024]{1,0:T(8,128)} %constant_dynamic-slice_fusion.4) | data formatting | bytes 8388608 | tf_op jit(solution)/shard_map/while/body/eval_jaxpr/reshape | solution.py:25
  92.4 1.7 %constant_dynamic-slice_fusion.5 = f32[512,1024]{1,0:T(8,128)S(1)} fusion(f32[1536,1024]{1,0:T(8,128)} %get-tuple-element.345, s32[]{:T(128)S(6)} %select_n.76), kind=kLoop, calls=%fused_computation.31.clone.1 | loop fusion | bytes 4194308 | tf_op jit(solution)/shard_map/while/body/eval_jaxpr/dynamic_slice | solution.py:22
  94.1 1.6 %mul.110 = f32[128,4,1024]{2,1,0:T(4,128)} reshape(f32[512,1024]{1,0:T(8,128)S(1)} %constant_dynamic-slice_fusion.5) | data formatting | bytes 4194304 | tf_op jit(solution)/shard_map/while/body/eval_jaxpr/mul | solution.py:29
  95.8 2.8 %multiply_bitcast_fusion.2 = f32[2,128,4,1024,1]{3,2,1,0,4:T(4,128)S(1)} fusion(f32[2,1024]{1,0:T(2,128)S(1)} %get-tuple-element.346, f32[128,4,1024]{2,1,0:T(4,128)} %mul.110), kind=kLoop, calls=%fused_computation.5.clone.1 | loop fusion | flops 1048576 | bytes 6299648 | tf_op jit(solution)/shard_map/while/body/eval_jaxpr/mul | solution.py:29
  98.6 17.6 %fusion.48 = f32[2,128,4,4,256]{4,1,3,2,0:T(8,128)S(1)} fusion(f32[4,256,1024,1,1]{2,0,1,3,4:T(4,128)S(1)} %bitcast.53, f32[2,128,4,1024,1]{3,2,1,0,4:T(4,128)S(1)} %multiply_bitcast_fusion.2), kind=kOutput, calls=%fused_computation.2.clone.1 | convolution fusion | flops 12884901888 | bytes 12582912 | tf_op jit(solution)/shard_map/while/body/eval_jaxpr/xrs,cs->xrc/dot_general | solution.py:30
  116.2 0.7 fusion.49
  116.9 6.0 %fusion.50 = f32[2,4,4,16,128]{3,2,1,0,4:T(4,128)S(1)} fusion(f32[2,128,4,4,256]{4,1,3,2,0:T(8,128)S(1)} %fusion.48, pred[16,128,256,1,1]{2,1,0,4,3:T(32,128)(4,1)S(1)} %fusion.49), kind=kOutput, calls=%fused_computation.11.clone.1 | convolution fusion | flops 201326592 | bytes 4980736 | tf_op jit(solution)/shard_map/while/body/eval_jaxpr/xiabj,nij->xabni/dot_general | solution.py:39
  124.4 1.1 multiply_reduce_fusion.3
  125.5 1.0 fusion.51
  126.5 0.6 compare_reduce_fusion.2
  127.2 0.6 fusion.52
  127.8 1.9 %collective-permute-start.1 = (f32[3,128]{1,0:T(4,128)S(1)}, f32[3,128]{1,0:T(4,128)S(1)}, u32[]{:S(2)}, u32[]{:S(2)}) collective-permute-start(f32[3,128]{1,0:T(4,128)S(1)} %slice.66), channel_id=1, source_target_pairs={{0,1},{1,4},{4,5},{5,8},{8,9},{9,12},{12,13},{2,3},{3,6},{6,7},{7,... | collective-permute-start | bytes 4616 | tf_op jit(solution)/shard_map/ppermute | solution.py:10
  129.7 1.1 collective-permute-done.1
  130.9 4.4 %psum.7 = f32[3,256]{1,0:T(4,128)} all-reduce(f32[3,256]{1,0:T(4,128)S(1)} %pad_add_fusion), channel_id=1, replica_groups=mesh['groups'=2,'atoms'=4,'states'=2,'sub'=2] {'states'}, use_global_device_ids=true, to_apply=%region_4.5 | all-reduce | flops 768 | bytes 6144 | tf_op jit(solution)/shard_map/psum | solution.py:78
  (29 shorter events, 3.0 us)
Async XLA Ops:
  0.0 3.7 %copy-start.3 = (f32[1024]{0:T(1024)S(1)}, f32[1024]{0:T(1024)}, u32[]{:S(2)}) copy-start(f32[1024]{0:T(1024)} %param.11) | copy-start | bytes 12292
  0.0 3.8 %copy-start.4 = (f32[1024]{0:T(1024)S(1)}, f32[1024]{0:T(1024)}, u32[]{:S(2)}) copy-start(f32[1024]{0:T(1024)} %param.12) | copy-start | bytes 12292
  1.8 28.4 %collective-permute-start = (f32[512,1024]{1,0:T(8,128)S(1)}, f32[512,1024]{1,0:T(8,128)}, u32[]{:S(2)}, u32[]{:S(2)}) collective-permute-start(f32[512,1024]{1,0:T(8,128)S(1)} %slice.64), channel_id=1, source_target_pairs={{1,0},{4,1},{5,4},{8,5},{9,8},{12,9},{13,12},{3,2},{6,3},{7,6},{10... | collective-permute-start | bytes 6291464 | tf_op jit(solution)/shard_map/ppermute | solution.py:10
  3.8 33.0 %copy-start.1 = (f32[48,16,256]{2,1,0:T(8,128)S(1)}, f32[48,16,256]{2,1,0:T(8,128)}, u32[]{:S(2)}) copy-start(f32[48,16,256]{2,1,0:T(8,128)} %param.14) | copy-start | bytes 2359300
  3.8 33.0 %copy-start.2 = (s32[16,256]{1,0:T(8,128)S(1)}, s32[16,256]{1,0:T(8,128)}, u32[]{:S(2)}) copy-start(s32[16,256]{1,0:T(8,128)} %param.13) | copy-start | bytes 49156
  50.3 2.8 %copy-start = (f32[256,4,1024]{2,1,0:T(4,128)S(1)}, f32[256,4,1024]{2,1,0:T(4,128)}, u32[]{:S(2)}) copy-start(f32[256,4,1024]{2,1,0:T(4,128)} %reshape.97) | copy-start | bytes 12582916 | tf_op jit(solution)/shard_map/while
  95.7 2.8 %copy-start = (f32[256,4,1024]{2,1,0:T(4,128)S(1)}, f32[256,4,1024]{2,1,0:T(4,128)}, u32[]{:S(2)}) copy-start(f32[256,4,1024]{2,1,0:T(4,128)} %reshape.97) | copy-start | bytes 12582916 | tf_op jit(solution)/shard_map/while
  127.8 3.1 %collective-permute-start.1 = (f32[3,128]{1,0:T(4,128)S(1)}, f32[3,128]{1,0:T(4,128)S(1)}, u32[]{:S(2)}, u32[]{:S(2)}) collective-permute-start(f32[3,128]{1,0:T(4,128)S(1)} %slice.66), channel_id=1, source_target_pairs={{0,1},{1,4},{4,5},{5,8},{8,9},{9,12},{12,13},{2,3},{3,6},{6,7},{7,... | collective-permute-start | bytes 4616 | tf_op jit(solution)/shard_map/ppermute | solution.py:10
where the time goes:
time: 137 us; the launch traced here: 135 us
  matrix products  49.3 us (36%)
  local copies, waits for them, and re-layouts  31.5 us (23%)
  waiting for transfers between devices  27.5 us (20%)
  other arithmetic  18.4 us (13%)
  blocking collectives  4.35 us (3%)
  starting transfers between devices  3.89 us (3%)
    dot_general x2, matrix products, step(): jnp.einsum('xrs,cs->xrc', scaled, near_rows, precision=lax.Precision.HIGH...  35.3 us
    ppermute x2, waiting for transfers between devices, shifted(): lax.ppermute(value, axis, [(source, source + steps) for source in range(f...  27.5 us
    dot_general x2, matrix products, step(): jnp.einsum('xiabj,nij->xabni', gram_blocks, onehot, precision=lax.Precisi...  12 us
    reshape x2, local copies, waits for them, and re-layouts, step(): near_rows.reshape(span, 4, states_local).transpose(1, 0, 2)  10.4 us
    dynamic_slice x2, local copies, waits for them, and re-layouts, step(): near_rows = lax.dynamic_slice_in_dim(window, first_atom * 4, span * 4, 0)  9.72 us
    concatenate x1, other arithmetic, local(): window = jnp.concatenate([coeffs, upper_rows], 0)  6.61 us
    mul x2, other arithmetic, step(): scaled = own_rows[None] * weights[:, None, :]  5.6 us
    psum x1, blocking collectives, local(): return lax.psum(own_force, 'states')  4.35 us
  transfers between devices with their start and end apart: 2, of which 2 were waited for; matrix products, arithmetic and copies ran while one was open for 0% of the time, Pallas kernels for 0%

commit v1 on v0

v1 whole, which is shorter than its diff:
```python
import functools

import jax
import jax.numpy as jnp
from jax import lax
from jax.experimental import pallas as pl
from jax.experimental.pallas import tpu as pltpu
from jax.sharding import PartitionSpec as P

LANES = 128
CHUNK = 64
SHARD = ("atoms", "sub")
VMEM_LIMIT = 48 * 1024 * 1024


def shifted(value, axis, steps):
    count = lax.axis_size(axis)
    first, last = (max(0, -steps), min(count, count - steps))
    return lax.ppermute(value, axis, [(source, source + steps) for source in range(first, last)])


def split(value):
    high = value.astype(jnp.bfloat16)
    return high, (value - high.astype(jnp.float32)).astype(jnp.bfloat16)


def fetch(rows_ref, columns_ref, copy_sem):
    copies = [
        pltpu.make_async_copy(
            rows_ref.at[:, c * LANES : (c + 1) * LANES], columns_ref.at[c], copy_sem.at[c]
        )
        for c in range(rows_ref.shape[1] // LANES)
    ]
    for copy in copies:
        copy.start()
    return copies


def gram(left_high, left_low, right_high, right_low):
    dot = functools.partial(
        lax.dot_general,
        dimension_numbers=(((1,), (1,)), ((), ())),
        preferred_element_type=jnp.float32,
    )
    return (
        dot(left_high, right_high) + dot(left_high, right_low) + dot(left_low, right_high)
    )


def pick_pairs(gram_ref, planes, rows, index, deriv, pair_ref):
    low = [part & 7 for part in index]
    high = [part >> 3 for part in index]
    pair = [[jnp.zeros((8, LANES), jnp.float32) for half in range(2)] for k in range(3)]
    for group in planes:

        def step(r, picked):
            hit = [part == r for part in high]
            out = []
            for at, (plane, block, key) in enumerate(group):
                tile = gram_ref[plane, pl.ds(pl.multiple_of(r * 8, 8), 8), block * LANES : (block + 1) * LANES]
                for half in range(2):
                    got = jnp.take_along_axis(tile, low[half], axis=0)
                    out.append(jnp.where(hit[half], got, picked[2 * at + half]))
            return tuple(out)

        start = tuple(jnp.zeros((8, LANES), jnp.float32) for plane in group for half in range(2))
        picked = lax.fori_loop(0, rows // 8, step, start, unroll=2)
        for at, (plane, block, key) in enumerate(group):
            for k in range(3):
                for half in range(2):
                    pair[k][half] = pair[k][half] + picked[2 * at + half] * deriv(k, key, half)
    for k in range(3):
        for half in range(2):
            pair_ref[16 * k + 8 * half : 16 * k + 8 * half + 8, :] = pair[k][half]
    return [jnp.sum(pair[k][0] + pair[k][1], axis=0, keepdims=True) for k in range(3)]


def spread(index_ref, pair_ref, spread_ref, rows):
    lane_rows = lax.broadcasted_iota(jnp.int32, (8, LANES), 0)

    def step(r, unused):
        at = pl.multiple_of(r * 8, 8)
        target = lane_rows + at
        total = [jnp.zeros((8, LANES), jnp.float32) for k in range(3)]
        for n in range(16):
            hit = jnp.broadcast_to(index_ref[n : n + 1, :], (8, LANES)) == target
            for k in range(3):
                term = jnp.broadcast_to(pair_ref[16 * k + n : 16 * k + n + 1, :], (8, LANES))
                total[k] = total[k] + jnp.where(hit, term, 0.0)
        for k in range(3):
            spread_ref[k, pl.ds(at, 8), :] = total[k]
        return unused

    lax.fori_loop(0, rows // 8, step, 0)
    ones = jnp.ones((8, LANES), jnp.float32)
    out = []
    for k in range(3):
        total = lax.dot_general(
            ones,
            spread_ref[k, :rows, :],
            (((1,), (1,)), ((), ())),
            precision=lax.Precision.HIGHEST,
            preferred_element_type=jnp.float32,
        )
        out.append(total[:1])
    return out


def inner_kernel(
    start_ref, coeffs_ref, occup_ref, energies_ref, nbr_ref, dham_ref, dovl_ref,
    own_high_ref, own_low_ref, force_ref,
    near_high_ref, near_low_ref, gram_ref, index_ref, pair_ref, spread_ref, columns_ref, copy_sem,
):
    atoms = nbr_ref.shape[1]
    occup = occup_ref[...]
    weights = [occup, occup * energies_ref[...]]
    columns = fetch(coeffs_ref, columns_ref, copy_sem)
    for c, copy in enumerate(columns):
        copy.wait()
        lanes = slice(c * LANES, (c + 1) * LANES)
        for a in range(4):
            for at in range(0, atoms, CHUNK):
                rows = columns_ref[c, pl.ds(a + 4 * at, CHUNK, stride=4), :]
                own = (at // LANES) * 512 + a * LANES + at % LANES
                own_high_ref[own : own + CHUNK, lanes], own_low_ref[own : own + CHUNK, lanes] = split(rows)
                for x in range(2):
                    near = (x * 4 + a) * atoms + at
                    near_high_ref[near : near + CHUNK, lanes], near_low_ref[near : near + CHUNK, lanes] = split(
                        rows * weights[x][:, lanes]
                    )
    force_ref[...] = jnp.zeros_like(force_ref)
    for tile in range(2):
        first = tile * LANES
        rows = atoms - first

        def multiply(xb, unused, first=first, rows=rows, tile=tile):
            at = pl.multiple_of(xb * atoms + first, LANES)
            gram_ref[xb, :rows, :] = gram(
                near_high_ref[pl.ds(at, rows), :],
                near_low_ref[pl.ds(at, rows), :],
                own_high_ref[tile * 512 : tile * 512 + 512, :],
                own_low_ref[tile * 512 : tile * 512 + 512, :],
            )
            return unused

        lax.fori_loop(0, 8, multiply, 0)
        index_ref[...] = nbr_ref[:, first : first + LANES] - (start_ref[0] + first)
        index = [index_ref[8 * half : 8 * half + 8, :] for half in range(2)]

        def deriv(k, key, half, first=first):
            x, ab = key
            block = (dham_ref, dovl_ref)[x][k * 16 + ab, 8 * half : 8 * half + 8, first : first + LANES]
            return -block if x else block

        planes = [
            [(x * 4 + b, a, (x, a * 4 + b)) for a in (2 * g, 2 * g + 1) for b in range(4)]
            for x in range(2)
            for g in range(2)
        ]
        mine = pick_pairs(gram_ref, planes, rows, index, deriv, pair_ref)
        theirs = spread(index_ref, pair_ref, spread_ref, rows)
        for k in range(3):
            force_ref[k : k + 1, first : first + LANES] += -2.0 * mine[k]
            force_ref[k : k + 1, first : first + rows] += 2.0 * theirs[k]


def cross_kernel(
    start_ref, above_ref, below_ref, blocks_ref, occup_ref, energies_ref, nbr_ref, dham_ref, dovl_ref,
    own_high_ref, own_low_ref, inner_ref,
    force_ref, up_ref, down_ref,
    near_high_ref, near_low_ref, gram_ref, index_ref, pair_ref, spread_ref,
    above_columns_ref, below_columns_ref, above_sem, below_sem,
):
    atoms = nbr_ref.shape[1]
    above_copies = fetch(above_ref, above_columns_ref, above_sem)
    below_copies = fetch(below_ref, below_columns_ref, below_sem)
    lower = above_ref.shape[0] // 4
    upper = below_ref.shape[0] // 4
    half_lanes = LANES // 2
    occup = occup_ref[...]
    weights = [occup, occup * energies_ref[...]]
    force_ref[...] = inner_ref[...]
    up_ref[...] = jnp.zeros_like(up_ref)
    down_ref[...] = jnp.zeros_like(down_ref)

    for c, copy in enumerate(above_copies):
        copy.wait()
        lanes = slice(c * LANES, (c + 1) * LANES)
        for b in range(4):
            rows = above_columns_ref[c, pl.ds(b, lower, stride=4), :]
            for x in range(2):
                at = (x * 4 + b) * lower
                near_high_ref[at : at + lower, lanes], near_low_ref[at : at + lower, lanes] = split(
                    rows * weights[x][:, lanes]
                )

    def multiply(xb, unused):
        at = pl.multiple_of(xb * lower, 16)
        gram_ref[xb, :lower, :] = gram(
            near_high_ref[pl.ds(at, lower), :],
            near_low_ref[pl.ds(at, lower), :],
            own_high_ref[512:, :],
            own_low_ref[512:, :],
        )
        return unused

    lax.fori_loop(0, 8, multiply, 0)
    index_ref[...] = nbr_ref[:, LANES:] - (start_ref[0] + atoms)
    index = [index_ref[8 * half : 8 * half + 8, :] for half in range(2)]

    def deriv(k, key, half):
        x, ab = key
        block = (dham_ref, dovl_ref)[x][k * 16 + ab, 8 * half : 8 * half + 8, LANES:]
        return -block if x else block

    planes = [
        [(x * 4 + b, a, (x, a * 4 + b)) for a in (2 * g, 2 * g + 1) for b in range(4)]
        for x in range(2)
        for g in range(2)
    ]
    mine = pick_pairs(gram_ref, planes, lower, index, deriv, pair_ref)
    theirs = spread(index_ref, pair_ref, spread_ref, lower)
    for k in range(3):
        force_ref[k : k + 1, LANES:] += -2.0 * mine[k]
        up_ref[k : k + 1, :lower] = 2.0 * theirs[k]

    if upper < half_lanes:
        near_high_ref[:512, :] = jnp.zeros_like(near_high_ref[:512, :])
        near_low_ref[:512, :] = jnp.zeros_like(near_low_ref[:512, :])
    for c, copy in enumerate(below_copies):
        copy.wait()
        lanes = slice(c * LANES, (c + 1) * LANES)
        for a in range(4):
            rows = below_columns_ref[c, pl.ds(a, upper, stride=4), :]
            for x in range(2):
                at = a * LANES + x * half_lanes
                near_high_ref[at : at + upper, lanes], near_low_ref[at : at + upper, lanes] = split(
                    rows * weights[x][:, lanes]
                )

    def multiply_lower(b, unused):
        at = pl.multiple_of(b * LANES + lower, 16)
        gram_ref[b, :upper, :] = gram(
            own_high_ref[pl.ds(at, upper), :],
            own_low_ref[pl.ds(at, upper), :],
            near_high_ref[:512, :],
            near_low_ref[:512, :],
        )
        return unused

    lax.fori_loop(0, 4, multiply_lower, 0)
    index_ref[...] = blocks_ref[48].astype(jnp.int32) - lower
    index = [index_ref[8 * half : 8 * half + 8, :] for half in range(2)]

    def deriv_lower(k, key, half):
        return blocks_ref[k * 16 + key, 8 * half : 8 * half + 8, :]

    planes = [[(b, a, a * 4 + b) for a in (2 * g, 2 * g + 1) for b in range(4)] for g in range(2)]
    mine = pick_pairs(gram_ref, planes, upper, index, deriv_lower, pair_ref)
    theirs = spread(index_ref, pair_ref, spread_ref, upper)
    for k in range(3):
        down_ref[k : k + 1, :] = -2.0 * mine[k]
        force_ref[k : k + 1, lower:LANES] += 2.0 * theirs[k]


def local(coeffs, occup, energies, nbr, dham, dovl):
    slots, atoms = nbr.shape
    states = coeffs.shape[1]
    halo = atoms // 2
    upper = halo // 2
    lower = halo - upper
    half_lanes = LANES // 2
    start = lax.axis_index(SHARD) * atoms
    above = shifted(coeffs[: 4 * lower], SHARD, -1)
    below = shifted(coeffs[4 * (atoms - upper) :], SHARD, 1)
    target = jnp.where(nbr[:, atoms - upper :] >= 0, nbr[:, atoms - upper :] - (start + atoms), -1)
    target = jnp.pad(target.astype(jnp.float32), ((0, 0), (0, half_lanes - upper)), constant_values=-1.0)
    blocks = jnp.concatenate(
        [
            jnp.pad(dham[:, :, atoms - upper :], ((0, 0), (0, 0), (0, half_lanes - upper))),
            jnp.pad(-dovl[:, :, atoms - upper :], ((0, 0), (0, 0), (0, half_lanes - upper))),
        ],
        2,
    )
    blocks = jnp.concatenate([blocks, jnp.concatenate([target, target], 1)[None]], 0)
    blocks = shifted(blocks, SHARD, 1)
    start = start.reshape(1).astype(jnp.int32)
    occup = occup.reshape(1, states)
    energies = energies.reshape(1, states)

    vmem = pl.BlockSpec(memory_space=pltpu.VMEM)
    hbm = pl.BlockSpec(memory_space=pl.ANY)
    smem = pl.BlockSpec(memory_space=pltpu.SMEM)
    own_high, own_low, inner = pl.pallas_call(
        inner_kernel,
        out_shape=(
            jax.ShapeDtypeStruct((4 * atoms, states), jnp.bfloat16),
            jax.ShapeDtypeStruct((4 * atoms, states), jnp.bfloat16),
            jax.ShapeDtypeStruct((8, atoms), jnp.float32),
        ),
        in_specs=[smem, hbm] + [vmem] * 5,
        out_specs=(vmem, vmem, vmem),
        scratch_shapes=[
            pltpu.VMEM((8 * atoms, states), jnp.bfloat16),
            pltpu.VMEM((8 * atoms, states), jnp.bfloat16),
            pltpu.VMEM((8, atoms, 512), jnp.float32),
            pltpu.VMEM((slots, LANES), jnp.int32),
            pltpu.VMEM((3 * slots, LANES), jnp.float32),
            pltpu.VMEM((3, atoms, LANES), jnp.float32),
            pltpu.VMEM((states // LANES, 4 * atoms, LANES), jnp.float32),
            pltpu.SemaphoreType.DMA((states // LANES,)),
        ],
        compiler_params=pltpu.CompilerParams(vmem_limit_bytes=VMEM_LIMIT),
        cost_estimate=pl.CostEstimate(
            flops=3 * 2 * 8 * 384 * 512 * states, bytes_accessed=16 * 1024 * 1024, transcendentals=0
        ),
        name="inner_pairs",
    )(start, coeffs, occup, energies, nbr, dham, dovl)

    own, up, down = pl.pallas_call(
        cross_kernel,
        out_shape=(
            jax.ShapeDtypeStruct((8, atoms), jnp.float32),
            jax.ShapeDtypeStruct((8, LANES), jnp.float32),
            jax.ShapeDtypeStruct((8, LANES), jnp.float32),
        ),
        in_specs=[smem, hbm, hbm] + [vmem] * 9,
        out_specs=(vmem, vmem, vmem),
        scratch_shapes=[
            pltpu.VMEM((8 * LANES, states), jnp.bfloat16),
            pltpu.VMEM((8 * LANES, states), jnp.bfloat16),
            pltpu.VMEM((8, LANES, 512), jnp.float32),
            pltpu.VMEM((slots, LANES), jnp.int32),
            pltpu.VMEM((3 * slots, LANES), jnp.float32),
            pltpu.VMEM((3, LANES, LANES), jnp.float32),
            pltpu.VMEM((states // LANES, 4 * lower, LANES), jnp.float32),
            pltpu.VMEM((states // LANES, 4 * upper, LANES), jnp.float32),
            pltpu.SemaphoreType.DMA((states // LANES,)),
            pltpu.SemaphoreType.DMA((states // LANES,)),
        ],
        compiler_params=pltpu.CompilerParams(vmem_limit_bytes=VMEM_LIMIT),
        name="cross_pairs",
    )(start, above, below, blocks, occup, energies, nbr, dham, dovl, own_high, own_low, inner)

    up = shifted(up[:3], SHARD, 1)
    down = shifted(down[:3], SHARD, -1)
    down = (down[:, :half_lanes] + down[:, half_lanes:])[:, :upper]
    own = own[:3] + jnp.pad(up, ((0, 0), (0, atoms - LANES))) + jnp.pad(down, ((0, 0), (atoms - upper, 0)))
    return lax.psum(own, "states")


def solution(mesh):
    in_specs = (
        P(("groups", "atoms", "sub"), "states"),
        P(("groups", "states")),
        P(("groups", "states")),
        P(None, ("groups", "atoms", "sub")),
        P(None, None, ("groups", "atoms", "sub")),
        P(None, None, ("groups", "atoms", "sub")),
    )
    out_specs = P(None, ("groups", "atoms", "sub"))
    return jax.shard_map(local, mesh=mesh, in_specs=in_specs, out_specs=out_specs, check_vma=False)
```

time: 137 us -> 71.1 us (0.52)
  matrix products: 49.3 us -> 0 us
  Pallas kernels: 0 us -> 43.8 us
  waiting for transfers between devices: 27.5 us -> 0.64 us
  local copies, waits for them, and re-layouts: 31.5 us -> 4.74 us
  other arithmetic: 18.4 us -> 0.64 us
  starting transfers between devices: 3.89 us -> 15.7 us
    dot_general x6 -> x0, matrix products: 49.3 us -> none  [the longest x2 35.3 us: step(): jnp.einsum('xrs,cs->xrc', scaled, near_rows, precision=lax.Precision.HIGH...]
    pallas_call x0 -> x2, Pallas kernels: none -> 43.8 us  [the longest x1 25.5 us: local(): pl.pallas_call(inner_kernel, out_shape=(jax.ShapeDtypeStruct((4 * atoms,...]
    ppermute x2 -> x5, waiting for transfers between devices: 27.5 us -> 0.64 us  [shifted(): lax.ppermute(value, axis, [(source, source + steps) for source in range(f...]
    dynamic_slice x4 -> x0, local copies, waits for them, and re-layouts: 13.2 us -> none  [the longest x2 9.72 us: step(): near_rows = lax.dynamic_slice_in_dim(window, first_atom * 4, span * 4, 0)]
    ppermute x2 -> x5, starting transfers between devices: 3.89 us -> 15.7 us  [shifted(): lax.ppermute(value, axis, [(source, source + steps) for source in range(f...]
    reshape x2 -> x0, local copies, waits for them, and re-layouts: 10.4 us -> none  [step(): near_rows.reshape(span, 4, states_local).transpose(1, 0, 2)]
    concatenate x1, other arithmetic: 6.61 us -> 0.17 us  [local(): jnp.concatenate([blocks, jnp.concatenate([target, target], 1)[None]], 0)]
    mul x3 -> x0, other arithmetic: 5.6 us -> none  [the longest x2 5.6 us: step(): scaled = own_rows[None] * weights[:, None, :]]
  transfers between devices with their start and end apart: 2 -> 5, of which waited for: 2 -> 1; matrix products, arithmetic and copies ran while one was open for 0% -> 1% of each run, Pallas kernels for 0% -> 36%
where the time goes in v1:
time: 71.1 us; the launch traced here: 70.1 us
  Pallas kernels  43.8 us (62%)
  starting transfers between devices  15.7 us (22%)
  local copies, waits for them, and re-layouts  4.74 us (7%)
  blocking collectives  4.35 us (6%)
    pallas_call x1, Pallas kernels, local(): pl.pallas_call(inner_kernel, out_shape=(jax.ShapeDtypeStruct((4 * atoms,...  25.5 us
    pallas_call x1, Pallas kernels, local(): pl.pallas_call(cross_kernel, out_shape=(jax.ShapeDtypeStruct((8, atoms),...  18.4 us
    ppermute x5, starting transfers between devices, shifted(): lax.ppermute(value, axis, [(source, source + steps) for source in range(f...  15.7 us
    psum x1, blocking collectives, local(): return lax.psum(own, 'states')  4.35 us
    slice x1, local copies, waits for them, and re-layouts, local(): below = shifted(coeffs[4 * (atoms - upper):], SHARD, 1)  3.22 us
  transfers between devices with their start and end apart: 5, of which 1 were waited for; matrix products, arithmetic and copies ran while one was open for 1% of the time, Pallas kernels for 36%

profile of v1, /device:TPU:1, one launch (start us, length us, event | category | flops | bytes accessed | tf_op | source)
XLA Modules:
  0.0 70.1 jit_solution(17562158595118820677)
XLA Ops:
  0.0 0.0 copy-start.1
  0.0 0.0 copy-start.3
  0.0 0.0 copy-start.5
  0.0 0.0 copy-start.4
  0.0 3.2 %fusion = (f32[256,1024]{1,0:T(8,128)}, f32[256,1024]{1,0:T(8,128)}) fusion(f32[1024,1024]{1,0:T(8,128)} %coeffs_ref.1), kind=kLoop, calls=%fused_computation.6 | loop fusion | bytes 4194304 | tf_op jit(solution)/shard_map/slice | solution.py:275
  3.3 4.6 %collective-permute-start.1 = (f32[256,1024]{1,0:T(8,128)}, f32[256,1024]{1,0:T(8,128)S(1)}, u32[]{:S(2)}, u32[]{:S(2)}) collective-permute-start(f32[256,1024]{1,0:T(8,128)} %get-tuple-element.17), channel_id=1, source_target_pairs={{0,1},{1,4},{4,5},{5,8},{8,9},{9,12},{12,13},{2,3},{3,6},{6,7},{7,... | collective-permute-start | bytes 3145736 | tf_op jit(solution)/shard_map/ppermute | solution.py:19
  7.8 1.9 %collective-permute-start = (f32[256,1024]{1,0:T(8,128)}, f32[256,1024]{1,0:T(8,128)}, u32[]{:S(2)}, u32[]{:S(2)}) collective-permute-start(f32[256,1024]{1,0:T(8,128)} %get-tuple-element.18), channel_id=1, source_target_pairs={{1,0},{4,1},{5,4},{8,5},{9,8},{12,9},{13,12},{3,2},{6,3},{7,6},{10... | collective-permute-start | bytes 3145736 | tf_op jit(solution)/shard_map/ppermute | solution.py:19
  9.8 0.0 copy-done.1
  9.8 0.2 slice_negate_fusion
  10.0 0.0 copy-done.3
  10.0 0.1 select_convert_fusion
  10.1 0.1 maximum_bitcast_fusion
  10.1 0.0 copy-done.2
  10.1 0.2 slice.33
  10.3 0.2 pad_maximum_fusion
  10.5 3.6 %collective-permute-start.2 = (f32[49,16,128]{2,1,0:T(8,128)S(1)}, f32[49,16,128]{2,1,0:T(8,128)S(1)}, u32[]{:S(2)}, u32[]{:S(2)}) collective-permute-start(f32[49,16,128]{2,1,0:T(8,128)S(1)} %pad_maximum_fusion), channel_id=1, source_target_pairs={{0,1},{1,4},{4,5},{5,8},{8,9},{9,12},{12,13},{2,3},{3,6},{6,7},{7,... | collective-permute-start | bytes 1204232 | tf_op jit(solution)/shard_map/ppermute | solution.py:19
  14.1 0.0 copy-done.5
  14.1 0.0 copy-done.4
  14.2 25.5 %inner_pairs.1 = (bf16[1024,1024]{1,0:T(8,128)(2,1)S(1)}, bf16[1024,1024]{1,0:T(8,128)(2,1)S(1)}, f32[8,256]{1,0:T(8,128)S(1)}) custom-call(s32[1]{0:T(128)} %bitcast.start_ref, f32[1024,1024]{1,0:T(8,128)} %coeffs_ref.1, f32[1,1024]{1,0:T(1,128)S(1)} %bitcast.5, f32[1,1024]{1,0:T(1,128)S(1)} %bitcast.7, s32[16,256]{1,0:T(8,128)S(1)} %copy-done.3, ...), custom_call_target="tpu_custom_call" | custom-call | flops 9663676416 | bytes 16777216 | tf_op jit(solution)/shard_map/inner_pairs/pallas_call | solution.py:294
  39.6 0.0 copy-start
  39.6 1.3 %copy-done = bf16[1024,1024]{1,0:T(8,128)(2,1)} copy-done((bf16[1024,1024]{1,0:T(8,128)(2,1)}, bf16[1024,1024]{1,0:T(8,128)(2,1)S(1)}, u32[]{:S(2)}) %copy-start) | copy-done | bytes 2097176
  40.9 0.0 collective-permute-done.2.blocks_ref
  41.0 0.0 collective-permute-done.1.below_ref
  41.0 0.0 collective-permute-done.above_ref
  41.0 18.4 %cross_pairs.1 = (f32[8,256]{1,0:T(8,128)S(1)}, f32[8,128]{1,0:T(8,128)S(1)}, f32[8,128]{1,0:T(8,128)S(1)}) custom-call(s32[1]{0:T(128)} %bitcast.start_ref, f32[256,1024]{1,0:T(8,128)} %collective-permute-done.above_ref, f32[256,1024]{1,0:T(8,128)S(1)} %collective-permute-done.1.below_ref, f32[49,16,128]{2,1,0:T(8,128)S(1)} %collective-permute-done.2.blocks_ref, ...), custom_call_target="tpu_custom_call" | custom-call | tf_op jit(solution)/shard_map/cross_pairs/pallas_call | solution.py:320
  59.3 1.9 %collective-permute-start.4 = (f32[3,128]{1,0:T(4,128)S(1)}, f32[3,128]{1,0:T(4,128)S(1)}, u32[]{:S(2)}, u32[]{:S(2)}) collective-permute-start(f32[3,128]{1,0:T(4,128)S(1)} %slice.38), channel_id=1, source_target_pairs={{1,0},{4,1},{5,4},{8,5},{9,8},{12,9},{13,12},{3,2},{6,3},{7,6},{10... | collective-permute-start | bytes 4616 | tf_op jit(solution)/shard_map/ppermute | solution.py:19
  61.3 3.6 %collective-permute-start.3 = (f32[3,128]{1,0:T(4,128)S(1)}, f32[3,128]{1,0:T(4,128)S(1)}, u32[]{:S(2)}, u32[]{:S(2)}) collective-permute-start(f32[3,128]{1,0:T(4,128)S(1)} %slice.37), channel_id=1, source_target_pairs={{0,1},{1,4},{4,5},{5,8},{8,9},{9,12},{12,13},{2,3},{3,6},{6,7},{7,... | collective-permute-start | bytes 4616 | tf_op jit(solution)/shard_map/ppermute | solution.py:19
  64.9 0.0 collective-permute-done.4
  64.9 0.1 slice_add_fusion
  65.0 0.6 collective-permute-done.3
  65.6 0.1 pad_add_fusion
  65.7 4.4 %psum.7 = f32[3,256]{1,0:T(4,128)} all-reduce(f32[3,256]{1,0:T(4,128)S(1)} %pad_add_fusion), channel_id=1, replica_groups=mesh['groups'=2,'atoms'=4,'states'=2,'sub'=2] {'states'}, use_global_device_ids=true, to_apply=%region_0.1 | all-reduce | flops 768 | bytes 6144 | tf_op jit(solution)/shard_map/psum | solution.py:349
  (3 shorter events, 0.0 us)
Async XLA Ops:
  0.0 9.8 %copy-start.1 = (f32[48,16,256]{2,1,0:T(8,128)S(1)}, f32[48,16,256]{2,1,0:T(8,128)}, u32[]{:S(2)}) copy-start(f32[48,16,256]{2,1,0:T(8,128)} %dovl_ref.3) | copy-start | bytes 2359300
  0.0 10.0 %copy-start.3 = (s32[16,256]{1,0:T(8,128)S(1)}, s32[16,256]{1,0:T(8,128)}, u32[]{:S(2)}) copy-start(s32[16,256]{1,0:T(8,128)} %nbr_ref.3) | copy-start | bytes 49156
  0.0 10.1 %copy-start.2 = (f32[48,16,256]{2,1,0:T(8,128)S(1)}, f32[48,16,256]{2,1,0:T(8,128)}, u32[]{:S(2)}) copy-start(f32[48,16,256]{2,1,0:T(8,128)} %dham_ref.3) | copy-start | bytes 2359300
  0.0 14.1 %copy-start.5 = (f32[1024]{0:T(1024)S(1)}, f32[1024]{0:T(1024)}, u32[]{:S(2)}) copy-start(f32[1024]{0:T(1024)} %param.8) | copy-start | bytes 12292
  0.0 14.1 %copy-start.4 = (f32[1024]{0:T(1024)S(1)}, f32[1024]{0:T(1024)}, u32[]{:S(2)}) copy-start(f32[1024]{0:T(1024)} %param.7) | copy-start | bytes 12292
  3.3 37.7 %collective-permute-start.1 = (f32[256,1024]{1,0:T(8,128)}, f32[256,1024]{1,0:T(8,128)S(1)}, u32[]{:S(2)}, u32[]{:S(2)}) collective-permute-start(f32[256,1024]{1,0:T(8,128)} %get-tuple-element.17), channel_id=1, source_target_pairs={{0,1},{1,4},{4,5},{5,8},{8,9},{9,12},{12,13},{2,3},{3,6},{6,7},{7,... | collective-permute-start | bytes 3145736 | tf_op jit(solution)/shard_map/ppermute | solution.py:19
  7.8 33.1 %collective-permute-start = (f32[256,1024]{1,0:T(8,128)}, f32[256,1024]{1,0:T(8,128)}, u32[]{:S(2)}, u32[]{:S(2)}) collective-permute-start(f32[256,1024]{1,0:T(8,128)} %get-tuple-element.18), channel_id=1, source_target_pairs={{1,0},{4,1},{5,4},{8,5},{9,8},{12,9},{13,12},{3,2},{6,3},{7,6},{10... | collective-permute-start | bytes 3145736 | tf_op jit(solution)/shard_map/ppermute | solution.py:19
  10.5 30.5 %collective-permute-start.2 = (f32[49,16,128]{2,1,0:T(8,128)S(1)}, f32[49,16,128]{2,1,0:T(8,128)S(1)}, u32[]{:S(2)}, u32[]{:S(2)}) collective-permute-start(f32[49,16,128]{2,1,0:T(8,128)S(1)} %pad_maximum_fusion), channel_id=1, source_target_pairs={{0,1},{1,4},{4,5},{5,8},{8,9},{9,12},{12,13},{2,3},{3,6},{6,7},{7,... | collective-permute-start | bytes 1204232 | tf_op jit(solution)/shard_map/ppermute | solution.py:19
  39.6 1.3 %copy-start = (bf16[1024,1024]{1,0:T(8,128)(2,1)}, bf16[1024,1024]{1,0:T(8,128)(2,1)S(1)}, u32[]{:S(2)}) copy-start(bf16[1024,1024]{1,0:T(8,128)(2,1)S(1)} %get-tuple-element.12.own_low_ref) | copy-start | bytes 6291460
  59.3 5.6 %collective-permute-start.4 = (f32[3,128]{1,0:T(4,128)S(1)}, f32[3,128]{1,0:T(4,128)S(1)}, u32[]{:S(2)}, u32[]{:S(2)}) collective-permute-start(f32[3,128]{1,0:T(4,128)S(1)} %slice.38), channel_id=1, source_target_pairs={{1,0},{4,1},{5,4},{8,5},{9,8},{12,9},{13,12},{3,2},{6,3},{7,6},{10... | collective-permute-start | bytes 4616 | tf_op jit(solution)/shard_map/ppermute | solution.py:19
  61.3 4.4 %collective-permute-start.3 = (f32[3,128]{1,0:T(4,128)S(1)}, f32[3,128]{1,0:T(4,128)S(1)}, u32[]{:S(2)}, u32[]{:S(2)}) collective-permute-start(f32[3,128]{1,0:T(4,128)S(1)} %slice.37), channel_id=1, source_target_pairs={{0,1},{1,4},{4,5},{5,8},{8,9},{9,12},{12,13},{2,3},{3,6},{6,7},{7,... | collective-permute-start | bytes 4616 | tf_op jit(solution)/shard_map/ppermute | solution.py:19

commit v2 on v0

v2 whole, which is shorter than its diff:
```python
import functools

import jax
import jax.numpy as jnp
from jax import lax
from jax.experimental import pallas as pl
from jax.experimental.pallas import tpu as pltpu
from jax.sharding import PartitionSpec as P

LANES = 128
BLOCK = 64
SHARD = ("atoms", "sub")


def split(value):
    high = value.astype(jnp.bfloat16)
    return high, (value - high.astype(jnp.float32)).astype(jnp.bfloat16)


def gram(left_high, left_low, right_high, right_low):
    dot = functools.partial(
        lax.dot_general,
        dimension_numbers=(((1,), (1,)), ((), ())),
        preferred_element_type=jnp.float32,
    )
    return (
        dot(left_high, right_high) + dot(left_high, right_low) + dot(left_low, right_high)
    )


def lane_numbers():
    return lax.broadcasted_iota(jnp.int32, (8, LANES), 1)


def swap_halves(value):
    return pltpu.roll(value, BLOCK, 1)


def side_by_side(left, right, odd):
    if odd:
        return jnp.where(lane_numbers() < BLOCK, swap_halves(left), right)
    return jnp.where(lane_numbers() < BLOCK, left, swap_halves(right))


def pick_pairs(gram_ref, column, blocks, index, deriv):
    low = [part & 7 for part in index]
    high = [part >> 3 for part in index]
    pair = [[None, None] for k in range(3)]
    for x in range(2):
        picked = {}
        for r in range(8 * blocks):
            hit = [part == r for part in high]
            for b in range(4):
                row = (r // 8) * 512 + x * 256 + b * BLOCK + (r % 8) * 8
                for g in range(2):
                    at = column + g * LANES
                    tile = gram_ref[row : row + 8, at : at + LANES]
                    for half in range(2):
                        got = jnp.take_along_axis(tile, low[half], axis=0)
                        before = picked.get((b, g, half), 0.0)
                        picked[b, g, half] = jnp.where(hit[half], got, before)
        for (b, g, half), value in picked.items():
            for k in range(3):
                term = value * deriv(k, x, b, g, half)
                pair[k][half] = term if pair[k][half] is None else pair[k][half] + term
    return pair


def fold(pair):
    return [[value + swap_halves(value) for value in parts] for parts in pair]


def merge(even, odd):
    left = lane_numbers() < BLOCK
    return [[jnp.where(left, even[k][half], odd[k][half]) for half in range(2)] for k in range(3)]


def slot_sum(pair):
    return [jnp.sum(pair[k][0] + pair[k][1], axis=0, keepdims=True) for k in range(3)]


def spread(index_ref, pair, spread_ref, rows):
    lane_rows = lax.broadcasted_iota(jnp.int32, (8, LANES), 0)
    for r in range(rows // 8):
        slot = jnp.full((8, LANES), 16, jnp.int32)
        for n in range(16):
            hit = jnp.broadcast_to(index_ref[n : n + 1, :], (8, LANES)) == lane_rows + 8 * r
            slot = jnp.where(hit, n, slot)
        low = slot & 7
        for k in range(3):
            first = jnp.take_along_axis(pair[k][0], low, axis=0)
            second = jnp.take_along_axis(pair[k][1], low, axis=0)
            value = jnp.where(slot < 8, first, jnp.where(slot < 16, second, 0.0))
            spread_ref[k, 8 * r : 8 * r + 8, :] = value
    ones = jnp.ones((8, LANES), jnp.float32)
    out = []
    for k in range(3):
        total = lax.dot_general(
            ones,
            spread_ref[k, :rows, :],
            (((1,), (1,)), ((), ())),
            precision=lax.Precision.HIGHEST,
            preferred_element_type=jnp.float32,
        )
        out.append(total[:1])
    return out


def own_deriv(dham_ref, dovl_ref, tile, odd):
    def deriv(k, x, b, g, half):
        ref = (dham_ref, dovl_ref)[x]
        parts = [
            ref[k * 16 + (2 * g + parity) * 4 + b, 8 * half : 8 * half + 8, tile * LANES : (tile + 1) * LANES]
            for parity in range(2)
        ]
        both = side_by_side(parts[0], parts[1], odd)
        return -both if x else both

    return deriv


def block_index(index_ref, odd):
    return [
        side_by_side(index_ref[8 * half : 8 * half + 8, :], index_ref[8 * half : 8 * half + 8, :], odd)
        for half in range(2)
    ]


def inner_kernel(
    start_ref, coeffs_ref, occup_ref, energies_ref, nbr_ref, dham_ref, dovl_ref,
    own_high_ref, own_low_ref, near1_high_ref, near1_low_ref, force_ref,
    near0_high_ref, near0_low_ref, near2_high_ref, near2_low_ref, near3_high_ref, near3_low_ref,
    gram0_ref, gram1_ref, gram2_ref, gram3_ref, index_ref, spread_ref, columns_ref, copy_sem,
):
    states = coeffs_ref.shape[1]
    count = states // LANES
    near = [
        (near0_high_ref, near0_low_ref),
        (near1_high_ref, near1_low_ref),
        (near2_high_ref, near2_low_ref),
        (near3_high_ref, near3_low_ref),
    ]
    grams = [gram0_ref, gram1_ref, gram2_ref, gram3_ref]
    copies = {}
    for j in (3, 2, 1, 0):
        for c in range(count):
            copies[j, c] = pltpu.make_async_copy(
                coeffs_ref.at[j * 256 : j * 256 + 256, c * LANES : (c + 1) * LANES],
                columns_ref.at[c, j * 256 : j * 256 + 256, :],
                copy_sem.at[j * count + c],
            )
            copies[j, c].start()
    occup = occup_ref[...]
    weights = [occup, occup * energies_ref[...]]

    def prepare(j):
        for c in range(count):
            copies[j, c].wait()
            lanes = slice(c * LANES, (c + 1) * LANES)
            for a in range(4):
                rows = columns_ref[c, pl.ds(j * 256 + a, BLOCK, stride=4), :]
                own = slice(j * 256 + a * BLOCK, j * 256 + (a + 1) * BLOCK)
                own_high_ref[own, lanes], own_low_ref[own, lanes] = split(rows)
                for x in range(2):
                    at = slice(x * 256 + a * BLOCK, x * 256 + (a + 1) * BLOCK)
                    near[j][0][at, lanes], near[j][1][at, lanes] = split(rows * weights[x][:, lanes])

    def multiply(h):
        own = slice(h * 256, h * 256 + 256)
        for j in range(h, min(h + 3, 4)):
            grams[h][(j - h) * 512 : (j - h) * 512 + 512, :] = gram(
                near[j][0][...], near[j][1][...], own_high_ref[own, :], own_low_ref[own, :]
            )

    for tile in range(2):
        index_ref[tile] = nbr_ref[:, tile * LANES : (tile + 1) * LANES] - (start_ref[0] + tile * LANES)

    def pick(h):
        index = [part - BLOCK * (h % 2) for part in block_index(index_ref.at[h // 2], h % 2)]
        blocks = min(h + 3, 4) - h
        return fold(pick_pairs(grams[h], 0, blocks, index, own_deriv(dham_ref, dovl_ref, h // 2, h % 2)))

    def finish(tile, even, odd):
        pair = merge(even, odd)
        mine = slot_sum(pair)
        rows = 256 - tile * LANES
        theirs = spread(index_ref.at[tile], pair, spread_ref, rows)
        return mine, theirs

    prepare(3)
    multiply(3)
    prepare(2)
    multiply(2)
    pair3 = pick(3)
    prepare(1)
    multiply(1)
    pair2 = pick(2)
    prepare(0)
    mine1, theirs1 = finish(1, pair2, pair3)
    multiply(0)
    pair1 = pick(1)
    pair0 = pick(0)
    mine0, theirs0 = finish(0, pair0, pair1)
    force_ref[...] = jnp.zeros_like(force_ref)
    for k in range(3):
        force_ref[k : k + 1, :LANES] = 2.0 * (theirs0[k][:, :LANES] - mine0[k])
        force_ref[k : k + 1, LANES:] = 2.0 * (theirs0[k][:, LANES:] + theirs1[k] - mine1[k])


def cross_kernel(
    parity,
    start_ref, rows_ref, blocks_ref, occup_ref, energies_ref, nbr_ref, dham_ref, dovl_ref,
    own_high_ref, own_low_ref, near_high_ref, near_low_ref,
    force_ref, sent_ref,
    cut_high_ref, cut_low_ref, gram_ref, index_ref, spread_ref, columns_ref, copy_sem,
):
    atoms = nbr_ref.shape[1]
    states = rows_ref.shape[1]
    copies = [
        pltpu.make_async_copy(
            rows_ref.at[:, c * LANES : (c + 1) * LANES], columns_ref.at[c], copy_sem.at[c]
        )
        for c in range(states // LANES)
    ]
    for copy in copies:
        copy.start()
    force_ref[...] = jnp.zeros_like(force_ref)
    sent_ref[...] = jnp.zeros_like(sent_ref)
    for copy in copies:
        copy.wait()
    first = ((start_ref[0] // atoms) & 1) == parity

    @pl.when(first)
    def above():
        occup = occup_ref[...]
        weights = [occup, occup * energies_ref[...]]
        for c in range(states // LANES):
            lanes = slice(c * LANES, (c + 1) * LANES)
            for b in range(4):
                rows = columns_ref[c, pl.ds(b, BLOCK, stride=4), :]
                for x in range(2):
                    at = slice(x * 256 + b * BLOCK, x * 256 + (b + 1) * BLOCK)
                    cut_high_ref[at, lanes], cut_low_ref[at, lanes] = split(rows * weights[x][:, lanes])
        gram_ref[...] = gram(
            cut_high_ref[...], cut_low_ref[...], own_high_ref[512:, :], own_low_ref[512:, :]
        )
        index_ref[...] = nbr_ref[:, LANES:] - (start_ref[0] + atoms)
        even, odd = (
            fold(
                pick_pairs(
                    gram_ref, h * 256, 1, block_index(index_ref, h), own_deriv(dham_ref, dovl_ref, 1, h)
                )
            )
            for h in range(2)
        )
        pair = merge(even, odd)
        mine = slot_sum(pair)
        theirs = spread(index_ref, pair, spread_ref, BLOCK)
        for k in range(3):
            force_ref[k : k + 1, LANES:] = -2.0 * mine[k]
            sent_ref[k : k + 1, :BLOCK] = 2.0 * theirs[k]

    @pl.when(jnp.logical_not(first))
    def below():
        for c in range(states // LANES):
            lanes = slice(c * LANES, (c + 1) * LANES)
            for a in range(4):
                rows = columns_ref[c, pl.ds(a, BLOCK, stride=4), :]
                at = slice(a * BLOCK, (a + 1) * BLOCK)
                cut_high_ref[at, lanes], cut_low_ref[at, lanes] = split(rows)
        gram_ref[:, :256] = gram(
            near_high_ref[...], near_low_ref[...], cut_high_ref[:256, :], cut_low_ref[:256, :]
        )
        index_ref[...] = blocks_ref[48].astype(jnp.int32) - BLOCK
        index = [index_ref[8 * half : 8 * half + 8, :] for half in range(2)]

        def deriv(k, x, b, g, half):
            return blocks_ref[x * 24 + k * 8 + g * 4 + b, 8 * half : 8 * half + 8, :]

        pair = pick_pairs(gram_ref, 0, 1, index, deriv)
        theirs = spread(index_ref, pair, spread_ref, BLOCK)
        mine = slot_sum(fold(pair))
        for k in range(3):
            force_ref[k : k + 1, BLOCK:LANES] = 2.0 * theirs[k]
            sent_ref[k : k + 1, atoms - BLOCK :] = -2.0 * mine[k][:, BLOCK:]


def core_swap(value):
    return lax.ppermute(value, "sub", [(0, 1), (1, 0)])


def core_up(value):
    return lax.ppermute(value, "sub", [(0, 1)])


def shard_swap(value):
    count = lax.axis_size(SHARD)
    pairs = [pair for at in range(1, count - 1, 2) for pair in ((at, at + 1), (at + 1, at))]
    return lax.ppermute(value, SHARD, pairs)


def shard_up(value):
    count = lax.axis_size(SHARD)
    return lax.ppermute(value, SHARD, [(at, at + 1) for at in range(1, count - 1, 2)])


def local(coeffs, occup, energies, nbr, dham, dovl):
    slots, atoms = nbr.shape
    states = coeffs.shape[1]
    sub = lax.axis_index("sub")
    start = lax.axis_index(SHARD) * atoms

    far_rows = shard_swap(lax.dynamic_slice_in_dim(coeffs, sub * (4 * (atoms - BLOCK)), 4 * BLOCK))
    core_rows = core_swap(lax.dynamic_slice_in_dim(coeffs, (1 - sub) * (4 * (atoms - BLOCK)), 4 * BLOCK))
    last = nbr[:, atoms - BLOCK :]
    target = jnp.where(last >= 0, last - (start + atoms), -1).astype(jnp.float32)

    def parities(deriv):
        deriv = deriv[:, :, atoms - BLOCK :].reshape(3, 2, 2, 4, slots, BLOCK)
        return jnp.concatenate([deriv[:, :, 0], deriv[:, :, 1]], -1).reshape(24, slots, LANES)

    blocks = jnp.concatenate(
        [parities(dham), -parities(dovl), jnp.concatenate([target, target], 1)[None]], 0
    )
    core_blocks = core_up(blocks)
    far_blocks = shard_up(blocks)
    start = start.reshape(1).astype(jnp.int32)
    occup = occup.reshape(1, states)
    energies = energies.reshape(1, states)

    vmem = pl.BlockSpec(memory_space=pltpu.VMEM)
    hbm = pl.BlockSpec(memory_space=pl.ANY)
    smem = pl.BlockSpec(memory_space=pltpu.SMEM)
    half = jax.ShapeDtypeStruct((512, states), jnp.bfloat16)
    whole = jax.ShapeDtypeStruct((4 * atoms, states), jnp.bfloat16)
    force = jax.ShapeDtypeStruct((8, atoms), jnp.float32)
    prepared = pltpu.VMEM((512, states), jnp.bfloat16)
    own_high, own_low, near_high, near_low, inner = pl.pallas_call(
        inner_kernel,
        out_shape=(whole, whole, half, half, force),
        in_specs=[smem, hbm] + [vmem] * 5,
        out_specs=(vmem,) * 5,
        scratch_shapes=[prepared] * 6
        + [pltpu.VMEM((512 * n, 256), jnp.float32) for n in (3, 3, 2, 1)]
        + [
            pltpu.VMEM((2, slots, LANES), jnp.int32),
            pltpu.VMEM((3, atoms, LANES), jnp.float32),
            pltpu.VMEM((states // LANES, 4 * atoms, LANES), jnp.float32),
            pltpu.SemaphoreType.DMA((4 * states // LANES,)),
        ],
        compiler_params=pltpu.CompilerParams(vmem_limit_bytes=32 * 1024 * 1024),
        cost_estimate=pl.CostEstimate(
            flops=3 * 2 * 9 * 512 * 256 * states, bytes_accessed=16 * 1024 * 1024, transcendentals=0
        ),
        name="inner_pairs",
    )(start, coeffs, occup, energies, nbr, dham, dovl)

    def cross(parity, rows, blocks, name):
        return pl.pallas_call(
            functools.partial(cross_kernel, parity),
            out_shape=(force, force),
            in_specs=[smem, hbm] + [vmem] * 10,
            out_specs=(vmem, vmem),
            scratch_shapes=[
                prepared,
                prepared,
                pltpu.VMEM((512, 512), jnp.float32),
                pltpu.VMEM((slots, LANES), jnp.int32),
                pltpu.VMEM((3, BLOCK, LANES), jnp.float32),
                pltpu.VMEM((states // LANES, 4 * BLOCK, LANES), jnp.float32),
                pltpu.SemaphoreType.DMA((states // LANES,)),
            ],
            compiler_params=pltpu.CompilerParams(vmem_limit_bytes=20 * 1024 * 1024),
            cost_estimate=pl.CostEstimate(
                flops=3 * 2 * 2 * 512 * 256 * states, bytes_accessed=6 * 1024 * 1024, transcendentals=0
            ),
            name=name,
        )(start, rows, blocks, occup, energies, nbr, dham, dovl, own_high, own_low, near_high, near_low)

    core_force, core_sent = cross(0, core_rows, core_blocks, "core_pairs")
    core_back = core_swap(core_sent[:3])
    far_force, far_sent = cross(1, far_rows, far_blocks, "far_pairs")
    far_back = shard_swap(far_sent[:3])
    total = inner[:3] + core_force[:3] + core_back + far_force[:3] + far_back
    return lax.psum(total, "states")


def solution(mesh):
    in_specs = (
        P(("groups", "atoms", "sub"), "states"),
        P(("groups", "states")),
        P(("groups", "states")),
        P(None, ("groups", "atoms", "sub")),
        P(None, None, ("groups", "atoms", "sub")),
        P(None, None, ("groups", "atoms", "sub")),
    )
    out_specs = P(None, ("groups", "atoms", "sub"))
    return jax.shard_map(local, mesh=mesh, in_specs=in_specs, out_specs=out_specs, check_vma=False)
```

time: 137 us -> 45.7 us (0.33); the launches traced: 135 us -> 45.5 us
  matrix products: 49.3 us -> 0 us
  local copies, waits for them, and re-layouts: 31.5 us -> 3.66 us
  waiting for transfers between devices: 27.5 us -> 1.28 us
  Pallas kernels: 0 us -> 22.5 us
  other arithmetic: 18.4 us -> 0.4 us
  starting transfers between devices: 3.89 us -> 12.8 us
    dot_general x6 -> x0, matrix products: 49.3 us -> none  [the longest x2 35.3 us: step(): jnp.einsum('xrs,cs->xrc', scaled, near_rows, precision=lax.Precision.HIGH...]
    ppermute x2 -> x6, waiting for transfers between devices: 27.5 us -> 1.28 us  [the longest x2 1.27 us: shard_swap(): return lax.ppermute(value, SHARD, pairs)]
    pallas_call x0 -> x3, Pallas kernels: none -> 22.5 us  [the longest x1 16.7 us: local(): pl.pallas_call(inner_kernel, out_shape=(whole, whole, half, half, force),...]
    reshape x2 -> x0, local copies, waits for them, and re-layouts: 10.4 us -> none  [step(): near_rows.reshape(span, 4, states_local).transpose(1, 0, 2)]
    dynamic_slice x4 -> x1, local copies, waits for them, and re-layouts: 13.2 us -> 3.24 us  [local(): lax.dynamic_slice_in_dim(coeffs, (1 - sub) * (4 * (atoms - BLOCK)), 4 * B...]
    ppermute x2 -> x6, starting transfers between devices: 3.89 us -> 12.8 us  [the longest x2 8.2 us: shard_swap(): return lax.ppermute(value, SHARD, pairs)]
    concatenate x1, other arithmetic: 6.61 us -> 0.12 us  [local(): jnp.concatenate([parities(dham), -parities(dovl), jnp.concatenate([target...]
    mul x3 -> x0, other arithmetic: 5.6 us -> none  [the longest x2 5.6 us: step(): scaled = own_rows[None] * weights[:, None, :]]
  transfers between devices with their start and end apart: 2 -> 6, of which waited for: 2 -> 1; matrix products, arithmetic and copies ran while one was open for 0% -> 2% of each run, Pallas kernels for 0% -> 45%
where the time goes in v2:
time: 45.7 us; the launch traced here: 45.5 us
  Pallas kernels  22.5 us (49%)
  starting transfers between devices  12.8 us (28%)
  blocking collectives  4.62 us (10%)
  local copies, waits for them, and re-layouts  3.66 us (8%)
  waiting for transfers between devices  1.28 us (3%)
    pallas_call x1, Pallas kernels, local(): pl.pallas_call(inner_kernel, out_shape=(whole, whole, half, half, force),...  16.7 us
    ppermute x2, starting transfers between devices, shard_swap(): return lax.ppermute(value, SHARD, pairs)  8.2 us
    pallas_call x2, Pallas kernels, cross(): pl.pallas_call(functools.partial(cross_kernel, parity), out_shape=(force,...  5.79 us
    psum x1, blocking collectives, local(): return lax.psum(total, 'states')  4.62 us
    dynamic_slice x1, local copies, waits for them, and re-layouts, local(): lax.dynamic_slice_in_dim(coeffs, (1 - sub) * (4 * (atoms - BLOCK)), 4 * B...  3.24 us
    ppermute x1, starting transfers between devices, shard_up(): lax.ppermute(value, SHARD, [(at, at + 1) for at in range(1, count - 1, 2)])  2.07 us
    ppermute x1, starting transfers between devices, core_up(): return lax.ppermute(value, 'sub', [(0, 1)])  1.29 us
    ppermute x2, waiting for transfers between devices, shard_swap(): return lax.ppermute(value, SHARD, pairs)  1.27 us
  transfers between devices with their start and end apart: 6, of which 1 were waited for; matrix products, arithmetic and copies ran while one was open for 2% of the time, Pallas kernels for 45%

profile of v2, /device:TPU:1, one launch (start us, length us, event | category | flops | bytes accessed | tf_op | source)
XLA Modules:
  0.0 45.5 jit_solution(10302922961154360264)
XLA Ops:
  0.0 0.0 copy-start.4
  0.0 0.0 copy-start.5
  0.0 3.2 %constant_dynamic-slice_fusion.1 = (f32[256,1024]{1,0:T(8,128)}, f32[256,1024]{1,0:T(8,128)}) fusion(f32[1024,1024]{1,0:T(8,128)} %coeffs_ref.1, s32[]{:T(128)S(6)} %select_n.10, s32[]{:T(128)S(6)} %select_n.12), kind=kLoop, calls=%fused_computation.6 | loop fusion | bytes 4194312 | tf_op jit(solution)/shard_map/dynamic_slice | solution.py:314
  3.3 0.0 collective-permute-start
  3.3 4.5 %collective-permute-start.3 = (f32[256,1024]{1,0:T(8,128)}, f32[256,1024]{1,0:T(8,128)}, u32[]{:S(2)}, u32[]{:S(2)}) collective-permute-start(f32[256,1024]{1,0:T(8,128)} %get-tuple-element.24), channel_id=1, source_target_pairs={{1,4},{4,1},{5,8},{8,5},{9,12},{12,9},{3,6},{6,3},{7,10},{10,7},{1... | collective-permute-start | bytes 3145736 | tf_op jit(solution)/shard_map/ppermute | solution.py:299
  7.9 0.0 copy-done.1
  7.9 0.0 copy-start.2
  7.9 0.2 slice.37
  8.1 0.0 copy-done
  8.1 0.2 slice.40
  8.3 0.0 copy-done.3
  8.3 0.1 select_convert_fusion
  8.4 0.1 maximum_negate_fusion
  8.5 0.1 maximum_bitcast_fusion
  8.6 0.1 pad_maximum_fusion
  8.7 2.1 %collective-permute-start.4 = (f32[49,16,128]{2,1,0:T(8,128)S(1)}, f32[49,16,128]{2,1,0:T(8,128)S(1)}, u32[]{:S(2)}, u32[]{:S(2)}) collective-permute-start(f32[49,16,128]{2,1,0:T(8,128)S(1)} %pad_maximum_fusion), channel_id=1, source_target_pairs={{1,4},{5,8},{9,12},{3,6},{7,10},{11,14},{17,20},{21,24},{25,28},{1... | collective-permute-start | bytes 1204232 | tf_op jit(solution)/shard_map/ppermute | solution.py:304
  10.8 1.3 %collective-permute-start.1 = (f32[49,16,128]{2,1,0:T(8,128)S(1)}, f32[49,16,128]{2,1,0:T(8,128)S(1)}, u32[]{:S(2)}, u32[]{:S(2)}) collective-permute-start(f32[49,16,128]{2,1,0:T(8,128)S(1)} %pad_maximum_fusion), channel_id=1, source_target_pairs={{0,1},{2,3},{4,5},{6,7},{8,9},{10,11},{12,13},{14,15},{16,17},{18,... | collective-permute-start | bytes 1204232 | tf_op jit(solution)/shard_map/ppermute | solution.py:293
  12.1 0.0 copy-done.4
  12.1 0.0 copy-done.5
  12.1 0.0 copy-done.2
  12.2 16.7 %inner_pairs.1 = (bf16[1024,1024]{1,0:T(8,128)(2,1)S(1)}, bf16[1024,1024]{1,0:T(8,128)(2,1)S(1)}, bf16[512,1024]{1,0:T(8,128)(2,1)S(1)}, bf16[512,1024]{1,0:T(8,128)(2,1)S(1)}, f32[8,256]{1,0:T(8,128)S(1)}) custom-call(s32[1]{0:T(128)} %bitcast.start_ref, f32[1024,1024]{1,0:T(8,128)S(1)} %copy-done.2, f32[1,1024]{1,0:T(1,128)S(1)} %bitcast.19, ...), custom_call_target="tpu_custom_call" | custom-call | flops 7247757312 | bytes 16777216 | tf_op jit(solution)/shard_map/inner_pairs/pallas_call | solution.py:338
  28.8 0.0 collective-permute-done.4.blocks_ref
  28.9 0.0 collective-permute-done.3.rows_ref
  28.9 3.7 %far_pairs.1 = (f32[8,256]{1,0:T(8,128)S(1)}, f32[8,256]{1,0:T(8,128)S(1)}) custom-call(s32[1]{0:T(128)} %bitcast.start_ref, f32[256,1024]{1,0:T(8,128)} %collective-permute-done.3.rows_ref, f32[49,16,128]{2,1,0:T(8,128)S(1)} %collective-permute-done.4.blocks_ref, f32[1,1024]{1,0:T(1,128)S(1)} %bitcast.20, f32[1,1024]{1,0:T(1,128)S(1)} %bitcast.23, ...), custom_call_target="tpu_custom_call" | custom-call | flops 1610612736 | bytes 6291456 | tf_op jit(solution)/shard_map/far_pairs/pallas_call | solution.py:359
  32.6 0.0 collective-permute-done.1.blocks_ref
  32.6 0.0 collective-permute-done.rows_ref
  32.6 2.0 %core_pairs.1 = (f32[8,256]{1,0:T(8,128)S(1)}, f32[8,256]{1,0:T(8,128)S(1)}) custom-call(s32[1]{0:T(128)} %bitcast.start_ref, f32[256,1024]{1,0:T(8,128)S(1)} %collective-permute-done.rows_ref, f32[49,16,128]{2,1,0:T(8,128)S(1)} %collective-permute-done.1.blocks_ref, f32[1,1024]{1,0:T(1,128)S(1)} %bitcast.21, f32[1,1024]{1,0:T(1,128)S(1)} %bitcast.24, ...), custom_call_target="tpu_custom_call" | custom-call | flops 1610612736 | bytes 6291456 | tf_op jit(solution)/shard_map/core_pairs/pallas_call | solution.py:359
  34.7 1.2 %collective-permute-start.2 = (f32[3,256]{1,0:T(4,128)S(1)}, f32[3,256]{1,0:T(4,128)S(1)}, u32[]{:S(2)}, u32[]{:S(2)}) collective-permute-start(f32[3,256]{1,0:T(4,128)S(1)} %slice.45), channel_id=1, source_target_pairs={{0,1},{1,0},{2,3},{3,2},{4,5},{5,4},{6,7},{7,6},{8,9},{9,8},{10,11... | collective-permute-start | bytes 9224 | tf_op jit(solution)/shard_map/ppermute | solution.py:289
  35.9 3.7 %collective-permute-start.5 = (f32[3,256]{1,0:T(4,128)S(1)}, f32[3,256]{1,0:T(4,128)S(1)}, u32[]{:S(2)}, u32[]{:S(2)}) collective-permute-start(f32[3,256]{1,0:T(4,128)S(1)} %slice.47), channel_id=1, source_target_pairs={{1,4},{4,1},{5,8},{8,5},{9,12},{12,9},{3,6},{6,3},{7,10},{10,7},{1... | collective-permute-start | bytes 9224 | tf_op jit(solution)/shard_map/ppermute | solution.py:299
  39.6 0.0 collective-permute-done.2
  39.6 1.3 %collective-permute-done.5 = f32[3,256]{1,0:T(4,128)S(1)} collective-permute-done((f32[3,256]{1,0:T(4,128)S(1)}, f32[3,256]{1,0:T(4,128)S(1)}, u32[]{:S(2)}, u32[]{:S(2)}) %collective-permute-start.5) | collective-permute-done | bytes 3104 | tf_op jit(solution)/shard_map/ppermute | solution.py:299
  40.9 4.6 %psum.7 = f32[3,256]{1,0:T(4,128)} all-reduce(f32[3,256]{1,0:T(4,128)S(1)} %add_add_fusion), channel_id=1, replica_groups=mesh['groups'=2,'atoms'=4,'states'=2,'sub'=2] {'states'}, use_global_device_ids=true, to_apply=%region_0.1 | all-reduce | flops 768 | bytes 6144 | tf_op jit(solution)/shard_map/psum | solution.py:385
  (8 shorter events, 0.1 us)
Async XLA Ops:
  0.0 7.9 %copy-start.1 = (f32[48,16,256]{2,1,0:T(8,128)S(1)}, f32[48,16,256]{2,1,0:T(8,128)}, u32[]{:S(2)}) copy-start(f32[48,16,256]{2,1,0:T(8,128)} %dham_ref.5) | copy-start | bytes 2359300
  0.0 8.1 %copy-start = (f32[48,16,256]{2,1,0:T(8,128)S(1)}, f32[48,16,256]{2,1,0:T(8,128)}, u32[]{:S(2)}) copy-start(f32[48,16,256]{2,1,0:T(8,128)} %dovl_ref.5) | copy-start | bytes 2359300
  0.0 8.3 %copy-start.3 = (s32[16,256]{1,0:T(8,128)S(1)}, s32[16,256]{1,0:T(8,128)}, u32[]{:S(2)}) copy-start(s32[16,256]{1,0:T(8,128)} %nbr_ref.5) | copy-start | bytes 49156
  0.0 12.1 %copy-start.4 = (f32[1024]{0:T(1024)S(1)}, f32[1024]{0:T(1024)}, u32[]{:S(2)}) copy-start(f32[1024]{0:T(1024)} %param.7) | copy-start | bytes 12292
  0.0 12.1 %copy-start.5 = (f32[1024]{0:T(1024)S(1)}, f32[1024]{0:T(1024)}, u32[]{:S(2)}) copy-start(f32[1024]{0:T(1024)} %param.8) | copy-start | bytes 12292
  3.3 29.4 %collective-permute-start = (f32[256,1024]{1,0:T(8,128)}, f32[256,1024]{1,0:T(8,128)S(1)}, u32[]{:S(2)}, u32[]{:S(2)}) collective-permute-start(f32[256,1024]{1,0:T(8,128)} %get-tuple-element.23), channel_id=1, source_target_pairs={{0,1},{1,0},{2,3},{3,2},{4,5},{5,4},{6,7},{7,6},{8,9},{9,8},{10,11... | collective-permute-start | bytes 3145736 | tf_op jit(solution)/shard_map/ppermute | solution.py:289
  3.3 25.5 %collective-permute-start.3 = (f32[256,1024]{1,0:T(8,128)}, f32[256,1024]{1,0:T(8,128)}, u32[]{:S(2)}, u32[]{:S(2)}) collective-permute-start(f32[256,1024]{1,0:T(8,128)} %get-tuple-element.24), channel_id=1, source_target_pairs={{1,4},{4,1},{5,8},{8,5},{9,12},{12,9},{3,6},{6,3},{7,10},{10,7},{1... | collective-permute-start | bytes 3145736 | tf_op jit(solution)/shard_map/ppermute | solution.py:299
  7.9 4.3 %copy-start.2 = (f32[1024,1024]{1,0:T(8,128)S(1)}, f32[1024,1024]{1,0:T(8,128)}, u32[]{:S(2)}) copy-start(f32[1024,1024]{1,0:T(8,128)} %coeffs_ref.1) | copy-start | bytes 12582916
  8.7 20.1 %collective-permute-start.4 = (f32[49,16,128]{2,1,0:T(8,128)S(1)}, f32[49,16,128]{2,1,0:T(8,128)S(1)}, u32[]{:S(2)}, u32[]{:S(2)}) collective-permute-start(f32[49,16,128]{2,1,0:T(8,128)S(1)} %pad_maximum_fusion), channel_id=1, source_target_pairs={{1,4},{5,8},{9,12},{3,6},{7,10},{11,14},{17,20},{21,24},{25,28},{1... | collective-permute-start | bytes 1204232 | tf_op jit(solution)/shard_map/ppermute | solution.py:304
  10.8 21.8 %collective-permute-start.1 = (f32[49,16,128]{2,1,0:T(8,128)S(1)}, f32[49,16,128]{2,1,0:T(8,128)S(1)}, u32[]{:S(2)}, u32[]{:S(2)}) collective-permute-start(f32[49,16,128]{2,1,0:T(8,128)S(1)} %pad_maximum_fusion), channel_id=1, source_target_pairs={{0,1},{2,3},{4,5},{6,7},{8,9},{10,11},{12,13},{14,15},{16,17},{18,... | collective-permute-start | bytes 1204232 | tf_op jit(solution)/shard_map/ppermute | solution.py:293
  34.7 4.9 %collective-permute-start.2 = (f32[3,256]{1,0:T(4,128)S(1)}, f32[3,256]{1,0:T(4,128)S(1)}, u32[]{:S(2)}, u32[]{:S(2)}) collective-permute-start(f32[3,256]{1,0:T(4,128)S(1)} %slice.45), channel_id=1, source_target_pairs={{0,1},{1,0},{2,3},{3,2},{4,5},{5,4},{6,7},{7,6},{8,9},{9,8},{10,11... | collective-permute-start | bytes 9224 | tf_op jit(solution)/shard_map/ppermute | solution.py:289
  35.9 4.9 %collective-permute-start.5 = (f32[3,256]{1,0:T(4,128)S(1)}, f32[3,256]{1,0:T(4,128)S(1)}, u32[]{:S(2)}, u32[]{:S(2)}) collective-permute-start(f32[3,256]{1,0:T(4,128)S(1)} %slice.47), channel_id=1, source_target_pairs={{1,4},{4,1},{5,8},{8,5},{9,12},{12,9},{3,6},{6,3},{7,10},{10,7},{1... | collective-permute-start | bytes 9224 | tf_op jit(solution)/shard_map/ppermute | solution.py:299

commit v3 on v2

--- a/solution.py
+++ b/solution.py
@@ -9,6 +9,7 @@
 
 LANES = 128
 BLOCK = 64
+UPPER = 48
 SHARD = ("atoms", "sub")
 
 
@@ -42,16 +43,17 @@
     return jnp.where(lane_numbers() < BLOCK, left, swap_halves(right))
 
 
-def pick_pairs(gram_ref, column, blocks, index, deriv):
+def pick_pairs(gram_ref, column, size, index, deriv, blocks=1):
     low = [part & 7 for part in index]
     high = [part >> 3 for part in index]
     pair = [[None, None] for k in range(3)]
     for x in range(2):
         picked = {}
-        for r in range(8 * blocks):
+        for r in range(size // 8 * blocks):
             hit = [part == r for part in high]
             for b in range(4):
-                row = (r // 8) * 512 + x * 256 + b * BLOCK + (r % 8) * 8
+                block, part = divmod(r, size // 8)
+                row = ((block * 2 + x) * 4 + b) * size + part * 8
                 for g in range(2):
                     at = column + g * LANES
                     tile = gram_ref[row : row + 8, at : at + LANES]
@@ -178,7 +180,7 @@
     def pick(h):
         index = [part - BLOCK * (h % 2) for part in block_index(index_ref.at[h // 2], h % 2)]
         blocks = min(h + 3, 4) - h
-        return fold(pick_pairs(grams[h], 0, blocks, index, own_deriv(dham_ref, dovl_ref, h // 2, h % 2)))
+        return fold(pick_pairs(grams[h], 0, BLOCK, index, own_deriv(dham_ref, dovl_ref, h // 2, h % 2), blocks))
 
     def finish(tile, even, odd):
         pair = merge(even, odd)
@@ -187,17 +189,13 @@
         theirs = spread(index_ref.at[tile], pair, spread_ref, rows)
         return mine, theirs
 
-    prepare(3)
-    multiply(3)
-    prepare(2)
-    multiply(2)
+    for j in (3, 2, 1, 0):
+        prepare(j)
+    for h in (3, 2, 1, 0):
+        multiply(h)
     pair3 = pick(3)
-    prepare(1)
-    multiply(1)
     pair2 = pick(2)
-    prepare(0)
     mine1, theirs1 = finish(1, pair2, pair3)
-    multiply(0)
     pair1 = pick(1)
     pair0 = pick(0)
     mine0, theirs0 = finish(0, pair0, pair1)
@@ -207,39 +205,95 @@
         force_ref[k : k + 1, LANES:] = 2.0 * (theirs0[k][:, LANES:] + theirs1[k] - mine1[k])
 
 
+def payload_rows(atoms, states):
+    planes = -(-48 // (states // LANES))
+    return max(4 * (atoms // 2 - UPPER), 4 * UPPER + 16 * planes + 16)
+
+
+def pack_kernel(
+    start_ref, coeffs_ref, nbr_ref, dham_ref, dovl_ref, core_ref, far_ref,
+    ham_ref, ovl_ref, core_sem, far_sem, deriv_sem,
+):
+    atoms = nbr_ref.shape[1]
+    count, rows, unused = core_ref.shape
+    lower = 4 * (atoms // 2 - UPPER)
+    first = ((start_ref[0] // atoms) & 1) == 0
+    fetched = [
+        pltpu.make_async_copy(source.at[:, :, atoms - LANES :], target, deriv_sem.at[at])
+        for at, (source, target) in enumerate([(dham_ref, ham_ref), (dovl_ref, ovl_ref)])
+    ]
+
+    def fill(up_ref, up_sem, down_ref, down_sem):
+        copies = []
+        for c in range(count):
+            lanes = slice(c * LANES, (c + 1) * LANES)
+            up_rows = coeffs_ref.at[4 * (atoms - UPPER) :, lanes]
+            copies.append(pltpu.make_async_copy(up_rows, up_ref.at[c, : 4 * UPPER, :], up_sem.at[c]))
+            down_rows = coeffs_ref.at[:lower, lanes]
+            copies.append(pltpu.make_async_copy(down_rows, down_ref.at[c, :lower, :], down_sem.at[c]))
+        for copy in fetched + copies:
+            copy.start()
+        if rows > lower:
+            down_ref[:, lower:, :] = jnp.zeros((count, rows - lower, LANES), jnp.float32)
+        up_ref[:, 4 * UPPER :, :] = jnp.zeros((count, rows - 4 * UPPER, LANES), jnp.float32)
+        planes = -(-48 // count)
+        last = nbr_ref[:, atoms - LANES :]
+        target = jnp.where(last >= 0, last - (start_ref[0] + atoms), -1).astype(jnp.float32)
+        at = 4 * UPPER + 16 * planes
+        for half in range(2):
+            part = target[8 * half : 8 * half + 8]
+            up_ref[0, at + 8 * half : at + 8 * half + 8, :] = side_by_side(part, part, 1)
+        for copy in fetched:
+            copy.wait()
+        for x, ref in enumerate((ham_ref, ovl_ref)):
+            for k in range(3):
+                for g in range(2):
+                    for b in range(4):
+                        plane = x * 24 + k * 8 + g * 4 + b
+                        for half in range(2):
+                            parts = [
+                                ref[k * 16 + (2 * g + parity) * 4 + b, 8 * half : 8 * half + 8, :]
+                                for parity in range(2)
+                            ]
+                            both = side_by_side(parts[0], parts[1], 1)
+                            at = 4 * UPPER + 16 * (plane // count) + 8 * half
+                            up_ref[plane % count, at : at + 8, :] = -both if x else both
+        for copy in copies:
+            copy.wait()
+
+    @pl.when(first)
+    def even():
+        fill(core_ref, core_sem, far_ref, far_sem)
+
+    @pl.when(jnp.logical_not(first))
+    def odd():
+        fill(far_ref, far_sem, core_ref, core_sem)
+
+
 def cross_kernel(
     parity,
-    start_ref, rows_ref, blocks_ref, occup_ref, energies_ref, nbr_ref, dham_ref, dovl_ref,
+    start_ref, payload_ref, before_ref, back_ref, occup_ref, energies_ref, nbr_ref, dham_ref, dovl_ref,
     own_high_ref, own_low_ref, near_high_ref, near_low_ref,
     force_ref, sent_ref,
-    cut_high_ref, cut_low_ref, gram_ref, index_ref, spread_ref, columns_ref, copy_sem,
+    cut_high_ref, cut_low_ref, gram_ref, index_ref, spread_ref,
 ):
     atoms = nbr_ref.shape[1]
-    states = rows_ref.shape[1]
-    copies = [
-        pltpu.make_async_copy(
-            rows_ref.at[:, c * LANES : (c + 1) * LANES], columns_ref.at[c], copy_sem.at[c]
-        )
-        for c in range(states // LANES)
-    ]
-    for copy in copies:
-        copy.start()
-    force_ref[...] = jnp.zeros_like(force_ref)
+    count = payload_ref.shape[0]
+    lower = atoms // 2 - UPPER
+    force_ref[...] = before_ref[...] + back_ref[...]
     sent_ref[...] = jnp.zeros_like(sent_ref)
-    for copy in copies:
-        copy.wait()
     first = ((start_ref[0] // atoms) & 1) == parity
 
     @pl.when(first)
     def above():
         occup = occup_ref[...]
         weights = [occup, occup * energies_ref[...]]
-        for c in range(states // LANES):
+        for c in range(count):
             lanes = slice(c * LANES, (c + 1) * LANES)
             for b in range(4):
-                rows = columns_ref[c, pl.ds(b, BLOCK, stride=4), :]
+                rows = payload_ref[c, pl.ds(b, lower, stride=4), :]
                 for x in range(2):
-                    at = slice(x * 256 + b * BLOCK, x * 256 + (b + 1) * BLOCK)
+                    at = slice((x * 4 + b) * lower, (x * 4 + b + 1) * lower)
                     cut_high_ref[at, lanes], cut_low_ref[at, lanes] = split(rows * weights[x][:, lanes])
         gram_ref[...] = gram(
             cut_high_ref[...], cut_low_ref[...], own_high_ref[512:, :], own_low_ref[512:, :]
@@ -248,49 +302,54 @@
         even, odd = (
             fold(
                 pick_pairs(
-                    gram_ref, h * 256, 1, block_index(index_ref, h), own_deriv(dham_ref, dovl_ref, 1, h)
+                    gram_ref, h * 256, lower, block_index(index_ref, h), own_deriv(dham_ref, dovl_ref, 1, h)
                 )
             )
             for h in range(2)
         )
         pair = merge(even, odd)
         mine = slot_sum(pair)
-        theirs = spread(index_ref, pair, spread_ref, BLOCK)
+        theirs = spread(index_ref, pair, spread_ref, lower)
         for k in range(3):
-            force_ref[k : k + 1, LANES:] = -2.0 * mine[k]
-            sent_ref[k : k + 1, :BLOCK] = 2.0 * theirs[k]
+            force_ref[k : k + 1, LANES:] += -2.0 * mine[k]
+            sent_ref[k : k + 1, :lower] = 2.0 * theirs[k]
 
     @pl.when(jnp.logical_not(first))
     def below():
-        for c in range(states // LANES):
+        skip = BLOCK - UPPER
+        for c in range(count):
             lanes = slice(c * LANES, (c + 1) * LANES)
             for a in range(4):
-                rows = columns_ref[c, pl.ds(a, BLOCK, stride=4), :]
-                at = slice(a * BLOCK, (a + 1) * BLOCK)
+                rows = payload_ref[c, pl.ds(a, UPPER, stride=4), :]
+                at = slice(a * BLOCK + skip, (a + 1) * BLOCK)
                 cut_high_ref[at, lanes], cut_low_ref[at, lanes] = split(rows)
-        gram_ref[:, :256] = gram(
+                at = slice(a * BLOCK, a * BLOCK + skip)
+                cut_high_ref[at, lanes] = jnp.zeros((skip, LANES), jnp.bfloat16)
+                cut_low_ref[at, lanes] = jnp.zeros((skip, LANES), jnp.bfloat16)
+        gram_ref[:512, :256] = gram(
             near_high_ref[...], near_low_ref[...], cut_high_ref[:256, :], cut_low_ref[:256, :]
         )
-        index_ref[...] = blocks_ref[48].astype(jnp.int32) - BLOCK
+        planes = -(-48 // count)
+        at = 4 * UPPER + 16 * planes
+        target = payload_ref[0, at : at + 16, :].astype(jnp.int32)
+        index_ref[...] = jnp.where(target >= lower, target - BLOCK, -1)
         index = [index_ref[8 * half : 8 * half + 8, :] for half in range(2)]
 
         def deriv(k, x, b, g, half):
-            return blocks_ref[x * 24 + k * 8 + g * 4 + b, 8 * half : 8 * half + 8, :]
-
-        pair = pick_pairs(gram_ref, 0, 1, index, deriv)
+            plane = x * 24 + k * 8 + g * 4 + b
+            at = 4 * UPPER + 16 * (plane // count) + 8 * half
+            return payload_ref[plane % count, at : at + 8, :]
+
+        pair = pick_pairs(gram_ref, 0, BLOCK, index, deriv)
         theirs = spread(index_ref, pair, spread_ref, BLOCK)
         mine = slot_sum(fold(pair))
         for k in range(3):
-            force_ref[k : k + 1, BLOCK:LANES] = 2.0 * theirs[k]
+            force_ref[k : k + 1, BLOCK:LANES] += 2.0 * theirs[k]
             sent_ref[k : k + 1, atoms - BLOCK :] = -2.0 * mine[k][:, BLOCK:]
 
 
 def core_swap(value):
     return lax.ppermute(value, "sub", [(0, 1), (1, 0)])
-
-
-def core_up(value):
-    return lax.ppermute(value, "sub", [(0, 1)])
 
 
 def shard_swap(value):
@@ -299,42 +358,40 @@
     return lax.ppermute(value, SHARD, pairs)
 
 
-def shard_up(value):
-    count = lax.axis_size(SHARD)
-    return lax.ppermute(value, SHARD, [(at, at + 1) for at in range(1, count - 1, 2)])
-
-
 def local(coeffs, occup, energies, nbr, dham, dovl):
     slots, atoms = nbr.shape
     states = coeffs.shape[1]
-    sub = lax.axis_index("sub")
-    start = lax.axis_index(SHARD) * atoms
-
-    far_rows = shard_swap(lax.dynamic_slice_in_dim(coeffs, sub * (4 * (atoms - BLOCK)), 4 * BLOCK))
-    core_rows = core_swap(lax.dynamic_slice_in_dim(coeffs, (1 - sub) * (4 * (atoms - BLOCK)), 4 * BLOCK))
-    last = nbr[:, atoms - BLOCK :]
-    target = jnp.where(last >= 0, last - (start + atoms), -1).astype(jnp.float32)
-
-    def parities(deriv):
-        deriv = deriv[:, :, atoms - BLOCK :].reshape(3, 2, 2, 4, slots, BLOCK)
-        return jnp.concatenate([deriv[:, :, 0], deriv[:, :, 1]], -1).reshape(24, slots, LANES)
-
-    blocks = jnp.concatenate(
-        [parities(dham), -parities(dovl), jnp.concatenate([target, target], 1)[None]], 0
-    )
-    core_blocks = core_up(blocks)
-    far_blocks = shard_up(blocks)
-    start = start.reshape(1).astype(jnp.int32)
+    start = (lax.axis_index(SHARD) * atoms).reshape(1).astype(jnp.int32)
     occup = occup.reshape(1, states)
     energies = energies.reshape(1, states)
+    count = states // LANES
 
     vmem = pl.BlockSpec(memory_space=pltpu.VMEM)
-    hbm = pl.BlockSpec(memory_space=pl.ANY)
+    hbm = pl.BlockSpec(memory_space=pltpu.HBM)
     smem = pl.BlockSpec(memory_space=pltpu.SMEM)
     half = jax.ShapeDtypeStruct((512, states), jnp.bfloat16)
     whole = jax.ShapeDtypeStruct((4 * atoms, states), jnp.bfloat16)
     force = jax.ShapeDtypeStruct((8, atoms), jnp.float32)
     prepared = pltpu.VMEM((512, states), jnp.bfloat16)
+    lower = atoms // 2 - UPPER
+    payload = jax.ShapeDtypeStruct((count, payload_rows(atoms, states), LANES), jnp.float32)
+    core_payload, far_payload = pl.pallas_call(
+        pack_kernel,
+        out_shape=(payload, payload),
+        in_specs=[smem, hbm, vmem, hbm, hbm],
+        out_specs=(vmem, vmem),
+        scratch_shapes=[
+            pltpu.VMEM((48, slots, LANES), jnp.float32),
+            pltpu.VMEM((48, slots, LANES), jnp.float32),
+            pltpu.SemaphoreType.DMA((count,)),
+            pltpu.SemaphoreType.DMA((count,)),
+            pltpu.SemaphoreType.DMA((2,)),
+        ],
+        compiler_params=pltpu.CompilerParams(vmem_limit_bytes=52 * 1024 * 1024),
+        name="pack",
+    )(start, coeffs, nbr, dham, dovl)
+    far_payload = shard_swap(far_payload)
+    core_payload = core_swap(core_payload)
     own_high, own_low, near_high, near_low, inner = pl.pallas_call(
         inner_kernel,
         out_shape=(whole, whole, half, half, force),
@@ -355,33 +412,32 @@
         name="inner_pairs",
     )(start, coeffs, occup, energies, nbr, dham, dovl)
 
-    def cross(parity, rows, blocks, name):
+    def cross(parity, payload, before, back, name):
+        cut = pltpu.VMEM((8 * lower, states), jnp.bfloat16)
         return pl.pallas_call(
             functools.partial(cross_kernel, parity),
             out_shape=(force, force),
-            in_specs=[smem, hbm] + [vmem] * 10,
+            in_specs=[smem] + [vmem] * 12,
             out_specs=(vmem, vmem),
             scratch_shapes=[
-                prepared,
-                prepared,
-                pltpu.VMEM((512, 512), jnp.float32),
+                cut,
+                cut,
+                pltpu.VMEM((8 * lower, 512), jnp.float32),
                 pltpu.VMEM((slots, LANES), jnp.int32),
-                pltpu.VMEM((3, BLOCK, LANES), jnp.float32),
-                pltpu.VMEM((states // LANES, 4 * BLOCK, LANES), jnp.float32),
-                pltpu.SemaphoreType.DMA((states // LANES,)),
+                pltpu.VMEM((3, lower, LANES), jnp.float32),
             ],
             compiler_params=pltpu.CompilerParams(vmem_limit_bytes=20 * 1024 * 1024),
             cost_estimate=pl.CostEstimate(
                 flops=3 * 2 * 2 * 512 * 256 * states, bytes_accessed=6 * 1024 * 1024, transcendentals=0
             ),
             name=name,
-        )(start, rows, blocks, occup, energies, nbr, dham, dovl, own_high, own_low, near_high, near_low)
-
-    core_force, core_sent = cross(0, core_rows, core_blocks, "core_pairs")
-    core_back = core_swap(core_sent[:3])
-    far_force, far_sent = cross(1, far_rows, far_blocks, "far_pairs")
-    far_back = shard_swap(far_sent[:3])
-    total = inner[:3] + core_force[:3] + core_back + far_force[:3] + far_back
+        )(start, payload, before, back, occup, energies, nbr, dham, dovl, own_high, own_low, near_high, near_low)
+
+    total, core_sent = cross(0, core_payload, inner, jnp.zeros((8, atoms), jnp.float32), "core_pairs")
+    total, far_sent = cross(1, far_payload, total, core_swap(core_sent), "far_pairs")
+    total = (total + shard_swap(far_sent))[:3]
+    if lax.axis_size("states") == 2:
+        return total + lax.ppermute(total, "states", [(0, 1), (1, 0)])
     return lax.psum(total, "states")
 
 

time: 45.7 us -> 39.1 us (0.86)
  starting transfers between devices: 12.8 us -> 8.1 us
  blocking collectives: 4.62 us -> 0 us
  waiting for transfers between devices: 1.28 us -> 5.21 us
  local copies, waits for them, and re-layouts: 3.66 us -> 3 us
  Pallas kernels: 22.5 us -> 21.9 us
    psum x1 -> x0, blocking collectives: 4.62 us -> none  [local(): return lax.psum(total, 'states')]
    pallas_call x0 -> x1, Pallas kernels: none -> 3.5 us  [local(): pl.pallas_call(pack_kernel, out_shape=(payload, payload), in_specs=[smem,...]
    dynamic_slice x1 -> x0, local copies, waits for them, and re-layouts: 3.24 us -> none  [local(): lax.dynamic_slice_in_dim(coeffs, (1 - sub) * (4 * (atoms - BLOCK)), 4 * B...]
    pallas_call x1, Pallas kernels: 16.7 us -> 13.5 us  [local(): pl.pallas_call(inner_kernel, out_shape=(whole, whole, half, half, force),...]
    unnamed x12, local copies, waits for them, and re-layouts: 0.03 us -> 2.99 us
    ppermute x2 -> x1, starting transfers between devices: 3.36 us -> 1.21 us  [local(): return total + lax.ppermute(total, 'states', [(0, 1), (1, 0)])]
    ppermute x2, waiting for transfers between devices: 1.27 us -> 2.77 us  [shard_swap(): return lax.ppermute(value, SHARD, pairs)]
    ppermute x2, starting transfers between devices: 8.2 us -> 6.76 us  [shard_swap(): return lax.ppermute(value, SHARD, pairs)]
  transfers between devices with their start and end apart: 6 -> 5, of which waited for: 1 -> 3; matrix products, arithmetic and copies ran while one was open for 2% -> 0% of each run, Pallas kernels for 45% -> 40%
where the time goes in v3:
time: 39.1 us; the launch traced here: 38.8 us
  Pallas kernels  21.9 us (56%)
  starting transfers between devices  8.1 us (21%)
  waiting for transfers between devices  5.21 us (13%)
  local copies, waits for them, and re-layouts  3 us (8%)
  other arithmetic  0.6 us (2%)
    pallas_call x1, Pallas kernels, local(): pl.pallas_call(inner_kernel, out_shape=(whole, whole, half, half, force),...  13.5 us
    ppermute x2, starting transfers between devices, shard_swap(): return lax.ppermute(value, SHARD, pairs)  6.76 us
    pallas_call x2, Pallas kernels, cross(): pl.pallas_call(functools.partial(cross_kernel, parity), out_shape=(force,...  4.87 us
    pallas_call x1, Pallas kernels, local(): pl.pallas_call(pack_kernel, out_shape=(payload, payload), in_specs=[smem,...  3.5 us
    unnamed x12, local copies, waits for them, and re-layouts  2.99 us
    ppermute x2, waiting for transfers between devices, shard_swap(): return lax.ppermute(value, SHARD, pairs)  2.77 us
    ppermute x1, waiting for transfers between devices, local(): return total + lax.ppermute(total, 'states', [(0, 1), (1, 0)])  1.24 us
    ppermute x1, starting transfers between devices, local(): return total + lax.ppermute(total, 'states', [(0, 1), (1, 0)])  1.21 us
  transfers between devices with their start and end apart: 5, of which 3 were waited for; matrix products, arithmetic and copies ran while one was open for 0% of the time, Pallas kernels for 40%

profile of v3, /device:TPU:1, one launch (start us, length us, event | category | flops | bytes accessed | tf_op | source)
XLA Modules:
  0.0 38.8 jit_solution(5300576436144068150)
XLA Ops:
  0.0 0.0 copy-start
  0.0 1.1 %copy-done = f32[48,16,256]{2,1,0:T(8,128)S(1)} copy-done((f32[48,16,256]{2,1,0:T(8,128)S(1)}, f32[48,16,256]{2,1,0:T(8,128)}, u32[]{:S(2)}) %copy-start) | copy-done | bytes 786456
  1.1 0.0 copy-start.1
  1.1 1.1 %copy-done.1 = f32[48,16,256]{2,1,0:T(8,128)S(1)} copy-done((f32[48,16,256]{2,1,0:T(8,128)S(1)}, f32[48,16,256]{2,1,0:T(8,128)}, u32[]{:S(2)}) %copy-start.1) | copy-done | bytes 786456
  2.3 0.0 copy-start.3
  2.3 0.7 %copy-done.3 = s32[16,256]{1,0:T(8,128)S(1)} copy-done((s32[16,256]{1,0:T(8,128)S(1)}, s32[16,256]{1,0:T(8,128)}, u32[]{:S(2)}) %copy-start.3) | copy-done | bytes 16408
  3.0 0.0 copy-start.2
  3.0 0.0 copy-start.4
  3.0 0.0 copy-start.5
  3.0 3.5 %pack.1 = (f32[8,320,128]{2,1,0:T(8,128)}, f32[8,320,128]{2,1,0:T(8,128)}) custom-call(s32[1]{0:T(128)} %bitcast.start_ref, f32[1024,1024]{1,0:T(8,128)} %coeffs_ref.3, s32[16,256]{1,0:T(8,128)S(1)} %copy-done.3, f32[48,16,256]{2,1,0:T(8,128)S(1)} %copy-done, f32[48,16,256]{2,1,0:T(8,128)S(1)} %copy-done.1), custom_call_target="tpu_custom_call" | custom-call | tf_op jit(solution)/shard_map/pack/pallas_call | solution.py:378
  6.5 0.1 collective-permute-start.1
  6.6 4.5 %collective-permute-start = (f32[8,320,128]{2,1,0:T(8,128)}, f32[8,320,128]{2,1,0:T(8,128)S(1)}, u32[]{:S(2)}, u32[]{:S(2)}) collective-permute-start(f32[8,320,128]{2,1,0:T(8,128)} %get-tuple-element.16), channel_id=1, source_target_pairs={{1,4},{4,1},{5,8},{8,5},{9,12},{12,9},{3,6},{6,3},{7,10},{10,7},{1... | collective-permute-start | bytes 3932168 | tf_op jit(solution)/shard_map/ppermute | solution.py:358
  11.2 0.0 copy-done.2
  11.2 0.0 copy-done.4
  11.2 0.0 copy-done.5
  11.2 13.5 %inner_pairs.1 = (bf16[1024,1024]{1,0:T(8,128)(2,1)S(1)}, bf16[1024,1024]{1,0:T(8,128)(2,1)S(1)}, bf16[512,1024]{1,0:T(8,128)(2,1)S(1)}, bf16[512,1024]{1,0:T(8,128)(2,1)S(1)}, f32[8,256]{1,0:T(8,128)S(1)}) custom-call(s32[1]{0:T(128)} %bitcast.start_ref, f32[1024,1024]{1,0:T(8,128)S(1)} %copy-done.2, f32[1,1024]{1,0:T(1,128)S(1)} %bitcast.3, ...), custom_call_target="tpu_custom_call" | custom-call | flops 7247757312 | bytes 16777216 | tf_op jit(solution)/shard_map/inner_pairs/pallas_call | solution.py:395
  24.7 0.0 collective-permute-done.1.payload_ref
  24.7 2.0 %core_pairs.1 = (f32[8,256]{1,0:T(8,128)S(1)}, f32[8,256]{1,0:T(8,128)S(1)}) custom-call(s32[1]{0:T(128)} %bitcast.start_ref, f32[8,320,128]{2,1,0:T(8,128)S(1)} %collective-permute-done.1.payload_ref, f32[8,256]{1,0:T(8,128)S(1)} %get-tuple-element.18.before_ref, f32[8,256]{1,0:T(8,128)S(1)} %broadcast_in_dim.3.back_ref, f32[1,1024]{1,0:T(1,128)S(1)} %bitcast.4, ...), custom_call_target="tpu_custom_call" | custom-call | flops 1610612736 | bytes 6291456 | tf_op jit(solution)/shard_map/core_pairs/pallas_call | solution.py:417
  26.7 0.0 collective-permute-start.2
  26.7 0.0 collective-permute-done.payload_ref
  26.7 1.2 %collective-permute-done.2.back_ref = f32[8,256]{1,0:T(8,128)S(1)} collective-permute-done((f32[8,256]{1,0:T(8,128)S(1)}, f32[8,256]{1,0:T(8,128)S(1)}, u32[]{:S(2)}, u32[]{:S(2)}) %collective-permute-start.2) | collective-permute-done | bytes 8224 | tf_op jit(solution)/shard_map/ppermute | solution.py:352
  27.9 2.9 %far_pairs.1 = (f32[8,256]{1,0:T(8,128)S(1)}, f32[8,256]{1,0:T(8,128)S(1)}) custom-call(s32[1]{0:T(128)} %bitcast.start_ref, f32[8,320,128]{2,1,0:T(8,128)S(1)} %collective-permute-done.payload_ref, f32[8,256]{1,0:T(8,128)S(1)} %get-tuple-element.23.before_ref, f32[8,256]{1,0:T(8,128)S(1)} %collective-permute-done.2.back_ref, f32[1,1024]{1,0:T(1,128)S(1)} %bitcast.5, ...), custom_call_target="tpu_custom_call" | custom-call | flops 1610612736 | bytes 6291456 | tf_op jit(solution)/shard_map/far_pairs/pallas_call | solution.py:417
  30.8 2.2 %collective-permute-start.3 = (f32[8,256]{1,0:T(8,128)S(1)}, f32[8,256]{1,0:T(8,128)S(1)}, u32[]{:S(2)}, u32[]{:S(2)}) collective-permute-start(f32[8,256]{1,0:T(8,128)S(1)} %get-tuple-element.26), channel_id=1, source_target_pairs={{1,4},{4,1},{5,8},{8,5},{9,12},{12,9},{3,6},{6,3},{7,10},{10,7},{1... | collective-permute-start | bytes 24584 | tf_op jit(solution)/shard_map/ppermute | solution.py:358
  33.0 2.8 %collective-permute-done.3 = f32[8,256]{1,0:T(8,128)S(1)} collective-permute-done((f32[8,256]{1,0:T(8,128)S(1)}, f32[8,256]{1,0:T(8,128)S(1)}, u32[]{:S(2)}, u32[]{:S(2)}) %collective-permute-start.3) | collective-permute-done | bytes 8224 | tf_op jit(solution)/shard_map/ppermute | solution.py:358
  35.8 1.2 %collective-permute-start.4 = (f32[3,256]{1,0:T(4,128)S(1)}, f32[3,256]{1,0:T(4,128)S(1)}, u32[]{:S(2)}, u32[]{:S(2)}) collective-permute-start(f32[3,256]{1,0:T(4,128)S(1)} %slice_add_fusion), channel_id=1, source_target_pairs={{0,2},{2,0},{1,3},{3,1},{4,6},{6,4},{5,7},{7,5},{8,10},{10,8},{9,1... | collective-permute-start | bytes 9224 | tf_op jit(solution)/shard_map/ppermute | solution.py:440
  37.0 1.2 %collective-permute-done.4 = f32[3,256]{1,0:T(4,128)S(1)} collective-permute-done((f32[3,256]{1,0:T(4,128)S(1)}, f32[3,256]{1,0:T(4,128)S(1)}, u32[]{:S(2)}, u32[]{:S(2)}) %collective-permute-start.4) | collective-permute-done | bytes 3104 | tf_op jit(solution)/shard_map/ppermute | solution.py:440
  38.2 0.6 %add.11 = f32[3,256]{1,0:T(4,128)} add(f32[3,256]{1,0:T(4,128)S(1)} %slice_add_fusion, f32[3,256]{1,0:T(4,128)S(1)} %collective-permute-done.4) | non-fusion elementwise | flops 768 | bytes 9216 | tf_op jit(solution)/shard_map/add | solution.py:440
  (2 shorter events, 0.0 us)
Async XLA Ops:
  0.0 1.1 %copy-start = (f32[48,16,256]{2,1,0:T(8,128)S(1)}, f32[48,16,256]{2,1,0:T(8,128)}, u32[]{:S(2)}) copy-start(f32[48,16,256]{2,1,0:T(8,128)} %dham_ref.7) | copy-start | bytes 2359300
  1.1 1.1 %copy-start.1 = (f32[48,16,256]{2,1,0:T(8,128)S(1)}, f32[48,16,256]{2,1,0:T(8,128)}, u32[]{:S(2)}) copy-start(f32[48,16,256]{2,1,0:T(8,128)} %dovl_ref.7) | copy-start | bytes 2359300
  2.3 0.7 %copy-start.3 = (s32[16,256]{1,0:T(8,128)S(1)}, s32[16,256]{1,0:T(8,128)}, u32[]{:S(2)}) copy-start(s32[16,256]{1,0:T(8,128)} %nbr_ref.7) | copy-start | bytes 49156
  3.0 8.2 %copy-start.2 = (f32[1024,1024]{1,0:T(8,128)S(1)}, f32[1024,1024]{1,0:T(8,128)}, u32[]{:S(2)}) copy-start(f32[1024,1024]{1,0:T(8,128)} %coeffs_ref.3) | copy-start | bytes 12582916
  3.0 8.2 %copy-start.4 = (f32[1024]{0:T(1024)S(1)}, f32[1024]{0:T(1024)}, u32[]{:S(2)}) copy-start(f32[1024]{0:T(1024)} %param.7) | copy-start | bytes 12292
  3.0 8.2 %copy-start.5 = (f32[1024]{0:T(1024)S(1)}, f32[1024]{0:T(1024)}, u32[]{:S(2)}) copy-start(f32[1024]{0:T(1024)} %param.8) | copy-start | bytes 12292
  6.5 18.2 %collective-permute-start.1 = (f32[8,320,128]{2,1,0:T(8,128)}, f32[8,320,128]{2,1,0:T(8,128)S(1)}, u32[]{:S(2)}, u32[]{:S(2)}) collective-permute-start(f32[8,320,128]{2,1,0:T(8,128)} %get-tuple-element.17), channel_id=1, source_target_pairs={{0,1},{1,0},{2,3},{3,2},{4,5},{5,4},{6,7},{7,6},{8,9},{9,8},{10,11... | collective-permute-start | bytes 3932168 | tf_op jit(solution)/shard_map/ppermute | solution.py:352
  6.6 20.1 %collective-permute-start = (f32[8,320,128]{2,1,0:T(8,128)}, f32[8,320,128]{2,1,0:T(8,128)S(1)}, u32[]{:S(2)}, u32[]{:S(2)}) collective-permute-start(f32[8,320,128]{2,1,0:T(8,128)} %get-tuple-element.16), channel_id=1, source_target_pairs={{1,4},{4,1},{5,8},{8,5},{9,12},{12,9},{3,6},{6,3},{7,10},{10,7},{1... | collective-permute-start | bytes 3932168 | tf_op jit(solution)/shard_map/ppermute | solution.py:358
  26.7 1.2 %collective-permute-start.2 = (f32[8,256]{1,0:T(8,128)S(1)}, f32[8,256]{1,0:T(8,128)S(1)}, u32[]{:S(2)}, u32[]{:S(2)}) collective-permute-start(f32[8,256]{1,0:T(8,128)S(1)} %get-tuple-element.24), channel_id=1, source_target_pairs={{0,1},{1,0},{2,3},{3,2},{4,5},{5,4},{6,7},{7,6},{8,9},{9,8},{10,11... | collective-permute-start | bytes 24584 | tf_op jit(solution)/shard_map/ppermute | solution.py:352
  30.8 5.0 %collective-permute-start.3 = (f32[8,256]{1,0:T(8,128)S(1)}, f32[8,256]{1,0:T(8,128)S(1)}, u32[]{:S(2)}, u32[]{:S(2)}) collective-permute-start(f32[8,256]{1,0:T(8,128)S(1)} %get-tuple-element.26), channel_id=1, source_target_pairs={{1,4},{4,1},{5,8},{8,5},{9,12},{12,9},{3,6},{6,3},{7,10},{10,7},{1... | collective-permute-start | bytes 24584 | tf_op jit(solution)/shard_map/ppermute | solution.py:358
  35.8 2.5 %collective-permute-start.4 = (f32[3,256]{1,0:T(4,128)S(1)}, f32[3,256]{1,0:T(4,128)S(1)}, u32[]{:S(2)}, u32[]{:S(2)}) collective-permute-start(f32[3,256]{1,0:T(4,128)S(1)} %slice_add_fusion), channel_id=1, source_target_pairs={{0,2},{2,0},{1,3},{3,1},{4,6},{6,4},{5,7},{7,5},{8,10},{10,8},{9,1... | collective-permute-start | bytes 9224 | tf_op jit(solution)/shard_map/ppermute | solution.py:440

commit v4 on v3

--- a/solution.py
+++ b/solution.py
@@ -212,7 +212,7 @@
 
 def pack_kernel(
     start_ref, coeffs_ref, nbr_ref, dham_ref, dovl_ref, core_ref, far_ref,
-    ham_ref, ovl_ref, core_sem, far_sem, deriv_sem,
+    ham_ref, ovl_ref, last_ref, core_sem, far_sem, deriv_sem,
 ):
     atoms = nbr_ref.shape[1]
     count, rows, unused = core_ref.shape
@@ -222,6 +222,9 @@
         pltpu.make_async_copy(source.at[:, :, atoms - LANES :], target, deriv_sem.at[at])
         for at, (source, target) in enumerate([(dham_ref, ham_ref), (dovl_ref, ovl_ref)])
     ]
+    fetched.append(
+        pltpu.make_async_copy(nbr_ref.at[:, atoms - LANES :], last_ref, deriv_sem.at[2])
+    )
 
     def fill(up_ref, up_sem, down_ref, down_sem):
         copies = []
@@ -237,14 +240,14 @@
             down_ref[:, lower:, :] = jnp.zeros((count, rows - lower, LANES), jnp.float32)
         up_ref[:, 4 * UPPER :, :] = jnp.zeros((count, rows - 4 * UPPER, LANES), jnp.float32)
         planes = -(-48 // count)
-        last = nbr_ref[:, atoms - LANES :]
+        for copy in fetched:
+            copy.wait()
+        last = last_ref[...]
         target = jnp.where(last >= 0, last - (start_ref[0] + atoms), -1).astype(jnp.float32)
         at = 4 * UPPER + 16 * planes
         for half in range(2):
             part = target[8 * half : 8 * half + 8]
             up_ref[0, at + 8 * half : at + 8 * half + 8, :] = side_by_side(part, part, 1)
-        for copy in fetched:
-            copy.wait()
         for x, ref in enumerate((ham_ref, ovl_ref)):
             for k in range(3):
                 for g in range(2):
@@ -348,6 +351,10 @@
             sent_ref[k : k + 1, atoms - BLOCK :] = -2.0 * mine[k][:, BLOCK:]
 
 
+def in_hbm(value):
+    return pltpu.with_memory_space_constraint(value, pltpu.HBM)
+
+
 def core_swap(value):
     return lax.ppermute(value, "sub", [(0, 1), (1, 0)])
 
@@ -378,18 +385,19 @@
     core_payload, far_payload = pl.pallas_call(
         pack_kernel,
         out_shape=(payload, payload),
-        in_specs=[smem, hbm, vmem, hbm, hbm],
+        in_specs=[smem] + [hbm] * 4,
         out_specs=(vmem, vmem),
         scratch_shapes=[
             pltpu.VMEM((48, slots, LANES), jnp.float32),
             pltpu.VMEM((48, slots, LANES), jnp.float32),
+            pltpu.VMEM((slots, LANES), jnp.int32),
             pltpu.SemaphoreType.DMA((count,)),
             pltpu.SemaphoreType.DMA((count,)),
-            pltpu.SemaphoreType.DMA((2,)),
+            pltpu.SemaphoreType.DMA((3,)),
         ],
-        compiler_params=pltpu.CompilerParams(vmem_limit_bytes=52 * 1024 * 1024),
+        compiler_params=pltpu.CompilerParams(vmem_limit_bytes=12 * 1024 * 1024),
         name="pack",
-    )(start, coeffs, nbr, dham, dovl)
+    )(start, *(in_hbm(value) for value in (coeffs, nbr, dham, dovl)))
     far_payload = shard_swap(far_payload)
     core_payload = core_swap(core_payload)
     own_high, own_low, near_high, near_low, inner = pl.pallas_call(
@@ -410,7 +418,7 @@
             flops=3 * 2 * 9 * 512 * 256 * states, bytes_accessed=16 * 1024 * 1024, transcendentals=0
         ),
         name="inner_pairs",
-    )(start, coeffs, occup, energies, nbr, dham, dovl)
+    )(start, in_hbm(coeffs), occup, energies, nbr, dham, dovl)
 
     def cross(parity, payload, before, back, name):
         cut = pltpu.VMEM((8 * lower, states), jnp.bfloat16)

time: 39.1 us -> 35.1 us (0.90)
  local copies, waits for them, and re-layouts: 3 us -> 0.02 us
  Pallas kernels: 21.9 us -> 20.9 us
    unnamed x12 -> x10, local copies, waits for them, and re-layouts: 2.99 us -> 0.02 us
    pallas_call x1, Pallas kernels: 3.5 us -> 2.23 us  [local(): pl.pallas_call(pack_kernel, out_shape=(payload, payload), in_specs=[smem]...]
  transfers between devices with their start and end apart: 5 -> 5, of which waited for: 3 -> 3; matrix products, arithmetic and copies ran while one was open for 0% -> 0% of each run, Pallas kernels for 40% -> 45%
where the time goes in v4:
time: 35.1 us; the launch traced here: 34.9 us
  Pallas kernels  20.9 us (60%)
  starting transfers between devices  8.1 us (23%)
  waiting for transfers between devices  5.22 us (15%)
  other arithmetic  0.6 us (2%)
    pallas_call x1, Pallas kernels, local(): pl.pallas_call(inner_kernel, out_shape=(whole, whole, half, half, force),...  13.8 us
    ppermute x2, starting transfers between devices, shard_swap(): return lax.ppermute(value, SHARD, pairs)  6.77 us
    pallas_call x2, Pallas kernels, cross(): pl.pallas_call(functools.partial(cross_kernel, parity), out_shape=(force,...  4.87 us
    ppermute x2, waiting for transfers between devices, shard_swap(): return lax.ppermute(value, SHARD, pairs)  2.77 us
    pallas_call x1, Pallas kernels, local(): pl.pallas_call(pack_kernel, out_shape=(payload, payload), in_specs=[smem]...  2.23 us
    ppermute x1, waiting for transfers between devices, local(): return total + lax.ppermute(total, 'states', [(0, 1), (1, 0)])  1.25 us
    ppermute x1, starting transfers between devices, local(): return total + lax.ppermute(total, 'states', [(0, 1), (1, 0)])  1.21 us
    ppermute x2, waiting for transfers between devices, core_swap(): return lax.ppermute(value, 'sub', [(0, 1), (1, 0)])  1.2 us
  transfers between devices with their start and end apart: 5, of which 3 were waited for; matrix products, arithmetic and copies ran while one was open for 0% of the time, Pallas kernels for 45%

profile of v4, /device:TPU:1, one launch (start us, length us, event | category | flops | bytes accessed | tf_op | source)
XLA Modules:
  0.0 34.9 jit_solution(8631219709832510327)
XLA Ops:
  0.0 0.0 copy-start
  0.0 0.0 copy-start.1
  0.0 0.0 copy-start.2
  0.0 0.0 copy-start.3
  0.0 0.0 copy-start.4
  0.0 2.2 %pack.1 = (f32[8,320,128]{2,1,0:T(8,128)S(1)}, f32[8,320,128]{2,1,0:T(8,128)S(1)}) custom-call(s32[1]{0:T(128)} %bitcast.start_ref, f32[1024,1024]{1,0:T(8,128)} %coeffs_ref.3, s32[16,256]{1,0:T(8,128)} %nbr_ref.7, f32[48,16,256]{2,1,0:T(8,128)} %dham_ref.7, f32[48,16,256]{2,1,0:T(8,128)} %dovl_ref.7), custom_call_target="tpu_custom_call" | custom-call | tf_op jit(solution)/shard_map/pack/pallas_call | solution.py:385
  2.3 0.1 collective-permute-start.1
  2.4 4.6 %collective-permute-start = (f32[8,320,128]{2,1,0:T(8,128)S(1)}, f32[8,320,128]{2,1,0:T(8,128)S(1)}, u32[]{:S(2)}, u32[]{:S(2)}) collective-permute-start(f32[8,320,128]{2,1,0:T(8,128)S(1)} %get-tuple-element.16), channel_id=1, source_target_pairs={{1,4},{4,1},{5,8},{8,5},{9,12},{12,9},{3,6},{6,3},{7,10},{10,7},{1... | collective-permute-start | bytes 3932168 | tf_op jit(solution)/shard_map/ppermute | solution.py:365
  6.9 0.0 copy-done
  7.0 0.0 copy-done.1
  7.0 0.0 copy-done.2
  7.0 0.0 copy-done.3
  7.0 0.0 copy-done.4
  7.0 13.8 %inner_pairs.1 = (bf16[1024,1024]{1,0:T(8,128)(2,1)S(1)}, bf16[1024,1024]{1,0:T(8,128)(2,1)S(1)}, bf16[512,1024]{1,0:T(8,128)(2,1)S(1)}, bf16[512,1024]{1,0:T(8,128)(2,1)S(1)}, f32[8,256]{1,0:T(8,128)S(1)}) custom-call(s32[1]{0:T(128)} %bitcast.start_ref, f32[1024,1024]{1,0:T(8,128)} %coeffs_ref.3, f32[1,1024]{1,0:T(1,128)S(1)} %bitcast.3, ...), custom_call_target="tpu_custom_call" | custom-call | flops 7247757312 | bytes 16777216 | tf_op jit(solution)/shard_map/inner_pairs/pallas_call | solution.py:403
  20.8 0.0 collective-permute-done.1.payload_ref
  20.8 2.0 %core_pairs.1 = (f32[8,256]{1,0:T(8,128)S(1)}, f32[8,256]{1,0:T(8,128)S(1)}) custom-call(s32[1]{0:T(128)} %bitcast.start_ref, f32[8,320,128]{2,1,0:T(8,128)S(1)} %collective-permute-done.1.payload_ref, f32[8,256]{1,0:T(8,128)S(1)} %get-tuple-element.18.before_ref, f32[8,256]{1,0:T(8,128)S(1)} %broadcast_in_dim.3.back_ref, f32[1,1024]{1,0:T(1,128)S(1)} %bitcast.4, ...), custom_call_target="tpu_custom_call" | custom-call | flops 1610612736 | bytes 6291456 | tf_op jit(solution)/shard_map/core_pairs/pallas_call | solution.py:425
  22.8 0.0 collective-permute-start.2
  22.8 0.0 collective-permute-done.payload_ref
  22.8 1.2 %collective-permute-done.2.back_ref = f32[8,256]{1,0:T(8,128)S(1)} collective-permute-done((f32[8,256]{1,0:T(8,128)S(1)}, f32[8,256]{1,0:T(8,128)S(1)}, u32[]{:S(2)}, u32[]{:S(2)}) %collective-permute-start.2) | collective-permute-done | bytes 8224 | tf_op jit(solution)/shard_map/ppermute | solution.py:359
  24.0 2.9 %far_pairs.1 = (f32[8,256]{1,0:T(8,128)S(1)}, f32[8,256]{1,0:T(8,128)S(1)}) custom-call(s32[1]{0:T(128)} %bitcast.start_ref, f32[8,320,128]{2,1,0:T(8,128)S(1)} %collective-permute-done.payload_ref, f32[8,256]{1,0:T(8,128)S(1)} %get-tuple-element.23.before_ref, f32[8,256]{1,0:T(8,128)S(1)} %collective-permute-done.2.back_ref, f32[1,1024]{1,0:T(1,128)S(1)} %bitcast.5, ...), custom_call_target="tpu_custom_call" | custom-call | flops 1610612736 | bytes 6291456 | tf_op jit(solution)/shard_map/far_pairs/pallas_call | solution.py:425
  26.9 2.2 %collective-permute-start.3 = (f32[8,256]{1,0:T(8,128)S(1)}, f32[8,256]{1,0:T(8,128)S(1)}, u32[]{:S(2)}, u32[]{:S(2)}) collective-permute-start(f32[8,256]{1,0:T(8,128)S(1)} %get-tuple-element.26), channel_id=1, source_target_pairs={{1,4},{4,1},{5,8},{8,5},{9,12},{12,9},{3,6},{6,3},{7,10},{10,7},{1... | collective-permute-start | bytes 24584 | tf_op jit(solution)/shard_map/ppermute | solution.py:365
  29.1 2.8 %collective-permute-done.3 = f32[8,256]{1,0:T(8,128)S(1)} collective-permute-done((f32[8,256]{1,0:T(8,128)S(1)}, f32[8,256]{1,0:T(8,128)S(1)}, u32[]{:S(2)}, u32[]{:S(2)}) %collective-permute-start.3) | collective-permute-done | bytes 8224 | tf_op jit(solution)/shard_map/ppermute | solution.py:365
  31.9 1.2 %collective-permute-start.4 = (f32[3,256]{1,0:T(4,128)S(1)}, f32[3,256]{1,0:T(4,128)S(1)}, u32[]{:S(2)}, u32[]{:S(2)}) collective-permute-start(f32[3,256]{1,0:T(4,128)S(1)} %slice_add_fusion), channel_id=1, source_target_pairs={{0,2},{2,0},{1,3},{3,1},{4,6},{6,4},{5,7},{7,5},{8,10},{10,8},{9,1... | collective-permute-start | bytes 9224 | tf_op jit(solution)/shard_map/ppermute | solution.py:448
  33.1 1.2 %collective-permute-done.4 = f32[3,256]{1,0:T(4,128)S(1)} collective-permute-done((f32[3,256]{1,0:T(4,128)S(1)}, f32[3,256]{1,0:T(4,128)S(1)}, u32[]{:S(2)}, u32[]{:S(2)}) %collective-permute-start.4) | collective-permute-done | bytes 3104 | tf_op jit(solution)/shard_map/ppermute | solution.py:448
  34.3 0.6 %add.11 = f32[3,256]{1,0:T(4,128)} add(f32[3,256]{1,0:T(4,128)S(1)} %slice_add_fusion, f32[3,256]{1,0:T(4,128)S(1)} %collective-permute-done.4) | non-fusion elementwise | flops 768 | bytes 9216 | tf_op jit(solution)/shard_map/add | solution.py:448
  (2 shorter events, 0.0 us)
Async XLA Ops:
  0.0 6.9 %copy-start = (f32[48,16,256]{2,1,0:T(8,128)S(1)}, f32[48,16,256]{2,1,0:T(8,128)}, u32[]{:S(2)}) copy-start(f32[48,16,256]{2,1,0:T(8,128)} %dham_ref.7) | copy-start | bytes 2359300
  0.0 7.0 %copy-start.1 = (f32[48,16,256]{2,1,0:T(8,128)S(1)}, f32[48,16,256]{2,1,0:T(8,128)}, u32[]{:S(2)}) copy-start(f32[48,16,256]{2,1,0:T(8,128)} %dovl_ref.7) | copy-start | bytes 2359300
  0.0 7.0 %copy-start.2 = (s32[16,256]{1,0:T(8,128)S(1)}, s32[16,256]{1,0:T(8,128)}, u32[]{:S(2)}) copy-start(s32[16,256]{1,0:T(8,128)} %nbr_ref.7) | copy-start | bytes 49156
  0.0 7.0 %copy-start.3 = (f32[1024]{0:T(1024)S(1)}, f32[1024]{0:T(1024)}, u32[]{:S(2)}) copy-start(f32[1024]{0:T(1024)} %param.7) | copy-start | bytes 12292
  0.0 7.0 %copy-start.4 = (f32[1024]{0:T(1024)S(1)}, f32[1024]{0:T(1024)}, u32[]{:S(2)}) copy-start(f32[1024]{0:T(1024)} %param.8) | copy-start | bytes 12292
  2.3 18.5 %collective-permute-start.1 = (f32[8,320,128]{2,1,0:T(8,128)S(1)}, f32[8,320,128]{2,1,0:T(8,128)S(1)}, u32[]{:S(2)}, u32[]{:S(2)}) collective-permute-start(f32[8,320,128]{2,1,0:T(8,128)S(1)} %get-tuple-element.17), channel_id=1, source_target_pairs={{0,1},{1,0},{2,3},{3,2},{4,5},{5,4},{6,7},{7,6},{8,9},{9,8},{10,11... | collective-permute-start | bytes 3932168 | tf_op jit(solution)/shard_map/ppermute | solution.py:359
  2.4 20.5 %collective-permute-start = (f32[8,320,128]{2,1,0:T(8,128)S(1)}, f32[8,320,128]{2,1,0:T(8,128)S(1)}, u32[]{:S(2)}, u32[]{:S(2)}) collective-permute-start(f32[8,320,128]{2,1,0:T(8,128)S(1)} %get-tuple-element.16), channel_id=1, source_target_pairs={{1,4},{4,1},{5,8},{8,5},{9,12},{12,9},{3,6},{6,3},{7,10},{10,7},{1... | collective-permute-start | bytes 3932168 | tf_op jit(solution)/shard_map/ppermute | solution.py:365
  22.8 1.2 %collective-permute-start.2 = (f32[8,256]{1,0:T(8,128)S(1)}, f32[8,256]{1,0:T(8,128)S(1)}, u32[]{:S(2)}, u32[]{:S(2)}) collective-permute-start(f32[8,256]{1,0:T(8,128)S(1)} %get-tuple-element.24), channel_id=1, source_target_pairs={{0,1},{1,0},{2,3},{3,2},{4,5},{5,4},{6,7},{7,6},{8,9},{9,8},{10,11... | collective-permute-start | bytes 24584 | tf_op jit(solution)/shard_map/ppermute | solution.py:359
  26.9 5.0 %collective-permute-start.3 = (f32[8,256]{1,0:T(8,128)S(1)}, f32[8,256]{1,0:T(8,128)S(1)}, u32[]{:S(2)}, u32[]{:S(2)}) collective-permute-start(f32[8,256]{1,0:T(8,128)S(1)} %get-tuple-element.26), channel_id=1, source_target_pairs={{1,4},{4,1},{5,8},{8,5},{9,12},{12,9},{3,6},{6,3},{7,10},{10,7},{1... | collective-permute-start | bytes 24584 | tf_op jit(solution)/shard_map/ppermute | solution.py:365
  31.9 2.5 %collective-permute-start.4 = (f32[3,256]{1,0:T(4,128)S(1)}, f32[3,256]{1,0:T(4,128)S(1)}, u32[]{:S(2)}, u32[]{:S(2)}) collective-permute-start(f32[3,256]{1,0:T(4,128)S(1)} %slice_add_fusion), channel_id=1, source_target_pairs={{0,2},{2,0},{1,3},{3,1},{4,6},{6,4},{5,7},{7,5},{8,10},{10,8},{9,1... | collective-permute-start | bytes 9224 | tf_op jit(solution)/shard_map/ppermute | solution.py:448

commit v5 on v4

--- a/solution.py
+++ b/solution.py
@@ -64,7 +64,10 @@
         for (b, g, half), value in picked.items():
             for k in range(3):
                 term = value * deriv(k, x, b, g, half)
-                pair[k][half] = term if pair[k][half] is None else pair[k][half] + term
+                if pair[k][half] is None:
+                    pair[k][half] = term
+                else:
+                    pair[k][half] = pair[k][half] - term if x else pair[k][half] + term
     return pair
 
 
@@ -115,8 +118,7 @@
             ref[k * 16 + (2 * g + parity) * 4 + b, 8 * half : 8 * half + 8, tile * LANES : (tile + 1) * LANES]
             for parity in range(2)
         ]
-        both = side_by_side(parts[0], parts[1], odd)
-        return -both if x else both
+        return side_by_side(parts[0], parts[1], odd)
 
     return deriv
 
@@ -132,7 +134,7 @@
     start_ref, coeffs_ref, occup_ref, energies_ref, nbr_ref, dham_ref, dovl_ref,
     own_high_ref, own_low_ref, near1_high_ref, near1_low_ref, force_ref,
     near0_high_ref, near0_low_ref, near2_high_ref, near2_low_ref, near3_high_ref, near3_low_ref,
-    gram0_ref, gram1_ref, gram2_ref, gram3_ref, index_ref, spread_ref, columns_ref, copy_sem,
+    gram0_ref, gram1_ref, gram2_ref, gram3_ref, index_ref, spread_ref, columns_ref, ham_ref, ovl_ref, copy_sem, deriv_sem,
 ):
     states = coeffs_ref.shape[1]
     count = states // LANES
@@ -143,22 +145,25 @@
         (near3_high_ref, near3_low_ref),
     ]
     grams = [gram0_ref, gram1_ref, gram2_ref, gram3_ref]
-    copies = {}
-    for j in (3, 2, 1, 0):
-        for c in range(count):
-            copies[j, c] = pltpu.make_async_copy(
-                coeffs_ref.at[j * 256 : j * 256 + 256, c * LANES : (c + 1) * LANES],
-                columns_ref.at[c, j * 256 : j * 256 + 256, :],
-                copy_sem.at[j * count + c],
-            )
-            copies[j, c].start()
+    copies = [
+        pltpu.make_async_copy(
+            coeffs_ref.at[:, c * LANES : (c + 1) * LANES], columns_ref.at[c], copy_sem.at[c]
+        )
+        for c in range(count)
+    ]
+    derivs = [
+        pltpu.make_async_copy(source, target, deriv_sem.at[at])
+        for at, (source, target) in enumerate([(dham_ref, ham_ref), (dovl_ref, ovl_ref)])
+    ]
+    for copy in copies + derivs:
+        copy.start()
     occup = occup_ref[...]
     weights = [occup, occup * energies_ref[...]]
 
-    def prepare(j):
-        for c in range(count):
-            copies[j, c].wait()
-            lanes = slice(c * LANES, (c + 1) * LANES)
+    for c, copy in enumerate(copies):
+        copy.wait()
+        lanes = slice(c * LANES, (c + 1) * LANES)
+        for j in range(4):
             for a in range(4):
                 rows = columns_ref[c, pl.ds(j * 256 + a, BLOCK, stride=4), :]
                 own = slice(j * 256 + a * BLOCK, j * 256 + (a + 1) * BLOCK)
@@ -180,7 +185,7 @@
     def pick(h):
         index = [part - BLOCK * (h % 2) for part in block_index(index_ref.at[h // 2], h % 2)]
         blocks = min(h + 3, 4) - h
-        return fold(pick_pairs(grams[h], 0, BLOCK, index, own_deriv(dham_ref, dovl_ref, h // 2, h % 2), blocks))
+        return fold(pick_pairs(grams[h], 0, BLOCK, index, own_deriv(ham_ref, ovl_ref, h // 2, h % 2), blocks))
 
     def finish(tile, even, odd):
         pair = merge(even, odd)
@@ -189,10 +194,10 @@
         theirs = spread(index_ref.at[tile], pair, spread_ref, rows)
         return mine, theirs
 
-    for j in (3, 2, 1, 0):
-        prepare(j)
     for h in (3, 2, 1, 0):
         multiply(h)
+    for copy in derivs:
+        copy.wait()
     pair3 = pick(3)
     pair2 = pick(2)
     mine1, theirs1 = finish(1, pair2, pair3)
@@ -258,9 +263,8 @@
                                 ref[k * 16 + (2 * g + parity) * 4 + b, 8 * half : 8 * half + 8, :]
                                 for parity in range(2)
                             ]
-                            both = side_by_side(parts[0], parts[1], 1)
                             at = 4 * UPPER + 16 * (plane // count) + 8 * half
-                            up_ref[plane % count, at : at + 8, :] = -both if x else both
+                            up_ref[plane % count, at : at + 8, :] = side_by_side(parts[0], parts[1], 1)
         for copy in copies:
             copy.wait()
 
@@ -275,20 +279,26 @@
 
 def cross_kernel(
     parity,
-    start_ref, payload_ref, before_ref, back_ref, occup_ref, energies_ref, nbr_ref, dham_ref, dovl_ref,
+    start_ref, payload_ref, before_ref, occup_ref, energies_ref, nbr_ref, dham_ref, dovl_ref,
     own_high_ref, own_low_ref, near_high_ref, near_low_ref,
     force_ref, sent_ref,
-    cut_high_ref, cut_low_ref, gram_ref, index_ref, spread_ref,
+    cut_high_ref, cut_low_ref, gram_ref, index_ref, spread_ref, ham_ref, ovl_ref, deriv_sem,
 ):
     atoms = nbr_ref.shape[1]
     count = payload_ref.shape[0]
     lower = atoms // 2 - UPPER
-    force_ref[...] = before_ref[...] + back_ref[...]
+    force_ref[...] = before_ref[...]
     sent_ref[...] = jnp.zeros_like(sent_ref)
     first = ((start_ref[0] // atoms) & 1) == parity
 
     @pl.when(first)
     def above():
+        derivs = [
+            pltpu.make_async_copy(source.at[:, :, LANES:], target, deriv_sem.at[at])
+            for at, (source, target) in enumerate([(dham_ref, ham_ref), (dovl_ref, ovl_ref)])
+        ]
+        for copy in derivs:
+            copy.start()
         occup = occup_ref[...]
         weights = [occup, occup * energies_ref[...]]
         for c in range(count):
@@ -301,11 +311,13 @@
         gram_ref[...] = gram(
             cut_high_ref[...], cut_low_ref[...], own_high_ref[512:, :], own_low_ref[512:, :]
         )
+        for copy in derivs:
+            copy.wait()
         index_ref[...] = nbr_ref[:, LANES:] - (start_ref[0] + atoms)
         even, odd = (
             fold(
                 pick_pairs(
-                    gram_ref, h * 256, lower, block_index(index_ref, h), own_deriv(dham_ref, dovl_ref, 1, h)
+                    gram_ref, h * 256, lower, block_index(index_ref, h), own_deriv(ham_ref, ovl_ref, 0, h)
                 )
             )
             for h in range(2)
@@ -403,7 +415,7 @@
     own_high, own_low, near_high, near_low, inner = pl.pallas_call(
         inner_kernel,
         out_shape=(whole, whole, half, half, force),
-        in_specs=[smem, hbm] + [vmem] * 5,
+        in_specs=[smem, hbm, vmem, vmem, vmem, hbm, hbm],
         out_specs=(vmem,) * 5,
         scratch_shapes=[prepared] * 6
         + [pltpu.VMEM((512 * n, 256), jnp.float32) for n in (3, 3, 2, 1)]
@@ -411,21 +423,24 @@
             pltpu.VMEM((2, slots, LANES), jnp.int32),
             pltpu.VMEM((3, atoms, LANES), jnp.float32),
             pltpu.VMEM((states // LANES, 4 * atoms, LANES), jnp.float32),
-            pltpu.SemaphoreType.DMA((4 * states // LANES,)),
+            pltpu.VMEM((48, slots, atoms), jnp.float32),
+            pltpu.VMEM((48, slots, atoms), jnp.float32),
+            pltpu.SemaphoreType.DMA((count,)),
+            pltpu.SemaphoreType.DMA((2,)),
         ],
         compiler_params=pltpu.CompilerParams(vmem_limit_bytes=32 * 1024 * 1024),
         cost_estimate=pl.CostEstimate(
             flops=3 * 2 * 9 * 512 * 256 * states, bytes_accessed=16 * 1024 * 1024, transcendentals=0
         ),
         name="inner_pairs",
-    )(start, in_hbm(coeffs), occup, energies, nbr, dham, dovl)
-
-    def cross(parity, payload, before, back, name):
+    )(start, in_hbm(coeffs), occup, energies, nbr, in_hbm(dham), in_hbm(dovl))
+
+    def cross(parity, payload, before, name):
         cut = pltpu.VMEM((8 * lower, states), jnp.bfloat16)
         return pl.pallas_call(
             functools.partial(cross_kernel, parity),
             out_shape=(force, force),
-            in_specs=[smem] + [vmem] * 12,
+            in_specs=[smem] + [vmem] * 5 + [hbm, hbm] + [vmem] * 4,
             out_specs=(vmem, vmem),
             scratch_shapes=[
                 cut,
@@ -433,17 +448,21 @@
                 pltpu.VMEM((8 * lower, 512), jnp.float32),
                 pltpu.VMEM((slots, LANES), jnp.int32),
                 pltpu.VMEM((3, lower, LANES), jnp.float32),
+                pltpu.VMEM((48, slots, LANES), jnp.float32),
+                pltpu.VMEM((48, slots, LANES), jnp.float32),
+                pltpu.SemaphoreType.DMA((2,)),
             ],
             compiler_params=pltpu.CompilerParams(vmem_limit_bytes=20 * 1024 * 1024),
             cost_estimate=pl.CostEstimate(
                 flops=3 * 2 * 2 * 512 * 256 * states, bytes_accessed=6 * 1024 * 1024, transcendentals=0
             ),
             name=name,
-        )(start, payload, before, back, occup, energies, nbr, dham, dovl, own_high, own_low, near_high, near_low)
-
-    total, core_sent = cross(0, core_payload, inner, jnp.zeros((8, atoms), jnp.float32), "core_pairs")
-    total, far_sent = cross(1, far_payload, total, core_swap(core_sent), "far_pairs")
-    total = (total + shard_swap(far_sent))[:3]
+        )(start, payload, before, occup, energies, nbr, in_hbm(dham), in_hbm(dovl), own_high, own_low, near_high, near_low)
+
+    total, core_sent = cross(0, core_payload, inner, "core_pairs")
+    core_back = core_swap(core_sent)
+    total, far_sent = cross(1, far_payload, total, "far_pairs")
+    total = (total + core_back + shard_swap(far_sent))[:3]
     if lax.axis_size("states") == 2:
         return total + lax.ppermute(total, "states", [(0, 1), (1, 0)])
     return lax.psum(total, "states")

time: 35.1 us -> 35.3 us (level)
  Pallas kernels: 20.9 us -> 22.3 us
  waiting for transfers between devices: 5.22 us -> 4.22 us
    ppermute x2, waiting for transfers between devices: 1.2 us -> 0.01 us  [core_swap(): return lax.ppermute(value, 'sub', [(0, 1), (1, 0)])]
    pallas_call x1, Pallas kernels: 13.8 us -> 14.8 us  [local(): pl.pallas_call(inner_kernel, out_shape=(whole, whole, half, half, force),...]
    pallas_call x2, Pallas kernels: 4.87 us -> 5.38 us  [cross(): pl.pallas_call(functools.partial(cross_kernel, parity), out_shape=(force,...]
  transfers between devices with their start and end apart: 5 -> 5, of which waited for: 3 -> 2; matrix products, arithmetic and copies ran while one was open for 0% -> 0% of each run, Pallas kernels for 45% -> 48%
where the time goes in v5:
time: 35.3 us; the launch traced here: 35.1 us
  Pallas kernels  22.3 us (63%)
  starting transfers between devices  7.88 us (22%)
  waiting for transfers between devices  4.22 us (12%)
  other arithmetic  0.6 us (2%)
    pallas_call x1, Pallas kernels, local(): pl.pallas_call(inner_kernel, out_shape=(whole, whole, half, half, force),...  14.8 us
    ppermute x2, starting transfers between devices, shard_swap(): return lax.ppermute(value, SHARD, pairs)  6.48 us
    pallas_call x2, Pallas kernels, cross(): pl.pallas_call(functools.partial(cross_kernel, parity), out_shape=(force,...  5.38 us
    ppermute x2, waiting for transfers between devices, shard_swap(): return lax.ppermute(value, SHARD, pairs)  2.97 us
    pallas_call x1, Pallas kernels, local(): pl.pallas_call(pack_kernel, out_shape=(payload, payload), in_specs=[smem]...  2.15 us
    ppermute x1, waiting for transfers between devices, local(): return total + lax.ppermute(total, 'states', [(0, 1), (1, 0)])  1.25 us
    ppermute x1, starting transfers between devices, local(): return total + lax.ppermute(total, 'states', [(0, 1), (1, 0)])  1.21 us
  transfers between devices with their start and end apart: 5, of which 2 were waited for; matrix products, arithmetic and copies ran while one was open for 0% of the time, Pallas kernels for 48%

profile of v5, /device:TPU:1, one launch (start us, length us, event | category | flops | bytes accessed | tf_op | source)
XLA Modules:
  0.0 35.1 jit_solution(18009328871185069563)
XLA Ops:
  0.0 0.0 copy-start
  0.0 0.0 copy-start.1
  0.0 0.0 copy-start.2
  0.0 2.1 %pack.1 = (f32[8,320,128]{2,1,0:T(8,128)S(1)}, f32[8,320,128]{2,1,0:T(8,128)S(1)}) custom-call(s32[1]{0:T(128)} %bitcast.start_ref, f32[1024,1024]{1,0:T(8,128)} %coeffs_ref.3, s32[16,256]{1,0:T(8,128)} %nbr_ref.7, f32[48,16,256]{2,1,0:T(8,128)} %dham_ref.7, f32[48,16,256]{2,1,0:T(8,128)} %dovl_ref.7), custom_call_target="tpu_custom_call" | custom-call | tf_op jit(solution)/shard_map/pack/pallas_call | solution.py:397
  2.2 0.1 collective-permute-start.1
  2.3 4.6 %collective-permute-start = (f32[8,320,128]{2,1,0:T(8,128)S(1)}, f32[8,320,128]{2,1,0:T(8,128)S(1)}, u32[]{:S(2)}, u32[]{:S(2)}) collective-permute-start(f32[8,320,128]{2,1,0:T(8,128)S(1)} %get-tuple-element.16), channel_id=1, source_target_pairs={{1,4},{4,1},{5,8},{8,5},{9,12},{12,9},{3,6},{6,3},{7,10},{10,7},{1... | collective-permute-start | bytes 3932168 | tf_op jit(solution)/shard_map/ppermute | solution.py:377
  6.8 0.0 copy-done
  6.9 0.0 copy-done.1
  6.9 0.0 copy-done.2
  6.9 14.8 %inner_pairs.1 = (bf16[1024,1024]{1,0:T(8,128)(2,1)S(1)}, bf16[1024,1024]{1,0:T(8,128)(2,1)S(1)}, bf16[512,1024]{1,0:T(8,128)(2,1)S(1)}, bf16[512,1024]{1,0:T(8,128)(2,1)S(1)}, f32[8,256]{1,0:T(8,128)S(1)}) custom-call(s32[1]{0:T(128)} %bitcast.start_ref, f32[1024,1024]{1,0:T(8,128)} %coeffs_ref.3, f32[1,1024]{1,0:T(1,128)S(1)} %bitcast.3, ...), custom_call_target="tpu_custom_call" | custom-call | flops 7247757312 | bytes 16777216 | tf_op jit(solution)/shard_map/inner_pairs/pallas_call | solution.py:415
  21.6 0.0 collective-permute-done.1.payload_ref
  21.7 2.0 %core_pairs.1 = (f32[8,256]{1,0:T(8,128)S(1)}, f32[8,256]{1,0:T(8,128)S(1)}) custom-call(s32[1]{0:T(128)} %bitcast.start_ref, f32[8,320,128]{2,1,0:T(8,128)S(1)} %collective-permute-done.1.payload_ref, f32[8,256]{1,0:T(8,128)S(1)} %get-tuple-element.18.before_ref, f32[1,1024]{1,0:T(1,128)S(1)} %bitcast.4, f32[1,1024]{1,0:T(1,128)S(1)} %bitcast.7, ...), custom_call_target="tpu_custom_call" | custom-call | flops 1610612736 | bytes 6291456 | tf_op jit(solution)/shard_map/core_pairs/pallas_call | solution.py:440
  23.7 0.0 collective-permute-done.payload_ref
  23.7 3.3 %far_pairs.1 = (f32[8,256]{1,0:T(8,128)S(1)}, f32[8,256]{1,0:T(8,128)S(1)}) custom-call(s32[1]{0:T(128)} %bitcast.start_ref, f32[8,320,128]{2,1,0:T(8,128)S(1)} %collective-permute-done.payload_ref, f32[8,256]{1,0:T(8,128)S(1)} %get-tuple-element.23.before_ref, f32[1,1024]{1,0:T(1,128)S(1)} %bitcast.5, f32[1,1024]{1,0:T(1,128)S(1)} %bitcast.8, ...), custom_call_target="tpu_custom_call" | custom-call | flops 1610612736 | bytes 6291456 | tf_op jit(solution)/shard_map/far_pairs/pallas_call | solution.py:440
  27.1 1.9 %collective-permute-start.3 = (f32[8,256]{1,0:T(8,128)S(1)}, f32[8,256]{1,0:T(8,128)S(1)}, u32[]{:S(2)}, u32[]{:S(2)}) collective-permute-start(f32[8,256]{1,0:T(8,128)S(1)} %get-tuple-element.26), channel_id=1, source_target_pairs={{1,4},{4,1},{5,8},{8,5},{9,12},{12,9},{3,6},{6,3},{7,10},{10,7},{1... | collective-permute-start | bytes 24584 | tf_op jit(solution)/shard_map/ppermute | solution.py:377
  29.0 0.1 collective-permute-start.2
  29.1 3.0 %collective-permute-done.3 = f32[8,256]{1,0:T(8,128)S(1)} collective-permute-done((f32[8,256]{1,0:T(8,128)S(1)}, f32[8,256]{1,0:T(8,128)S(1)}, u32[]{:S(2)}, u32[]{:S(2)}) %collective-permute-start.3) | collective-permute-done | bytes 8224 | tf_op jit(solution)/shard_map/ppermute | solution.py:377
  32.0 0.0 collective-permute-done.2
  32.0 1.2 %collective-permute-start.4 = (f32[3,256]{1,0:T(4,128)S(1)}, f32[3,256]{1,0:T(4,128)S(1)}, u32[]{:S(2)}, u32[]{:S(2)}) collective-permute-start(f32[3,256]{1,0:T(4,128)S(1)} %slice_add_fusion), channel_id=1, source_target_pairs={{0,2},{2,0},{1,3},{3,1},{4,6},{6,4},{5,7},{7,5},{8,10},{10,8},{9,1... | collective-permute-start | bytes 9224 | tf_op jit(solution)/shard_map/ppermute | solution.py:467
  33.3 1.2 %collective-permute-done.4 = f32[3,256]{1,0:T(4,128)S(1)} collective-permute-done((f32[3,256]{1,0:T(4,128)S(1)}, f32[3,256]{1,0:T(4,128)S(1)}, u32[]{:S(2)}, u32[]{:S(2)}) %collective-permute-start.4) | collective-permute-done | bytes 3104 | tf_op jit(solution)/shard_map/ppermute | solution.py:467
  34.5 0.6 %add.15 = f32[3,256]{1,0:T(4,128)} add(f32[3,256]{1,0:T(4,128)S(1)} %slice_add_fusion, f32[3,256]{1,0:T(4,128)S(1)} %collective-permute-done.4) | non-fusion elementwise | flops 768 | bytes 9216 | tf_op jit(solution)/shard_map/add | solution.py:467
  (1 shorter events, 0.0 us)
Async XLA Ops:
  0.0 6.8 %copy-start = (s32[16,256]{1,0:T(8,128)S(1)}, s32[16,256]{1,0:T(8,128)}, u32[]{:S(2)}) copy-start(s32[16,256]{1,0:T(8,128)} %nbr_ref.7) | copy-start | bytes 49156
  0.0 6.9 %copy-start.1 = (f32[1024]{0:T(1024)S(1)}, f32[1024]{0:T(1024)}, u32[]{:S(2)}) copy-start(f32[1024]{0:T(1024)} %param.7) | copy-start | bytes 12292
  0.0 6.9 %copy-start.2 = (f32[1024]{0:T(1024)S(1)}, f32[1024]{0:T(1024)}, u32[]{:S(2)}) copy-start(f32[1024]{0:T(1024)} %param.8) | copy-start | bytes 12292
  2.2 19.5 %collective-permute-start.1 = (f32[8,320,128]{2,1,0:T(8,128)S(1)}, f32[8,320,128]{2,1,0:T(8,128)S(1)}, u32[]{:S(2)}, u32[]{:S(2)}) collective-permute-start(f32[8,320,128]{2,1,0:T(8,128)S(1)} %get-tuple-element.17), channel_id=1, source_target_pairs={{0,1},{1,0},{2,3},{3,2},{4,5},{5,4},{6,7},{7,6},{8,9},{9,8},{10,11... | collective-permute-start | bytes 3932168 | tf_op jit(solution)/shard_map/ppermute | solution.py:371
  2.3 21.4 %collective-permute-start = (f32[8,320,128]{2,1,0:T(8,128)S(1)}, f32[8,320,128]{2,1,0:T(8,128)S(1)}, u32[]{:S(2)}, u32[]{:S(2)}) collective-permute-start(f32[8,320,128]{2,1,0:T(8,128)S(1)} %get-tuple-element.16), channel_id=1, source_target_pairs={{1,4},{4,1},{5,8},{8,5},{9,12},{12,9},{3,6},{6,3},{7,10},{10,7},{1... | collective-permute-start | bytes 3932168 | tf_op jit(solution)/shard_map/ppermute | solution.py:377
  27.1 5.0 %collective-permute-start.3 = (f32[8,256]{1,0:T(8,128)S(1)}, f32[8,256]{1,0:T(8,128)S(1)}, u32[]{:S(2)}, u32[]{:S(2)}) collective-permute-start(f32[8,256]{1,0:T(8,128)S(1)} %get-tuple-element.26), channel_id=1, source_target_pairs={{1,4},{4,1},{5,8},{8,5},{9,12},{12,9},{3,6},{6,3},{7,10},{10,7},{1... | collective-permute-start | bytes 24584 | tf_op jit(solution)/shard_map/ppermute | solution.py:377
  29.0 3.0 %collective-permute-start.2 = (f32[8,256]{1,0:T(8,128)S(1)}, f32[8,256]{1,0:T(8,128)S(1)}, u32[]{:S(2)}, u32[]{:S(2)}) collective-permute-start(f32[8,256]{1,0:T(8,128)S(1)} %get-tuple-element.25), channel_id=1, source_target_pairs={{0,1},{1,0},{2,3},{3,2},{4,5},{5,4},{6,7},{7,6},{8,9},{9,8},{10,11... | collective-permute-start | bytes 24584 | tf_op jit(solution)/shard_map/ppermute | solution.py:371
  32.0 2.5 %collective-permute-start.4 = (f32[3,256]{1,0:T(4,128)S(1)}, f32[3,256]{1,0:T(4,128)S(1)}, u32[]{:S(2)}, u32[]{:S(2)}) collective-permute-start(f32[3,256]{1,0:T(4,128)S(1)} %slice_add_fusion), channel_id=1, source_target_pairs={{0,2},{2,0},{1,3},{3,1},{4,6},{6,4},{5,7},{7,5},{8,10},{10,8},{9,1... | collective-permute-start | bytes 9224 | tf_op jit(solution)/shard_map/ppermute | solution.py:467

commit v6 on v5

--- a/solution.py
+++ b/solution.py
@@ -134,7 +134,7 @@
     start_ref, coeffs_ref, occup_ref, energies_ref, nbr_ref, dham_ref, dovl_ref,
     own_high_ref, own_low_ref, near1_high_ref, near1_low_ref, force_ref,
     near0_high_ref, near0_low_ref, near2_high_ref, near2_low_ref, near3_high_ref, near3_low_ref,
-    gram0_ref, gram1_ref, gram2_ref, gram3_ref, index_ref, spread_ref, columns_ref, ham_ref, ovl_ref, copy_sem, deriv_sem,
+    gram0_ref, gram1_ref, gram2_ref, gram3_ref, index_ref, spread_ref, columns_ref, copy_sem,
 ):
     states = coeffs_ref.shape[1]
     count = states // LANES
@@ -151,11 +151,7 @@
         )
         for c in range(count)
     ]
-    derivs = [
-        pltpu.make_async_copy(source, target, deriv_sem.at[at])
-        for at, (source, target) in enumerate([(dham_ref, ham_ref), (dovl_ref, ovl_ref)])
-    ]
-    for copy in copies + derivs:
+    for copy in copies:
         copy.start()
     occup = occup_ref[...]
     weights = [occup, occup * energies_ref[...]]
@@ -185,7 +181,7 @@
     def pick(h):
         index = [part - BLOCK * (h % 2) for part in block_index(index_ref.at[h // 2], h % 2)]
         blocks = min(h + 3, 4) - h
-        return fold(pick_pairs(grams[h], 0, BLOCK, index, own_deriv(ham_ref, ovl_ref, h // 2, h % 2), blocks))
+        return fold(pick_pairs(grams[h], 0, BLOCK, index, own_deriv(dham_ref, dovl_ref, h // 2, h % 2), blocks))
 
     def finish(tile, even, odd):
         pair = merge(even, odd)
@@ -196,8 +192,6 @@
 
     for h in (3, 2, 1, 0):
         multiply(h)
-    for copy in derivs:
-        copy.wait()
     pair3 = pick(3)
     pair2 = pick(2)
     mine1, theirs1 = finish(1, pair2, pair3)
@@ -282,7 +276,7 @@
     start_ref, payload_ref, before_ref, occup_ref, energies_ref, nbr_ref, dham_ref, dovl_ref,
     own_high_ref, own_low_ref, near_high_ref, near_low_ref,
     force_ref, sent_ref,
-    cut_high_ref, cut_low_ref, gram_ref, index_ref, spread_ref, ham_ref, ovl_ref, deriv_sem,
+    cut_high_ref, cut_low_ref, gram_ref, index_ref, spread_ref,
 ):
     atoms = nbr_ref.shape[1]
     count = payload_ref.shape[0]
@@ -293,12 +287,6 @@
 
     @pl.when(first)
     def above():
-        derivs = [
-            pltpu.make_async_copy(source.at[:, :, LANES:], target, deriv_sem.at[at])
-            for at, (source, target) in enumerate([(dham_ref, ham_ref), (dovl_ref, ovl_ref)])
-        ]
-        for copy in derivs:
-            copy.start()
         occup = occup_ref[...]
         weights = [occup, occup * energies_ref[...]]
         for c in range(count):
@@ -311,13 +299,11 @@
         gram_ref[...] = gram(
             cut_high_ref[...], cut_low_ref[...], own_high_ref[512:, :], own_low_ref[512:, :]
         )
-        for copy in derivs:
-            copy.wait()
         index_ref[...] = nbr_ref[:, LANES:] - (start_ref[0] + atoms)
         even, odd = (
             fold(
                 pick_pairs(
-                    gram_ref, h * 256, lower, block_index(index_ref, h), own_deriv(ham_ref, ovl_ref, 0, h)
+                    gram_ref, h * 256, lower, block_index(index_ref, h), own_deriv(dham_ref, dovl_ref, 1, h)
                 )
             )
             for h in range(2)
@@ -415,7 +401,7 @@
     own_high, own_low, near_high, near_low, inner = pl.pallas_call(
         inner_kernel,
         out_shape=(whole, whole, half, half, force),
-        in_specs=[smem, hbm, vmem, vmem, vmem, hbm, hbm],
+        in_specs=[smem, hbm] + [vmem] * 5,
         out_specs=(vmem,) * 5,
         scratch_shapes=[prepared] * 6
         + [pltpu.VMEM((512 * n, 256), jnp.float32) for n in (3, 3, 2, 1)]
@@ -423,24 +409,21 @@
             pltpu.VMEM((2, slots, LANES), jnp.int32),
             pltpu.VMEM((3, atoms, LANES), jnp.float32),
             pltpu.VMEM((states // LANES, 4 * atoms, LANES), jnp.float32),
-            pltpu.VMEM((48, slots, atoms), jnp.float32),
-            pltpu.VMEM((48, slots, atoms), jnp.float32),
             pltpu.SemaphoreType.DMA((count,)),
-            pltpu.SemaphoreType.DMA((2,)),
         ],
         compiler_params=pltpu.CompilerParams(vmem_limit_bytes=32 * 1024 * 1024),
         cost_estimate=pl.CostEstimate(
             flops=3 * 2 * 9 * 512 * 256 * states, bytes_accessed=16 * 1024 * 1024, transcendentals=0
         ),
         name="inner_pairs",
-    )(start, in_hbm(coeffs), occup, energies, nbr, in_hbm(dham), in_hbm(dovl))
+    )(start, in_hbm(coeffs), occup, energies, nbr, dham, dovl)
 
     def cross(parity, payload, before, name):
         cut = pltpu.VMEM((8 * lower, states), jnp.bfloat16)
         return pl.pallas_call(
             functools.partial(cross_kernel, parity),
             out_shape=(force, force),
-            in_specs=[smem] + [vmem] * 5 + [hbm, hbm] + [vmem] * 4,
+            in_specs=[smem] + [vmem] * 11,
             out_specs=(vmem, vmem),
             scratch_shapes=[
                 cut,
@@ -448,16 +431,13 @@
                 pltpu.VMEM((8 * lower, 512), jnp.float32),
                 pltpu.VMEM((slots, LANES), jnp.int32),
                 pltpu.VMEM((3, lower, LANES), jnp.float32),
-                pltpu.VMEM((48, slots, LANES), jnp.float32),
-                pltpu.VMEM((48, slots, LANES), jnp.float32),
-                pltpu.SemaphoreType.DMA((2,)),
             ],
             compiler_params=pltpu.CompilerParams(vmem_limit_bytes=20 * 1024 * 1024),
             cost_estimate=pl.CostEstimate(
                 flops=3 * 2 * 2 * 512 * 256 * states, bytes_accessed=6 * 1024 * 1024, transcendentals=0
             ),
             name=name,
-        )(start, payload, before, occup, energies, nbr, in_hbm(dham), in_hbm(dovl), own_high, own_low, near_high, near_low)
+        )(start, payload, before, occup, energies, nbr, dham, dovl, own_high, own_low, near_high, near_low)
 
     total, core_sent = cross(0, core_payload, inner, "core_pairs")
     core_back = core_swap(core_sent)

time: 35.3 us -> 33.6 us (0.952)
  Pallas kernels: 22.3 us -> 20.5 us
  starting transfers between devices: 7.88 us -> 8.63 us
  waiting for transfers between devices: 4.22 us -> 3.53 us
    pallas_call x1, Pallas kernels: 14.8 us -> 13.4 us  [local(): pl.pallas_call(inner_kernel, out_shape=(whole, whole, half, half, force),...]
    pallas_call x2, Pallas kernels: 5.38 us -> 4.9 us  [cross(): pl.pallas_call(functools.partial(cross_kernel, parity), out_shape=(force,...]
    ppermute x2, starting transfers between devices: 6.48 us -> 6.94 us  [shard_swap(): return lax.ppermute(value, SHARD, pairs)]
    ppermute x2, waiting for transfers between devices: 2.97 us -> 2.53 us  [shard_swap(): return lax.ppermute(value, SHARD, pairs)]
  transfers between devices with their start and end apart: 5 -> 5, of which waited for: 2 -> 2; matrix products, arithmetic and copies ran while one was open for 0% -> 0% of each run, Pallas kernels for 48% -> 46%
where the time goes in v6:
time: 33.6 us; the launch traced here: 33.4 us
  Pallas kernels  20.5 us (61%)
  starting transfers between devices  8.63 us (26%)
  waiting for transfers between devices  3.53 us (11%)
  other arithmetic  0.6 us (2%)
    pallas_call x1, Pallas kernels, local(): pl.pallas_call(inner_kernel, out_shape=(whole, whole, half, half, force),...  13.4 us
    ppermute x2, starting transfers between devices, shard_swap(): return lax.ppermute(value, SHARD, pairs)  6.94 us
    pallas_call x2, Pallas kernels, cross(): pl.pallas_call(functools.partial(cross_kernel, parity), out_shape=(force,...  4.9 us
    ppermute x2, waiting for transfers between devices, shard_swap(): return lax.ppermute(value, SHARD, pairs)  2.53 us
    pallas_call x1, Pallas kernels, local(): pl.pallas_call(pack_kernel, out_shape=(payload, payload), in_specs=[smem]...  2.23 us
    ppermute x1, starting transfers between devices, local(): return total + lax.ppermute(total, 'states', [(0, 1), (1, 0)])  1.51 us
    ppermute x1, waiting for transfers between devices, local(): return total + lax.ppermute(total, 'states', [(0, 1), (1, 0)])  0.99 us
  transfers between devices with their start and end apart: 5, of which 2 were waited for; matrix products, arithmetic and copies ran while one was open for 0% of the time, Pallas kernels for 46%

profile of v6, /device:TPU:1, one launch (start us, length us, event | category | flops | bytes accessed | tf_op | source)
XLA Modules:
  0.0 33.4 jit_solution(9024621462745733296)
XLA Ops:
  0.0 0.0 copy-start
  0.0 0.0 copy-start.1
  0.0 0.0 copy-start.2
  0.0 0.0 copy-start.3
  0.0 0.0 copy-start.4
  0.0 2.2 %pack.1 = (f32[8,320,128]{2,1,0:T(8,128)S(1)}, f32[8,320,128]{2,1,0:T(8,128)S(1)}) custom-call(s32[1]{0:T(128)} %bitcast.start_ref, f32[1024,1024]{1,0:T(8,128)} %coeffs_ref.3, s32[16,256]{1,0:T(8,128)} %nbr_ref.7, f32[48,16,256]{2,1,0:T(8,128)} %dham_ref.7, f32[48,16,256]{2,1,0:T(8,128)} %dovl_ref.7), custom_call_target="tpu_custom_call" | custom-call | tf_op jit(solution)/shard_map/pack/pallas_call | solution.py:383
  2.3 0.1 collective-permute-start.1
  2.4 4.6 %collective-permute-start = (f32[8,320,128]{2,1,0:T(8,128)S(1)}, f32[8,320,128]{2,1,0:T(8,128)S(1)}, u32[]{:S(2)}, u32[]{:S(2)}) collective-permute-start(f32[8,320,128]{2,1,0:T(8,128)S(1)} %get-tuple-element.16), channel_id=1, source_target_pairs={{1,4},{4,1},{5,8},{8,5},{9,12},{12,9},{3,6},{6,3},{7,10},{10,7},{1... | collective-permute-start | bytes 3932168 | tf_op jit(solution)/shard_map/ppermute | solution.py:363
  6.9 0.0 copy-done
  7.0 0.0 copy-done.1
  7.0 0.0 copy-done.2
  7.0 0.0 copy-done.3
  7.0 0.0 copy-done.4
  7.0 13.4 %inner_pairs.1 = (bf16[1024,1024]{1,0:T(8,128)(2,1)S(1)}, bf16[1024,1024]{1,0:T(8,128)(2,1)S(1)}, bf16[512,1024]{1,0:T(8,128)(2,1)S(1)}, bf16[512,1024]{1,0:T(8,128)(2,1)S(1)}, f32[8,256]{1,0:T(8,128)S(1)}) custom-call(s32[1]{0:T(128)} %bitcast.start_ref, f32[1024,1024]{1,0:T(8,128)} %coeffs_ref.3, f32[1,1024]{1,0:T(1,128)S(1)} %bitcast.3, ...), custom_call_target="tpu_custom_call" | custom-call | flops 7247757312 | bytes 16777216 | tf_op jit(solution)/shard_map/inner_pairs/pallas_call | solution.py:401
  20.4 0.0 collective-permute-done.1.payload_ref
  20.4 2.0 %core_pairs.1 = (f32[8,256]{1,0:T(8,128)S(1)}, f32[8,256]{1,0:T(8,128)S(1)}) custom-call(s32[1]{0:T(128)} %bitcast.start_ref, f32[8,320,128]{2,1,0:T(8,128)S(1)} %collective-permute-done.1.payload_ref, f32[8,256]{1,0:T(8,128)S(1)} %get-tuple-element.18.before_ref, f32[1,1024]{1,0:T(1,128)S(1)} %bitcast.4, f32[1,1024]{1,0:T(1,128)S(1)} %bitcast.7, ...), custom_call_target="tpu_custom_call" | custom-call | flops 1610612736 | bytes 6291456 | tf_op jit(solution)/shard_map/core_pairs/pallas_call | solution.py:423
  22.4 0.0 collective-permute-done.payload_ref
  22.4 2.9 %far_pairs.1 = (f32[8,256]{1,0:T(8,128)S(1)}, f32[8,256]{1,0:T(8,128)S(1)}) custom-call(s32[1]{0:T(128)} %bitcast.start_ref, f32[8,320,128]{2,1,0:T(8,128)S(1)} %collective-permute-done.payload_ref, f32[8,256]{1,0:T(8,128)S(1)} %get-tuple-element.23.before_ref, f32[1,1024]{1,0:T(1,128)S(1)} %bitcast.5, f32[1,1024]{1,0:T(1,128)S(1)} %bitcast.8, ...), custom_call_target="tpu_custom_call" | custom-call | flops 1610612736 | bytes 6291456 | tf_op jit(solution)/shard_map/far_pairs/pallas_call | solution.py:423
  25.3 2.4 %collective-permute-start.3 = (f32[8,256]{1,0:T(8,128)S(1)}, f32[8,256]{1,0:T(8,128)S(1)}, u32[]{:S(2)}, u32[]{:S(2)}) collective-permute-start(f32[8,256]{1,0:T(8,128)S(1)} %get-tuple-element.26), channel_id=1, source_target_pairs={{1,4},{4,1},{5,8},{8,5},{9,12},{12,9},{3,6},{6,3},{7,10},{10,7},{1... | collective-permute-start | bytes 24584 | tf_op jit(solution)/shard_map/ppermute | solution.py:363
  27.7 0.1 collective-permute-start.2
  27.8 2.5 %collective-permute-done.3 = f32[8,256]{1,0:T(8,128)S(1)} collective-permute-done((f32[8,256]{1,0:T(8,128)S(1)}, f32[8,256]{1,0:T(8,128)S(1)}, u32[]{:S(2)}, u32[]{:S(2)}) %collective-permute-start.3) | collective-permute-done | bytes 8224 | tf_op jit(solution)/shard_map/ppermute | solution.py:363
  30.3 0.0 collective-permute-done.2
  30.3 1.5 %collective-permute-start.4 = (f32[3,256]{1,0:T(4,128)S(1)}, f32[3,256]{1,0:T(4,128)S(1)}, u32[]{:S(2)}, u32[]{:S(2)}) collective-permute-start(f32[3,256]{1,0:T(4,128)S(1)} %slice_add_fusion), channel_id=1, source_target_pairs={{0,2},{2,0},{1,3},{3,1},{4,6},{6,4},{5,7},{7,5},{8,10},{10,8},{9,1... | collective-permute-start | bytes 9224 | tf_op jit(solution)/shard_map/ppermute | solution.py:447
  31.8 1.0 %collective-permute-done.4 = f32[3,256]{1,0:T(4,128)S(1)} collective-permute-done((f32[3,256]{1,0:T(4,128)S(1)}, f32[3,256]{1,0:T(4,128)S(1)}, u32[]{:S(2)}, u32[]{:S(2)}) %collective-permute-start.4) | collective-permute-done | bytes 3104 | tf_op jit(solution)/shard_map/ppermute | solution.py:447
  32.8 0.6 %add.15 = f32[3,256]{1,0:T(4,128)} add(f32[3,256]{1,0:T(4,128)S(1)} %slice_add_fusion, f32[3,256]{1,0:T(4,128)S(1)} %collective-permute-done.4) | non-fusion elementwise | flops 768 | bytes 9216 | tf_op jit(solution)/shard_map/add | solution.py:447
  (1 shorter events, 0.0 us)
Async XLA Ops:
  0.0 6.9 %copy-start = (f32[48,16,256]{2,1,0:T(8,128)S(1)}, f32[48,16,256]{2,1,0:T(8,128)}, u32[]{:S(2)}) copy-start(f32[48,16,256]{2,1,0:T(8,128)} %dham_ref.7) | copy-start | bytes 2359300
  0.0 7.0 %copy-start.1 = (f32[48,16,256]{2,1,0:T(8,128)S(1)}, f32[48,16,256]{2,1,0:T(8,128)}, u32[]{:S(2)}) copy-start(f32[48,16,256]{2,1,0:T(8,128)} %dovl_ref.7) | copy-start | bytes 2359300
  0.0 7.0 %copy-start.2 = (s32[16,256]{1,0:T(8,128)S(1)}, s32[16,256]{1,0:T(8,128)}, u32[]{:S(2)}) copy-start(s32[16,256]{1,0:T(8,128)} %nbr_ref.7) | copy-start | bytes 49156
  0.0 7.0 %copy-start.3 = (f32[1024]{0:T(1024)S(1)}, f32[1024]{0:T(1024)}, u32[]{:S(2)}) copy-start(f32[1024]{0:T(1024)} %param.7) | copy-start | bytes 12292
  0.0 7.0 %copy-start.4 = (f32[1024]{0:T(1024)S(1)}, f32[1024]{0:T(1024)}, u32[]{:S(2)}) copy-start(f32[1024]{0:T(1024)} %param.8) | copy-start | bytes 12292
  2.3 18.1 %collective-permute-start.1 = (f32[8,320,128]{2,1,0:T(8,128)S(1)}, f32[8,320,128]{2,1,0:T(8,128)S(1)}, u32[]{:S(2)}, u32[]{:S(2)}) collective-permute-start(f32[8,320,128]{2,1,0:T(8,128)S(1)} %get-tuple-element.17), channel_id=1, source_target_pairs={{0,1},{1,0},{2,3},{3,2},{4,5},{5,4},{6,7},{7,6},{8,9},{9,8},{10,11... | collective-permute-start | bytes 3932168 | tf_op jit(solution)/shard_map/ppermute | solution.py:357
  2.4 20.0 %collective-permute-start = (f32[8,320,128]{2,1,0:T(8,128)S(1)}, f32[8,320,128]{2,1,0:T(8,128)S(1)}, u32[]{:S(2)}, u32[]{:S(2)}) collective-permute-start(f32[8,320,128]{2,1,0:T(8,128)S(1)} %get-tuple-element.16), channel_id=1, source_target_pairs={{1,4},{4,1},{5,8},{8,5},{9,12},{12,9},{3,6},{6,3},{7,10},{10,7},{1... | collective-permute-start | bytes 3932168 | tf_op jit(solution)/shard_map/ppermute | solution.py:363
  25.3 5.0 %collective-permute-start.3 = (f32[8,256]{1,0:T(8,128)S(1)}, f32[8,256]{1,0:T(8,128)S(1)}, u32[]{:S(2)}, u32[]{:S(2)}) collective-permute-start(f32[8,256]{1,0:T(8,128)S(1)} %get-tuple-element.26), channel_id=1, source_target_pairs={{1,4},{4,1},{5,8},{8,5},{9,12},{12,9},{3,6},{6,3},{7,10},{10,7},{1... | collective-permute-start | bytes 24584 | tf_op jit(solution)/shard_map/ppermute | solution.py:363
  27.7 2.6 %collective-permute-start.2 = (f32[8,256]{1,0:T(8,128)S(1)}, f32[8,256]{1,0:T(8,128)S(1)}, u32[]{:S(2)}, u32[]{:S(2)}) collective-permute-start(f32[8,256]{1,0:T(8,128)S(1)} %get-tuple-element.25), channel_id=1, source_target_pairs={{0,1},{1,0},{2,3},{3,2},{4,5},{5,4},{6,7},{7,6},{8,9},{9,8},{10,11... | collective-permute-start | bytes 24584 | tf_op jit(solution)/shard_map/ppermute | solution.py:357
  30.3 2.5 %collective-permute-start.4 = (f32[3,256]{1,0:T(4,128)S(1)}, f32[3,256]{1,0:T(4,128)S(1)}, u32[]{:S(2)}, u32[]{:S(2)}) collective-permute-start(f32[3,256]{1,0:T(4,128)S(1)} %slice_add_fusion), channel_id=1, source_target_pairs={{0,2},{2,0},{1,3},{3,1},{4,6},{6,4},{5,7},{7,5},{8,10},{10,8},{9,1... | collective-permute-start | bytes 9224 | tf_op jit(solution)/shard_map/ppermute | solution.py:447

commit v7 on v6

--- a/solution.py
+++ b/solution.py
@@ -43,22 +43,19 @@
     return jnp.where(lane_numbers() < BLOCK, left, swap_halves(right))
 
 
-def pick_pairs(gram_ref, column, size, index, deriv, blocks=1):
+def pick_pairs(tile, steps, index, deriv):
     low = [part & 7 for part in index]
     high = [part >> 3 for part in index]
     pair = [[None, None] for k in range(3)]
     for x in range(2):
         picked = {}
-        for r in range(size // 8 * blocks):
+        for r in range(steps):
             hit = [part == r for part in high]
             for b in range(4):
-                block, part = divmod(r, size // 8)
-                row = ((block * 2 + x) * 4 + b) * size + part * 8
                 for g in range(2):
-                    at = column + g * LANES
-                    tile = gram_ref[row : row + 8, at : at + LANES]
+                    rows = tile(r, x, b, g)
                     for half in range(2):
-                        got = jnp.take_along_axis(tile, low[half], axis=0)
+                        got = jnp.take_along_axis(rows, low[half], axis=0)
                         before = picked.get((b, g, half), 0.0)
                         picked[b, g, half] = jnp.where(hit[half], got, before)
         for (b, g, half), value in picked.items():
@@ -71,6 +68,15 @@
     return pair
 
 
+def tiles(gram_ref, column, size):
+    def tile(r, x, b, g):
+        block, part = divmod(r, size // 8)
+        row = ((block * 2 + x) * 4 + b) * size + part * 8
+        return gram_ref[row : row + 8, column + g * LANES : column + (g + 1) * LANES]
+
+    return tile
+
+
 def fold(pair):
     return [[value + swap_halves(value) for value in parts] for parts in pair]
 
@@ -84,18 +90,23 @@
     return [jnp.sum(pair[k][0] + pair[k][1], axis=0, keepdims=True) for k in range(3)]
 
 
-def spread(index_ref, pair, spread_ref, rows):
-    lane_rows = lax.broadcasted_iota(jnp.int32, (8, LANES), 0)
+def slot_map(index_ref, r):
+    target = lax.broadcasted_iota(jnp.int32, (8, LANES), 0) + 8 * r
+    slot = jnp.full((8, LANES), 16, jnp.int32)
+    for n in range(16):
+        hit = jnp.broadcast_to(index_ref[n : n + 1, :], (8, LANES)) == target
+        slot = jnp.where(hit, n, slot)
+    return slot
+
+
+def spread(slot, pair, spread_ref, rows):
     for r in range(rows // 8):
-        slot = jnp.full((8, LANES), 16, jnp.int32)
-        for n in range(16):
-            hit = jnp.broadcast_to(index_ref[n : n + 1, :], (8, LANES)) == lane_rows + 8 * r
-            slot = jnp.where(hit, n, slot)
-        low = slot & 7
+        slots = slot(r)
+        low = slots & 7
         for k in range(3):
             first = jnp.take_along_axis(pair[k][0], low, axis=0)
             second = jnp.take_along_axis(pair[k][1], low, axis=0)
-            value = jnp.where(slot < 8, first, jnp.where(slot < 16, second, 0.0))
+            value = jnp.where(slots < 8, first, jnp.where(slots < 16, second, 0.0))
             spread_ref[k, 8 * r : 8 * r + 8, :] = value
     ones = jnp.ones((8, LANES), jnp.float32)
     out = []
@@ -111,16 +122,8 @@
     return out
 
 
-def own_deriv(dham_ref, dovl_ref, tile, odd):
-    def deriv(k, x, b, g, half):
-        ref = (dham_ref, dovl_ref)[x]
-        parts = [
-            ref[k * 16 + (2 * g + parity) * 4 + b, 8 * half : 8 * half + 8, tile * LANES : (tile + 1) * LANES]
-            for parity in range(2)
-        ]
-        return side_by_side(parts[0], parts[1], odd)
-
-    return deriv
+def deriv_at(k, x, b, g, half):
+    return (((k * 2 + x) * 4 + b) * 2 + g) * 2 + half
 
 
 def block_index(index_ref, odd):
@@ -132,7 +135,7 @@
 
 def inner_kernel(
     start_ref, coeffs_ref, occup_ref, energies_ref, nbr_ref, dham_ref, dovl_ref,
-    own_high_ref, own_low_ref, near1_high_ref, near1_low_ref, force_ref,
+    own_high_ref, own_low_ref, near1_high_ref, near1_low_ref, force_ref, deriv_ref, slot_ref,
     near0_high_ref, near0_low_ref, near2_high_ref, near2_low_ref, near3_high_ref, near3_low_ref,
     gram0_ref, gram1_ref, gram2_ref, gram3_ref, index_ref, spread_ref, columns_ref, copy_sem,
 ):
@@ -156,6 +159,25 @@
     occup = occup_ref[...]
     weights = [occup, occup * energies_ref[...]]
 
+    for tile in range(2):
+        index_ref[tile] = nbr_ref[:, tile * LANES : (tile + 1) * LANES] - (start_ref[0] + tile * LANES)
+    for h in range(4):
+        lanes = slice(h // 2 * LANES, (h // 2 + 1) * LANES)
+        for x, ref in enumerate((dham_ref, dovl_ref)):
+            for k in range(3):
+                for b in range(4):
+                    for g in range(2):
+                        for half in range(2):
+                            parts = [
+                                ref[k * 16 + (2 * g + parity) * 4 + b, 8 * half : 8 * half + 8, lanes]
+                                for parity in range(2)
+                            ]
+                            at = deriv_at(k, x, b, g, half)
+                            deriv_ref[h, at] = side_by_side(parts[0], parts[1], h % 2)
+    for r in range(32):
+        slot_ref[r] = slot_map(index_ref.at[0], r)
+    for r in range(32 - UPPER // 8):
+        slot_ref[32 + r] = slot_map(index_ref.at[1], r)
     for c, copy in enumerate(copies):
         copy.wait()
         lanes = slice(c * LANES, (c + 1) * LANES)
@@ -175,19 +197,17 @@
                 near[j][0][...], near[j][1][...], own_high_ref[own, :], own_low_ref[own, :]
             )
 
-    for tile in range(2):
-        index_ref[tile] = nbr_ref[:, tile * LANES : (tile + 1) * LANES] - (start_ref[0] + tile * LANES)
-
     def pick(h):
         index = [part - BLOCK * (h % 2) for part in block_index(index_ref.at[h // 2], h % 2)]
-        blocks = min(h + 3, 4) - h
-        return fold(pick_pairs(grams[h], 0, BLOCK, index, own_deriv(dham_ref, dovl_ref, h // 2, h % 2), blocks))
+        steps = (min(h + 3, 4) - h) * BLOCK // 8
+        return fold(
+            pick_pairs(tiles(grams[h], 0, BLOCK), steps, index, lambda *key: deriv_ref[h, deriv_at(*key)])
+        )
 
     def finish(tile, even, odd):
         pair = merge(even, odd)
         mine = slot_sum(pair)
-        rows = 256 - tile * LANES
-        theirs = spread(index_ref.at[tile], pair, spread_ref, rows)
+        theirs = spread(lambda r: slot_ref[32 * tile + r], pair, spread_ref, 256 - tile * LANES)
         return mine, theirs
 
     for h in (3, 2, 1, 0):
@@ -273,7 +293,7 @@
 
 def cross_kernel(
     parity,
-    start_ref, payload_ref, before_ref, occup_ref, energies_ref, nbr_ref, dham_ref, dovl_ref,
+    start_ref, payload_ref, before_ref, occup_ref, energies_ref, nbr_ref, deriv_ref, slot_ref,
     own_high_ref, own_low_ref, near_high_ref, near_low_ref,
     force_ref, sent_ref,
     cut_high_ref, cut_low_ref, gram_ref, index_ref, spread_ref,
@@ -289,28 +309,43 @@
     def above():
         occup = occup_ref[...]
         weights = [occup, occup * energies_ref[...]]
+        extra = lower - BLOCK
         for c in range(count):
             lanes = slice(c * LANES, (c + 1) * LANES)
             for b in range(4):
-                rows = payload_ref[c, pl.ds(b, lower, stride=4), :]
+                rows = payload_ref[c, pl.ds(b, BLOCK, stride=4), :]
                 for x in range(2):
-                    at = slice((x * 4 + b) * lower, (x * 4 + b + 1) * lower)
+                    at = slice((x * 4 + b) * BLOCK, (x * 4 + b + 1) * BLOCK)
                     cut_high_ref[at, lanes], cut_low_ref[at, lanes] = split(rows * weights[x][:, lanes])
-        gram_ref[...] = gram(
-            cut_high_ref[...], cut_low_ref[...], own_high_ref[512:, :], own_low_ref[512:, :]
+                rows = payload_ref[c, pl.ds(4 * BLOCK + b, extra, stride=4), :]
+                for x in range(2):
+                    at = slice(512 + (x * 4 + b) * extra, 512 + (x * 4 + b + 1) * extra)
+                    cut_high_ref[at, lanes], cut_low_ref[at, lanes] = split(rows * weights[x][:, lanes])
+        gram_ref[:512, :] = gram(
+            cut_high_ref[:512, :], cut_low_ref[:512, :], own_high_ref[512:, :], own_low_ref[512:, :]
+        )
+        gram_ref[512:, 256:] = gram(
+            cut_high_ref[512:, :], cut_low_ref[512:, :], own_high_ref[768:, :], own_low_ref[768:, :]
         )
         index_ref[...] = nbr_ref[:, LANES:] - (start_ref[0] + atoms)
-        even, odd = (
-            fold(
-                pick_pairs(
-                    gram_ref, h * 256, lower, block_index(index_ref, h), own_deriv(dham_ref, dovl_ref, 1, h)
-                )
+        near_tile = tiles(gram_ref, 256, BLOCK)
+        extra_tile = tiles(gram_ref.at[512:, :], 256, extra)
+
+        def odd_tile(r, *key):
+            return near_tile(r, *key) if r < BLOCK // 8 else extra_tile(r - BLOCK // 8, *key)
+
+        pairs = [
+            pick_pairs(
+                (tiles(gram_ref, 0, BLOCK), odd_tile)[h],
+                (BLOCK, lower)[h] // 8,
+                block_index(index_ref, h),
+                lambda *key: deriv_ref[2 + h, deriv_at(*key)],
             )
             for h in range(2)
-        )
-        pair = merge(even, odd)
+        ]
+        pair = merge(fold(pairs[0]), fold(pairs[1]))
         mine = slot_sum(pair)
-        theirs = spread(index_ref, pair, spread_ref, lower)
+        theirs = spread(lambda r: slot_ref[48 + r], pair, spread_ref, lower)
         for k in range(3):
             force_ref[k : k + 1, LANES:] += -2.0 * mine[k]
             sent_ref[k : k + 1, :lower] = 2.0 * theirs[k]
@@ -341,8 +376,8 @@
             at = 4 * UPPER + 16 * (plane // count) + 8 * half
             return payload_ref[plane % count, at : at + 8, :]
 
-        pair = pick_pairs(gram_ref, 0, BLOCK, index, deriv)
-        theirs = spread(index_ref, pair, spread_ref, BLOCK)
+        pair = pick_pairs(tiles(gram_ref, 0, BLOCK), BLOCK // 8, index, deriv)
+        theirs = spread(functools.partial(slot_map, index_ref), pair, spread_ref, BLOCK)
         mine = slot_sum(fold(pair))
         for k in range(3):
             force_ref[k : k + 1, BLOCK:LANES] += 2.0 * theirs[k]
@@ -398,11 +433,15 @@
     )(start, *(in_hbm(value) for value in (coeffs, nbr, dham, dovl)))
     far_payload = shard_swap(far_payload)
     core_payload = core_swap(core_payload)
-    own_high, own_low, near_high, near_low, inner = pl.pallas_call(
+    own_high, own_low, near_high, near_low, inner, derivs, slot_maps = pl.pallas_call(
         inner_kernel,
-        out_shape=(whole, whole, half, half, force),
+        out_shape=(
+            whole, whole, half, half, force,
+            jax.ShapeDtypeStruct((4, 96, 8, LANES), jnp.float32),
+            jax.ShapeDtypeStruct((64 - UPPER // 8, 8, LANES), jnp.int32),
+        ),
         in_specs=[smem, hbm] + [vmem] * 5,
-        out_specs=(vmem,) * 5,
+        out_specs=(vmem,) * 7,
         scratch_shapes=[prepared] * 6
         + [pltpu.VMEM((512 * n, 256), jnp.float32) for n in (3, 3, 2, 1)]
         + [
@@ -437,7 +476,7 @@
                 flops=3 * 2 * 2 * 512 * 256 * states, bytes_accessed=6 * 1024 * 1024, transcendentals=0
             ),
             name=name,
-        )(start, payload, before, occup, energies, nbr, dham, dovl, own_high, own_low, near_high, near_low)
+        )(start, payload, before, occup, energies, nbr, derivs, slot_maps, own_high, own_low, near_high, near_low)
 
     total, core_sent = cross(0, core_payload, inner, "core_pairs")
     core_back = core_swap(core_sent)

time: 33.6 us -> 33.9 us (level)
  starting transfers between devices: 8.63 us -> 8.1 us
  waiting for transfers between devices: 3.53 us -> 4.01 us
  Pallas kernels: 20.5 us -> 20.9 us
    ppermute x2, starting transfers between devices: 6.94 us -> 6.52 us  [shard_swap(): return lax.ppermute(value, SHARD, pairs)]
    ppermute x2, waiting for transfers between devices: 2.53 us -> 2.95 us  [shard_swap(): return lax.ppermute(value, SHARD, pairs)]
where the time goes in v7:
time: 33.9 us; the launch traced here: 33.8 us
  Pallas kernels  20.9 us (62%)
  starting transfers between devices  8.1 us (24%)
  waiting for transfers between devices  4.01 us (12%)
  other arithmetic  0.6 us (2%)
    pallas_call x1, Pallas kernels, local(): pl.pallas_call(inner_kernel, out_shape=(whole, whole, half, half, force,...  13.5 us
    ppermute x2, starting transfers between devices, shard_swap(): return lax.ppermute(value, SHARD, pairs)  6.52 us
    pallas_call x2, Pallas kernels, cross(): pl.pallas_call(functools.partial(cross_kernel, parity), out_shape=(force,...  5.2 us
    ppermute x2, waiting for transfers between devices, shard_swap(): return lax.ppermute(value, SHARD, pairs)  2.95 us
    pallas_call x1, Pallas kernels, local(): pl.pallas_call(pack_kernel, out_shape=(payload, payload), in_specs=[smem]...  2.23 us
    ppermute x1, starting transfers between devices, local(): return total + lax.ppermute(total, 'states', [(0, 1), (1, 0)])  1.4 us
    ppermute x1, waiting for transfers between devices, local(): return total + lax.ppermute(total, 'states', [(0, 1), (1, 0)])  1.06 us
  transfers between devices with their start and end apart: 5, of which 2 were waited for; matrix products, arithmetic and copies ran while one was open for 0% of the time, Pallas kernels for 46%

profile of v7, /device:TPU:1, one launch (start us, length us, event | category | flops | bytes accessed | tf_op | source)
XLA Modules:
  0.0 33.8 jit_solution(3140085429634753724)
XLA Ops:
  0.0 0.0 copy-start
  0.0 0.0 copy-start.1
  0.0 0.0 copy-start.2
  0.0 0.0 copy-start.3
  0.0 0.0 copy-start.4
  0.0 2.2 %pack.1 = (f32[8,320,128]{2,1,0:T(8,128)S(1)}, f32[8,320,128]{2,1,0:T(8,128)S(1)}) custom-call(s32[1]{0:T(128)} %bitcast.start_ref, f32[1024,1024]{1,0:T(8,128)} %coeffs_ref.3, s32[16,256]{1,0:T(8,128)} %nbr_ref.7, f32[48,16,256]{2,1,0:T(8,128)} %dham_ref.3, f32[48,16,256]{2,1,0:T(8,128)} %dovl_ref.3), custom_call_target="tpu_custom_call" | custom-call | tf_op jit(solution)/shard_map/pack/pallas_call | solution.py:418
  2.3 0.1 collective-permute-start.1
  2.4 4.6 %collective-permute-start = (f32[8,320,128]{2,1,0:T(8,128)S(1)}, f32[8,320,128]{2,1,0:T(8,128)S(1)}, u32[]{:S(2)}, u32[]{:S(2)}) collective-permute-start(f32[8,320,128]{2,1,0:T(8,128)S(1)} %get-tuple-element.18), channel_id=1, source_target_pairs={{1,4},{4,1},{5,8},{8,5},{9,12},{12,9},{3,6},{6,3},{7,10},{10,7},{1... | collective-permute-start | bytes 3932168 | tf_op jit(solution)/shard_map/ppermute | solution.py:398
  6.9 0.0 copy-done
  7.0 0.0 copy-done.1
  7.0 0.0 copy-done.2
  7.0 0.0 copy-done.3
  7.0 0.0 copy-done.4
  7.0 13.5 %inner_pairs.1 = (bf16[1024,1024]{1,0:T(8,128)(2,1)S(1)}, bf16[1024,1024]{1,0:T(8,128)(2,1)S(1)}, bf16[512,1024]{1,0:T(8,128)(2,1)S(1)}, bf16[512,1024]{1,0:T(8,...) custom-call(s32[1]{0:T(128)} %bitcast.start_ref, ...), custom_call_target="tpu_custom_call" | custom-call | flops 7247757312 | bytes 16777216 | tf_op jit(solution)/shard_map/inner_pairs/pallas_call | solution.py:436
  20.5 0.0 collective-permute-done.1.payload_ref
  20.5 2.0 %core_pairs.1 = (f32[8,256]{1,0:T(8,128)S(1)}, f32[8,256]{1,0:T(8,128)S(1)}) custom-call(s32[1]{0:T(128)} %bitcast.start_ref, f32[8,320,128]{2,1,0:T(8,128)S(1)} %collective-permute-done.1.payload_ref, f32[8,256]{1,0:T(8,128)S(1)} %get-tuple-element.20.before_ref, f32[1,1024]{1,0:T(1,128)S(1)} %bitcast.4, f32[1,1024]{1,0:T(1,128)S(1)} %bitcast.7, ...), custom_call_target="tpu_custom_call" | custom-call | flops 1610612736 | bytes 6291456 | tf_op jit(solution)/shard_map/core_pairs/pallas_call | solution.py:462
  22.5 0.0 collective-permute-done.payload_ref
  22.5 3.2 %far_pairs.1 = (f32[8,256]{1,0:T(8,128)S(1)}, f32[8,256]{1,0:T(8,128)S(1)}) custom-call(s32[1]{0:T(128)} %bitcast.start_ref, f32[8,320,128]{2,1,0:T(8,128)S(1)} %collective-permute-done.payload_ref, f32[8,256]{1,0:T(8,128)S(1)} %get-tuple-element.27.before_ref, f32[1,1024]{1,0:T(1,128)S(1)} %bitcast.5, f32[1,1024]{1,0:T(1,128)S(1)} %bitcast.8, ...), custom_call_target="tpu_custom_call" | custom-call | flops 1610612736 | bytes 6291456 | tf_op jit(solution)/shard_map/far_pairs/pallas_call | solution.py:462
  25.7 2.0 %collective-permute-start.3 = (f32[8,256]{1,0:T(8,128)S(1)}, f32[8,256]{1,0:T(8,128)S(1)}, u32[]{:S(2)}, u32[]{:S(2)}) collective-permute-start(f32[8,256]{1,0:T(8,128)S(1)} %get-tuple-element.30), channel_id=1, source_target_pairs={{1,4},{4,1},{5,8},{8,5},{9,12},{12,9},{3,6},{6,3},{7,10},{10,7},{1... | collective-permute-start | bytes 24584 | tf_op jit(solution)/shard_map/ppermute | solution.py:398
  27.7 0.1 collective-permute-start.2
  27.8 2.9 %collective-permute-done.3 = f32[8,256]{1,0:T(8,128)S(1)} collective-permute-done((f32[8,256]{1,0:T(8,128)S(1)}, f32[8,256]{1,0:T(8,128)S(1)}, u32[]{:S(2)}, u32[]{:S(2)}) %collective-permute-start.3) | collective-permute-done | bytes 8224 | tf_op jit(solution)/shard_map/ppermute | solution.py:398
  30.7 0.0 collective-permute-done.2
  30.7 1.4 %collective-permute-start.4 = (f32[3,256]{1,0:T(4,128)S(1)}, f32[3,256]{1,0:T(4,128)S(1)}, u32[]{:S(2)}, u32[]{:S(2)}) collective-permute-start(f32[3,256]{1,0:T(4,128)S(1)} %slice_add_fusion), channel_id=1, source_target_pairs={{0,2},{2,0},{1,3},{3,1},{4,6},{6,4},{5,7},{7,5},{8,10},{10,8},{9,1... | collective-permute-start | bytes 9224 | tf_op jit(solution)/shard_map/ppermute | solution.py:486
  32.1 1.1 %collective-permute-done.4 = f32[3,256]{1,0:T(4,128)S(1)} collective-permute-done((f32[3,256]{1,0:T(4,128)S(1)}, f32[3,256]{1,0:T(4,128)S(1)}, u32[]{:S(2)}, u32[]{:S(2)}) %collective-permute-start.4) | collective-permute-done | bytes 3104 | tf_op jit(solution)/shard_map/ppermute | solution.py:486
  33.2 0.6 %add.15 = f32[3,256]{1,0:T(4,128)} add(f32[3,256]{1,0:T(4,128)S(1)} %slice_add_fusion, f32[3,256]{1,0:T(4,128)S(1)} %collective-permute-done.4) | non-fusion elementwise | flops 768 | bytes 9216 | tf_op jit(solution)/shard_map/add | solution.py:486
  (1 shorter events, 0.0 us)
Async XLA Ops:
  0.0 6.9 %copy-start = (f32[48,16,256]{2,1,0:T(8,128)S(1)}, f32[48,16,256]{2,1,0:T(8,128)}, u32[]{:S(2)}) copy-start(f32[48,16,256]{2,1,0:T(8,128)} %dham_ref.3) | copy-start | bytes 2359300
  0.0 7.0 %copy-start.1 = (f32[48,16,256]{2,1,0:T(8,128)S(1)}, f32[48,16,256]{2,1,0:T(8,128)}, u32[]{:S(2)}) copy-start(f32[48,16,256]{2,1,0:T(8,128)} %dovl_ref.3) | copy-start | bytes 2359300
  0.0 7.0 %copy-start.2 = (s32[16,256]{1,0:T(8,128)S(1)}, s32[16,256]{1,0:T(8,128)}, u32[]{:S(2)}) copy-start(s32[16,256]{1,0:T(8,128)} %nbr_ref.7) | copy-start | bytes 49156
  0.0 7.0 %copy-start.3 = (f32[1024]{0:T(1024)S(1)}, f32[1024]{0:T(1024)}, u32[]{:S(2)}) copy-start(f32[1024]{0:T(1024)} %param.7) | copy-start | bytes 12292
  0.0 7.0 %copy-start.4 = (f32[1024]{0:T(1024)S(1)}, f32[1024]{0:T(1024)}, u32[]{:S(2)}) copy-start(f32[1024]{0:T(1024)} %param.8) | copy-start | bytes 12292
  2.3 18.2 %collective-permute-start.1 = (f32[8,320,128]{2,1,0:T(8,128)S(1)}, f32[8,320,128]{2,1,0:T(8,128)S(1)}, u32[]{:S(2)}, u32[]{:S(2)}) collective-permute-start(f32[8,320,128]{2,1,0:T(8,128)S(1)} %get-tuple-element.19), channel_id=1, source_target_pairs={{0,1},{1,0},{2,3},{3,2},{4,5},{5,4},{6,7},{7,6},{8,9},{9,8},{10,11... | collective-permute-start | bytes 3932168 | tf_op jit(solution)/shard_map/ppermute | solution.py:392
  2.4 20.2 %collective-permute-start = (f32[8,320,128]{2,1,0:T(8,128)S(1)}, f32[8,320,128]{2,1,0:T(8,128)S(1)}, u32[]{:S(2)}, u32[]{:S(2)}) collective-permute-start(f32[8,320,128]{2,1,0:T(8,128)S(1)} %get-tuple-element.18), channel_id=1, source_target_pairs={{1,4},{4,1},{5,8},{8,5},{9,12},{12,9},{3,6},{6,3},{7,10},{10,7},{1... | collective-permute-start | bytes 3932168 | tf_op jit(solution)/shard_map/ppermute | solution.py:398
  25.7 5.0 %collective-permute-start.3 = (f32[8,256]{1,0:T(8,128)S(1)}, f32[8,256]{1,0:T(8,128)S(1)}, u32[]{:S(2)}, u32[]{:S(2)}) collective-permute-start(f32[8,256]{1,0:T(8,128)S(1)} %get-tuple-element.30), channel_id=1, source_target_pairs={{1,4},{4,1},{5,8},{8,5},{9,12},{12,9},{3,6},{6,3},{7,10},{10,7},{1... | collective-permute-start | bytes 24584 | tf_op jit(solution)/shard_map/ppermute | solution.py:398
  27.7 3.0 %collective-permute-start.2 = (f32[8,256]{1,0:T(8,128)S(1)}, f32[8,256]{1,0:T(8,128)S(1)}, u32[]{:S(2)}, u32[]{:S(2)}) collective-permute-start(f32[8,256]{1,0:T(8,128)S(1)} %get-tuple-element.29), channel_id=1, source_target_pairs={{0,1},{1,0},{2,3},{3,2},{4,5},{5,4},{6,7},{7,6},{8,9},{9,8},{10,11... | collective-permute-start | bytes 24584 | tf_op jit(solution)/shard_map/ppermute | solution.py:392
  30.7 2.5 %collective-permute-start.4 = (f32[3,256]{1,0:T(4,128)S(1)}, f32[3,256]{1,0:T(4,128)S(1)}, u32[]{:S(2)}, u32[]{:S(2)}) collective-permute-start(f32[3,256]{1,0:T(4,128)S(1)} %slice_add_fusion), channel_id=1, source_target_pairs={{0,2},{2,0},{1,3},{3,1},{4,6},{6,4},{5,7},{7,5},{8,10},{10,8},{9,1... | collective-permute-start | bytes 9224 | tf_op jit(solution)/shard_map/ppermute | solution.py:486

commit v8 on v7

--- a/solution.py
+++ b/solution.py
@@ -176,7 +176,7 @@
                             deriv_ref[h, at] = side_by_side(parts[0], parts[1], h % 2)
     for r in range(32):
         slot_ref[r] = slot_map(index_ref.at[0], r)
-    for r in range(32 - UPPER // 8):
+    for r in range(32):
         slot_ref[32 + r] = slot_map(index_ref.at[1], r)
     for c, copy in enumerate(copies):
         copy.wait()
@@ -229,44 +229,57 @@
     return max(4 * (atoms // 2 - UPPER), 4 * UPPER + 16 * planes + 16)
 
 
-def pack_kernel(
-    start_ref, coeffs_ref, nbr_ref, dham_ref, dovl_ref, core_ref, far_ref,
-    ham_ref, ovl_ref, last_ref, core_sem, far_sem, deriv_sem,
+def is_lower(start_ref, atoms):
+    return ((start_ref[0] // atoms) & 1) == 0
+
+
+def far_pack_kernel(
+    start_ref, coeffs_ref, nbr_ref, dham_ref, dovl_ref, far_ref,
+    ham_ref, ovl_ref, last_ref, rows_sem, deriv_sem,
 ):
     atoms = nbr_ref.shape[1]
-    count, rows, unused = core_ref.shape
+    count, rows, unused = far_ref.shape
     lower = 4 * (atoms // 2 - UPPER)
-    first = ((start_ref[0] // atoms) & 1) == 0
-    fetched = [
-        pltpu.make_async_copy(source.at[:, :, atoms - LANES :], target, deriv_sem.at[at])
-        for at, (source, target) in enumerate([(dham_ref, ham_ref), (dovl_ref, ovl_ref)])
-    ]
-    fetched.append(
-        pltpu.make_async_copy(nbr_ref.at[:, atoms - LANES :], last_ref, deriv_sem.at[2])
-    )
-
-    def fill(up_ref, up_sem, down_ref, down_sem):
-        copies = []
-        for c in range(count):
-            lanes = slice(c * LANES, (c + 1) * LANES)
-            up_rows = coeffs_ref.at[4 * (atoms - UPPER) :, lanes]
-            copies.append(pltpu.make_async_copy(up_rows, up_ref.at[c, : 4 * UPPER, :], up_sem.at[c]))
-            down_rows = coeffs_ref.at[:lower, lanes]
-            copies.append(pltpu.make_async_copy(down_rows, down_ref.at[c, :lower, :], down_sem.at[c]))
-        for copy in fetched + copies:
+
+    def copy_rows(first, size):
+        copies = [
+            pltpu.make_async_copy(
+                coeffs_ref.at[first : first + size, c * LANES : (c + 1) * LANES],
+                far_ref.at[c, :size, :],
+                rows_sem.at[c],
+            )
+            for c in range(count)
+        ]
+        for copy in copies:
             copy.start()
-        if rows > lower:
-            down_ref[:, lower:, :] = jnp.zeros((count, rows - lower, LANES), jnp.float32)
-        up_ref[:, 4 * UPPER :, :] = jnp.zeros((count, rows - 4 * UPPER, LANES), jnp.float32)
-        planes = -(-48 // count)
+        if rows > size:
+            far_ref[:, size:, :] = jnp.zeros((count, rows - size, LANES), jnp.float32)
+        return copies
+
+    @pl.when(is_lower(start_ref, atoms))
+    def down():
+        for copy in copy_rows(0, lower):
+            copy.wait()
+
+    @pl.when(jnp.logical_not(is_lower(start_ref, atoms)))
+    def up():
+        sources = ((dham_ref.at[:, :, atoms - LANES :], ham_ref), (dovl_ref.at[:, :, atoms - LANES :], ovl_ref))
+        sources += ((nbr_ref.at[:, atoms - LANES :], last_ref),)
+        fetched = [
+            pltpu.make_async_copy(source, target, deriv_sem.at[at])
+            for at, (source, target) in enumerate(sources)
+        ]
+        for copy in fetched:
+            copy.start()
+        copies = copy_rows(4 * (atoms - UPPER), 4 * UPPER)
         for copy in fetched:
             copy.wait()
         last = last_ref[...]
         target = jnp.where(last >= 0, last - (start_ref[0] + atoms), -1).astype(jnp.float32)
-        at = 4 * UPPER + 16 * planes
+        at = 4 * UPPER + 16 * -(-48 // count)
         for half in range(2):
             part = target[8 * half : 8 * half + 8]
-            up_ref[0, at + 8 * half : at + 8 * half + 8, :] = side_by_side(part, part, 1)
+            far_ref[0, at + 8 * half : at + 8 * half + 8, :] = side_by_side(part, part, 1)
         for x, ref in enumerate((ham_ref, ovl_ref)):
             for k in range(3):
                 for g in range(2):
@@ -278,24 +291,95 @@
                                 for parity in range(2)
                             ]
                             at = 4 * UPPER + 16 * (plane // count) + 8 * half
-                            up_ref[plane % count, at : at + 8, :] = side_by_side(parts[0], parts[1], 1)
+                            far_ref[plane % count, at : at + 8, :] = side_by_side(parts[0], parts[1], 1)
         for copy in copies:
             copy.wait()
 
-    @pl.when(first)
-    def even():
-        fill(core_ref, core_sem, far_ref, far_sem)
-
-    @pl.when(jnp.logical_not(first))
-    def odd():
-        fill(far_ref, far_sem, core_ref, core_sem)
-
-
-def cross_kernel(
-    parity,
+
+def core_pack_kernel(start_ref, coeffs_ref, far_ref, first_ref, second_ref, copy_sem):
+    count, rows, unused = first_ref.shape
+
+    @pl.when(jnp.logical_not(is_lower(start_ref, rows)))
+    def pack():
+        copies = [
+            pltpu.make_async_copy(
+                coeffs_ref.at[at * rows : (at + 1) * rows, c * LANES : (c + 1) * LANES],
+                half_ref.at[c],
+                copy_sem.at[at * count + c],
+            )
+            for at, half_ref in enumerate((first_ref, second_ref))
+            for c in range(count)
+        ]
+        for copy in copies:
+            copy.start()
+        for copy in copies:
+            copy.wait()
+
+
+def above(
+    lower, start_ref, payload_refs, occup_ref, energies_ref, nbr_ref, deriv_ref, slot_ref,
+    own_high_ref, own_low_ref, force_ref, sent_ref,
+    cut_high_ref, cut_low_ref, gram_ref, index_ref, spread_ref,
+):
+    atoms = nbr_ref.shape[1]
+    occup = occup_ref[...]
+    weights = [occup, occup * energies_ref[...]]
+    size = BLOCK if lower % BLOCK == 0 else lower
+    for c in range(payload_refs[0].shape[0]):
+        lanes = slice(c * LANES, (c + 1) * LANES)
+        for block in range(lower // size):
+            for b in range(4):
+                rows = payload_refs[block][c, pl.ds(b, size, stride=4), :]
+                for x in range(2):
+                    at = ((block * 2 + x) * 4 + b) * size
+                    cut_high_ref[at : at + size, lanes], cut_low_ref[at : at + size, lanes] = split(
+                        rows * weights[x][:, lanes]
+                    )
+    for block in range(lower // size):
+        rows = slice(block * 8 * size, (block + 1) * 8 * size)
+        skip = 256 * block
+        gram_ref[rows, skip:] = gram(
+            cut_high_ref[rows, :], cut_low_ref[rows, :], own_high_ref[512 + skip :, :], own_low_ref[512 + skip :, :]
+        )
+    index_ref[...] = nbr_ref[:, LANES:] - (start_ref[0] + atoms)
+    even, odd = (
+        fold(
+            pick_pairs(
+                tiles(gram_ref, 256 * h, size),
+                (BLOCK, lower)[h] // 8,
+                block_index(index_ref, h),
+                lambda *key: deriv_ref[2 + h, deriv_at(*key)],
+            )
+        )
+        for h in range(2)
+    )
+    pair = merge(even, odd)
+    mine = slot_sum(pair)
+    theirs = spread(lambda r: slot_ref[48 + r], pair, spread_ref, lower)
+    for k in range(3):
+        force_ref[k : k + 1, LANES:] += -2.0 * mine[k]
+        sent_ref[k : k + 1, :lower] = 2.0 * theirs[k]
+
+
+def core_kernel(
+    start_ref, first_ref, second_ref, before_ref, occup_ref, energies_ref, nbr_ref, deriv_ref, slot_ref,
+    own_high_ref, own_low_ref, force_ref, sent_ref, *scratch,
+):
+    atoms = nbr_ref.shape[1]
+    force_ref[...] = before_ref[...]
+    sent_ref[...] = jnp.zeros_like(sent_ref)
+
+    @pl.when(is_lower(start_ref, atoms))
+    def run():
+        above(
+            atoms // 2, start_ref, (first_ref, second_ref), occup_ref, energies_ref, nbr_ref, deriv_ref, slot_ref,
+            own_high_ref, own_low_ref, force_ref, sent_ref, *scratch,
+        )
+
+
+def far_kernel(
     start_ref, payload_ref, before_ref, occup_ref, energies_ref, nbr_ref, deriv_ref, slot_ref,
-    own_high_ref, own_low_ref, near_high_ref, near_low_ref,
-    force_ref, sent_ref,
+    own_high_ref, own_low_ref, near_high_ref, near_low_ref, force_ref, sent_ref,
     cut_high_ref, cut_low_ref, gram_ref, index_ref, spread_ref,
 ):
     atoms = nbr_ref.shape[1]
@@ -303,54 +387,16 @@
     lower = atoms // 2 - UPPER
     force_ref[...] = before_ref[...]
     sent_ref[...] = jnp.zeros_like(sent_ref)
-    first = ((start_ref[0] // atoms) & 1) == parity
-
-    @pl.when(first)
-    def above():
-        occup = occup_ref[...]
-        weights = [occup, occup * energies_ref[...]]
-        extra = lower - BLOCK
-        for c in range(count):
-            lanes = slice(c * LANES, (c + 1) * LANES)
-            for b in range(4):
-                rows = payload_ref[c, pl.ds(b, BLOCK, stride=4), :]
-                for x in range(2):
-                    at = slice((x * 4 + b) * BLOCK, (x * 4 + b + 1) * BLOCK)
-                    cut_high_ref[at, lanes], cut_low_ref[at, lanes] = split(rows * weights[x][:, lanes])
-                rows = payload_ref[c, pl.ds(4 * BLOCK + b, extra, stride=4), :]
-                for x in range(2):
-                    at = slice(512 + (x * 4 + b) * extra, 512 + (x * 4 + b + 1) * extra)
-                    cut_high_ref[at, lanes], cut_low_ref[at, lanes] = split(rows * weights[x][:, lanes])
-        gram_ref[:512, :] = gram(
-            cut_high_ref[:512, :], cut_low_ref[:512, :], own_high_ref[512:, :], own_low_ref[512:, :]
-        )
-        gram_ref[512:, 256:] = gram(
-            cut_high_ref[512:, :], cut_low_ref[512:, :], own_high_ref[768:, :], own_low_ref[768:, :]
-        )
-        index_ref[...] = nbr_ref[:, LANES:] - (start_ref[0] + atoms)
-        near_tile = tiles(gram_ref, 256, BLOCK)
-        extra_tile = tiles(gram_ref.at[512:, :], 256, extra)
-
-        def odd_tile(r, *key):
-            return near_tile(r, *key) if r < BLOCK // 8 else extra_tile(r - BLOCK // 8, *key)
-
-        pairs = [
-            pick_pairs(
-                (tiles(gram_ref, 0, BLOCK), odd_tile)[h],
-                (BLOCK, lower)[h] // 8,
-                block_index(index_ref, h),
-                lambda *key: deriv_ref[2 + h, deriv_at(*key)],
-            )
-            for h in range(2)
-        ]
-        pair = merge(fold(pairs[0]), fold(pairs[1]))
-        mine = slot_sum(pair)
-        theirs = spread(lambda r: slot_ref[48 + r], pair, spread_ref, lower)
-        for k in range(3):
-            force_ref[k : k + 1, LANES:] += -2.0 * mine[k]
-            sent_ref[k : k + 1, :lower] = 2.0 * theirs[k]
-
-    @pl.when(jnp.logical_not(first))
+
+    @pl.when(jnp.logical_not(is_lower(start_ref, atoms)))
+    def run():
+        above(
+            lower, start_ref, (payload_ref,), occup_ref, energies_ref, nbr_ref, deriv_ref, slot_ref,
+            own_high_ref, own_low_ref, force_ref, sent_ref,
+            cut_high_ref, cut_low_ref, gram_ref, index_ref, spread_ref,
+        )
+
+    @pl.when(is_lower(start_ref, atoms))
     def below():
         skip = BLOCK - UPPER
         for c in range(count):
@@ -388,8 +434,12 @@
     return pltpu.with_memory_space_constraint(value, pltpu.HBM)
 
 
-def core_swap(value):
-    return lax.ppermute(value, "sub", [(0, 1), (1, 0)])
+def core_down(value):
+    return lax.ppermute(value, "sub", [(1, 0)])
+
+
+def core_up(value):
+    return lax.ppermute(value, "sub", [(0, 1)])
 
 
 def shard_swap(value):
@@ -413,32 +463,40 @@
     whole = jax.ShapeDtypeStruct((4 * atoms, states), jnp.bfloat16)
     force = jax.ShapeDtypeStruct((8, atoms), jnp.float32)
     prepared = pltpu.VMEM((512, states), jnp.bfloat16)
-    lower = atoms // 2 - UPPER
-    payload = jax.ShapeDtypeStruct((count, payload_rows(atoms, states), LANES), jnp.float32)
-    core_payload, far_payload = pl.pallas_call(
-        pack_kernel,
-        out_shape=(payload, payload),
+    coeffs, nbr_hbm, dham_hbm, dovl_hbm = (in_hbm(value) for value in (coeffs, nbr, dham, dovl))
+    far_payload = pl.pallas_call(
+        far_pack_kernel,
+        out_shape=jax.ShapeDtypeStruct((count, payload_rows(atoms, states), LANES), jnp.float32),
         in_specs=[smem] + [hbm] * 4,
-        out_specs=(vmem, vmem),
+        out_specs=vmem,
         scratch_shapes=[
             pltpu.VMEM((48, slots, LANES), jnp.float32),
             pltpu.VMEM((48, slots, LANES), jnp.float32),
             pltpu.VMEM((slots, LANES), jnp.int32),
             pltpu.SemaphoreType.DMA((count,)),
-            pltpu.SemaphoreType.DMA((count,)),
             pltpu.SemaphoreType.DMA((3,)),
         ],
         compiler_params=pltpu.CompilerParams(vmem_limit_bytes=12 * 1024 * 1024),
-        name="pack",
-    )(start, *(in_hbm(value) for value in (coeffs, nbr, dham, dovl)))
+        name="far_pack",
+    )(start, coeffs, nbr_hbm, dham_hbm, dovl_hbm)
+    core_half = jax.ShapeDtypeStruct((count, atoms, LANES), jnp.float32)
+    core_payload = pl.pallas_call(
+        core_pack_kernel,
+        out_shape=(core_half, core_half),
+        in_specs=[smem, hbm, pl.BlockSpec(memory_space=pl.ANY)],
+        out_specs=(vmem, vmem),
+        scratch_shapes=[pltpu.SemaphoreType.DMA((2 * count,))],
+        compiler_params=pltpu.CompilerParams(vmem_limit_bytes=12 * 1024 * 1024),
+        name="core_pack",
+    )(start, coeffs, far_payload)
     far_payload = shard_swap(far_payload)
-    core_payload = core_swap(core_payload)
+    core_payload = [core_down(half) for half in core_payload]
     own_high, own_low, near_high, near_low, inner, derivs, slot_maps = pl.pallas_call(
         inner_kernel,
         out_shape=(
             whole, whole, half, half, force,
             jax.ShapeDtypeStruct((4, 96, 8, LANES), jnp.float32),
-            jax.ShapeDtypeStruct((64 - UPPER // 8, 8, LANES), jnp.int32),
+            jax.ShapeDtypeStruct((64, 8, LANES), jnp.int32),
         ),
         in_specs=[smem, hbm] + [vmem] * 5,
         out_specs=(vmem,) * 7,
@@ -455,32 +513,35 @@
             flops=3 * 2 * 9 * 512 * 256 * states, bytes_accessed=16 * 1024 * 1024, transcendentals=0
         ),
         name="inner_pairs",
-    )(start, in_hbm(coeffs), occup, energies, nbr, dham, dovl)
-
-    def cross(parity, payload, before, name):
-        cut = pltpu.VMEM((8 * lower, states), jnp.bfloat16)
+    )(start, coeffs, occup, energies, nbr, dham, dovl)
+
+    def cross(kernel, rows, flops, name, *operands):
+        cut = pltpu.VMEM((8 * rows, states), jnp.bfloat16)
         return pl.pallas_call(
-            functools.partial(cross_kernel, parity),
+            kernel,
             out_shape=(force, force),
-            in_specs=[smem] + [vmem] * 11,
+            in_specs=[smem] + [vmem] * len(operands),
             out_specs=(vmem, vmem),
             scratch_shapes=[
                 cut,
                 cut,
-                pltpu.VMEM((8 * lower, 512), jnp.float32),
+                pltpu.VMEM((8 * rows, 512), jnp.float32),
                 pltpu.VMEM((slots, LANES), jnp.int32),
-                pltpu.VMEM((3, lower, LANES), jnp.float32),
+                pltpu.VMEM((3, rows, LANES), jnp.float32),
             ],
             compiler_params=pltpu.CompilerParams(vmem_limit_bytes=20 * 1024 * 1024),
             cost_estimate=pl.CostEstimate(
-                flops=3 * 2 * 2 * 512 * 256 * states, bytes_accessed=6 * 1024 * 1024, transcendentals=0
+                flops=flops, bytes_accessed=0, transcendentals=0
             ),
             name=name,
-        )(start, payload, before, occup, energies, nbr, derivs, slot_maps, own_high, own_low, near_high, near_low)
-
-    total, core_sent = cross(0, core_payload, inner, "core_pairs")
-    core_back = core_swap(core_sent)
-    total, far_sent = cross(1, far_payload, total, "far_pairs")
+        )(start, *operands)
+
+    shared = (occup, energies, nbr, derivs, slot_maps, own_high, own_low)
+    total, core_sent = cross(core_kernel, atoms // 2, 0, "core_pairs", *core_payload, inner, *shared)
+    core_back = core_up(core_sent)
+    total, far_sent = cross(
+        far_kernel, atoms // 2 - UPPER, 3 * 2 * 2 * 512 * 256 * states, "far_pairs", far_payload, total, *shared, near_high, near_low
+    )
     total = (total + core_back + shard_swap(far_sent))[:3]
     if lax.axis_size("states") == 2:
         return total + lax.ppermute(total, "states", [(0, 1), (1, 0)])

time: 33.9 us -> 37 us (1.091)
  starting transfers between devices: 8.1 us -> 13 us
  waiting for transfers between devices: 4.01 us -> 2.96 us
  Pallas kernels: 20.9 us -> 20 us
    ppermute x2 -> x3, starting transfers between devices: 0.18 us -> 4 us  [the longest x2 2.71 us: core_down(): return lax.ppermute(value, 'sub', [(1, 0)])]
    ppermute x2, waiting for transfers between devices: 2.95 us -> 1.71 us  [shard_swap(): return lax.ppermute(value, SHARD, pairs)]
    ppermute x2, starting transfers between devices: 6.52 us -> 7.75 us  [shard_swap(): return lax.ppermute(value, SHARD, pairs)]
    pallas_call x3 -> x4, Pallas kernels: 7.43 us -> 6.53 us  [the longest x2 3.03 us: cross(): pl.pallas_call(kernel, out_shape=(force, force), in_specs=[smem] + [vmem]...]
  transfers between devices with their start and end apart: 5 -> 6, of which waited for: 2 -> 2; matrix products, arithmetic and copies ran while one was open for 0% -> 0% of each run, Pallas kernels for 46% -> 50%
where the time goes in v8:
time: 37 us; the launch traced here: 36.8 us
  Pallas kernels  20 us (54%)
  starting transfers between devices  13 us (35%)
  waiting for transfers between devices  2.96 us (8%)
  other arithmetic  0.6 us (2%)
    pallas_call x1, Pallas kernels, local(): pl.pallas_call(inner_kernel, out_shape=(whole, whole, half, half, force,...  13.5 us
    ppermute x2, starting transfers between devices, shard_swap(): return lax.ppermute(value, SHARD, pairs)  7.75 us
    pallas_call x2, Pallas kernels, cross(): pl.pallas_call(kernel, out_shape=(force, force), in_specs=[smem] + [vmem]...  3.03 us
    ppermute x2, starting transfers between devices, core_down(): return lax.ppermute(value, 'sub', [(1, 0)])  2.71 us
    pallas_call x1, Pallas kernels, local(): pl.pallas_call(core_pack_kernel, out_shape=(core_half, core_half), in_spe...  1.78 us
    pallas_call x1, Pallas kernels, local(): pl.pallas_call(far_pack_kernel, out_shape=jax.ShapeDtypeStruct((count, pa...  1.73 us
    ppermute x2, waiting for transfers between devices, shard_swap(): return lax.ppermute(value, SHARD, pairs)  1.71 us
    ppermute x1, starting transfers between devices, core_up(): return lax.ppermute(value, 'sub', [(0, 1)])  1.29 us
  transfers between devices with their start and end apart: 6, of which 2 were waited for; matrix products, arithmetic and copies ran while one was open for 0% of the time, Pallas kernels for 50%

profile of v8, /device:TPU:1, one launch (start us, length us, event | category | flops | bytes accessed | tf_op | source)
XLA Modules:
  0.0 36.8 jit_solution(486575677320422618)
XLA Ops:
  0.0 1.7 %far_pack.1.far_ref = f32[8,320,128]{2,1,0:T(8,128)S(1)} custom-call(s32[1]{0:T(128)} %bitcast.start_ref, f32[1024,1024]{1,0:T(8,128)} %coeffs_ref.5, s32[16,256]{1,0:T(8,128)} %nbr_ref.7, f32[48,16,256]{2,1,0:T(8,128)} %dham_ref.3, f32[48,16,256]{2,1,0:T(8,128)} %dovl_ref.3), custom_call_target="tpu_custom_call" | custom-call | tf_op jit(solution)/shard_map/far_pack/pallas_call | solution.py:467
  1.7 0.0 copy-start
  1.7 0.0 copy-start.1
  1.8 0.0 copy-start.2
  1.8 0.0 copy-start.3
  1.8 0.0 copy-start.4
  1.8 4.5 %collective-permute-start = (f32[8,320,128]{2,1,0:T(8,128)S(1)}, f32[8,320,128]{2,1,0:T(8,128)S(1)}, u32[]{:S(2)}, u32[]{:S(2)}) collective-permute-start(f32[8,320,128]{2,1,0:T(8,128)S(1)} %far_pack.1.far_ref), channel_id=1, source_target_pairs={{1,4},{4,1},{5,8},{8,5},{9,12},{12,9},{3,6},{6,3},{7,10},{10,7},{1... | collective-permute-start | bytes 3932168 | tf_op jit(solution)/shard_map/ppermute | solution.py:448
  6.3 1.8 %core_pack.1 = (f32[8,256,128]{2,1,0:T(8,128)S(1)}, f32[8,256,128]{2,1,0:T(8,128)S(1)}) custom-call(s32[1]{0:T(128)} %bitcast.start_ref, f32[1024,1024]{1,0:T(8,128)} %coeffs_ref.5, f32[8,320,128]{2,1,0:T(8,128)S(1)} %far_pack.1.far_ref), custom_call_target="tpu_custom_call" | custom-call | tf_op jit(solution)/shard_map/core_pack/pallas_call | solution.py:483
  8.1 1.4 %collective-permute-start.1 = (f32[8,256,128]{2,1,0:T(8,128)S(1)}, f32[8,256,128]{2,1,0:T(8,128)S(1)}, u32[]{:S(2)}, u32[]{:S(2)}) collective-permute-start(f32[8,256,128]{2,1,0:T(8,128)S(1)} %get-tuple-element.18), channel_id=1, source_target_pairs={{1,0},{3,2},{5,4},{7,6},{9,8},{11,10},{13,12},{15,14},{17,16},{19,... | collective-permute-start | bytes 3145736 | tf_op jit(solution)/shard_map/ppermute | solution.py:438
  9.5 1.4 %collective-permute-start.2 = (f32[8,256,128]{2,1,0:T(8,128)S(1)}, f32[8,256,128]{2,1,0:T(8,128)S(1)}, u32[]{:S(2)}, u32[]{:S(2)}) collective-permute-start(f32[8,256,128]{2,1,0:T(8,128)S(1)} %get-tuple-element.19), channel_id=1, source_target_pairs={{1,0},{3,2},{5,4},{7,6},{9,8},{11,10},{13,12},{15,14},{17,16},{19,... | collective-permute-start | bytes 3145736 | tf_op jit(solution)/shard_map/ppermute | solution.py:438
  10.8 0.0 copy-done
  10.8 0.0 copy-done.1
  10.8 0.0 copy-done.2
  10.8 0.0 copy-done.3
  10.9 0.0 copy-done.4
  10.9 13.5 %inner_pairs.1 = (bf16[1024,1024]{1,0:T(8,128)(2,1)S(1)}, bf16[1024,1024]{1,0:T(8,128)(2,1)S(1)}, bf16[512,1024]{1,0:T(8,128)(2,1)S(1)}, bf16[512,1024]{1,0:T(8,...) custom-call(s32[1]{0:T(128)} %bitcast.start_ref, ...), custom_call_target="tpu_custom_call" | custom-call | flops 7247757312 | bytes 16777216 | tf_op jit(solution)/shard_map/inner_pairs/pallas_call | solution.py:494
  24.4 0.0 collective-permute-done.1.first_ref
  24.4 0.0 collective-permute-done.2.second_ref
  24.4 0.2 core_pairs.1
  24.6 1.3 %collective-permute-start.3 = (f32[8,256]{1,0:T(8,128)S(1)}, f32[8,256]{1,0:T(8,128)S(1)}, u32[]{:S(2)}, u32[]{:S(2)}) collective-permute-start(f32[8,256]{1,0:T(8,128)S(1)} %get-tuple-element.29), channel_id=1, source_target_pairs={{0,1},{2,3},{4,5},{6,7},{8,9},{10,11},{12,13},{14,15},{16,17},{18,... | collective-permute-start | bytes 24584 | tf_op jit(solution)/shard_map/ppermute | solution.py:442
  25.9 0.0 collective-permute-done.payload_ref
  25.9 2.8 %far_pairs.1 = (f32[8,256]{1,0:T(8,128)S(1)}, f32[8,256]{1,0:T(8,128)S(1)}) custom-call(s32[1]{0:T(128)} %bitcast.start_ref, f32[8,320,128]{2,1,0:T(8,128)S(1)} %collective-permute-done.payload_ref, f32[8,256]{1,0:T(8,128)S(1)} %get-tuple-element.25.before_ref, f32[1,1024]{1,0:T(1,128)S(1)} %bitcast.5, f32[1,1024]{1,0:T(1,128)S(1)} %bitcast.8, ...), custom_call_target="tpu_custom_call" | custom-call | flops 1610612736 | tf_op jit(solution)/shard_map/far_pairs/pallas_call | solution.py:520
  28.7 3.3 %collective-permute-start.4 = (f32[8,256]{1,0:T(8,128)S(1)}, f32[8,256]{1,0:T(8,128)S(1)}, u32[]{:S(2)}, u32[]{:S(2)}) collective-permute-start(f32[8,256]{1,0:T(8,128)S(1)} %get-tuple-element.30), channel_id=1, source_target_pairs={{1,4},{4,1},{5,8},{8,5},{9,12},{12,9},{3,6},{6,3},{7,10},{10,7},{1... | collective-permute-start | bytes 24584 | tf_op jit(solution)/shard_map/ppermute | solution.py:448
  32.0 0.0 collective-permute-done.3
  32.0 1.7 %collective-permute-done.4 = f32[8,256]{1,0:T(8,128)S(1)} collective-permute-done((f32[8,256]{1,0:T(8,128)S(1)}, f32[8,256]{1,0:T(8,128)S(1)}, u32[]{:S(2)}, u32[]{:S(2)}) %collective-permute-start.4) | collective-permute-done | bytes 8224 | tf_op jit(solution)/shard_map/ppermute | solution.py:448
  33.7 1.2 %collective-permute-start.5 = (f32[3,256]{1,0:T(4,128)S(1)}, f32[3,256]{1,0:T(4,128)S(1)}, u32[]{:S(2)}, u32[]{:S(2)}) collective-permute-start(f32[3,256]{1,0:T(4,128)S(1)} %slice_add_fusion), channel_id=1, source_target_pairs={{0,2},{2,0},{1,3},{3,1},{4,6},{6,4},{5,7},{7,5},{8,10},{10,8},{9,1... | collective-permute-start | bytes 9224 | tf_op jit(solution)/shard_map/ppermute | solution.py:547
  34.9 1.2 %collective-permute-done.5 = f32[3,256]{1,0:T(4,128)S(1)} collective-permute-done((f32[3,256]{1,0:T(4,128)S(1)}, f32[3,256]{1,0:T(4,128)S(1)}, u32[]{:S(2)}, u32[]{:S(2)}) %collective-permute-start.5) | collective-permute-done | bytes 3104 | tf_op jit(solution)/shard_map/ppermute | solution.py:547
  36.2 0.6 %add.15 = f32[3,256]{1,0:T(4,128)} add(f32[3,256]{1,0:T(4,128)S(1)} %slice_add_fusion, f32[3,256]{1,0:T(4,128)S(1)} %collective-permute-done.5) | non-fusion elementwise | flops 768 | bytes 9216 | tf_op jit(solution)/shard_map/add | solution.py:547
  (1 shorter events, 0.0 us)
Async XLA Ops:
  1.7 9.1 %copy-start = (f32[48,16,256]{2,1,0:T(8,128)S(1)}, f32[48,16,256]{2,1,0:T(8,128)}, u32[]{:S(2)}) copy-start(f32[48,16,256]{2,1,0:T(8,128)} %dham_ref.3) | copy-start | bytes 2359300
  1.7 9.1 %copy-start.1 = (f32[48,16,256]{2,1,0:T(8,128)S(1)}, f32[48,16,256]{2,1,0:T(8,128)}, u32[]{:S(2)}) copy-start(f32[48,16,256]{2,1,0:T(8,128)} %dovl_ref.3) | copy-start | bytes 2359300
  1.8 9.1 %copy-start.2 = (s32[16,256]{1,0:T(8,128)S(1)}, s32[16,256]{1,0:T(8,128)}, u32[]{:S(2)}) copy-start(s32[16,256]{1,0:T(8,128)} %nbr_ref.7) | copy-start | bytes 49156
  1.8 9.1 %copy-start.3 = (f32[1024]{0:T(1024)S(1)}, f32[1024]{0:T(1024)}, u32[]{:S(2)}) copy-start(f32[1024]{0:T(1024)} %param.7) | copy-start | bytes 12292
  1.8 9.1 %copy-start.4 = (f32[1024]{0:T(1024)S(1)}, f32[1024]{0:T(1024)}, u32[]{:S(2)}) copy-start(f32[1024]{0:T(1024)} %param.8) | copy-start | bytes 12292
  1.8 24.1 %collective-permute-start = (f32[8,320,128]{2,1,0:T(8,128)S(1)}, f32[8,320,128]{2,1,0:T(8,128)S(1)}, u32[]{:S(2)}, u32[]{:S(2)}) collective-permute-start(f32[8,320,128]{2,1,0:T(8,128)S(1)} %far_pack.1.far_ref), channel_id=1, source_target_pairs={{1,4},{4,1},{5,8},{8,5},{9,12},{12,9},{3,6},{6,3},{7,10},{10,7},{1... | collective-permute-start | bytes 3932168 | tf_op jit(solution)/shard_map/ppermute | solution.py:448
  8.1 16.3 %collective-permute-start.1 = (f32[8,256,128]{2,1,0:T(8,128)S(1)}, f32[8,256,128]{2,1,0:T(8,128)S(1)}, u32[]{:S(2)}, u32[]{:S(2)}) collective-permute-start(f32[8,256,128]{2,1,0:T(8,128)S(1)} %get-tuple-element.18), channel_id=1, source_target_pairs={{1,0},{3,2},{5,4},{7,6},{9,8},{11,10},{13,12},{15,14},{17,16},{19,... | collective-permute-start | bytes 3145736 | tf_op jit(solution)/shard_map/ppermute | solution.py:438
  9.5 14.9 %collective-permute-start.2 = (f32[8,256,128]{2,1,0:T(8,128)S(1)}, f32[8,256,128]{2,1,0:T(8,128)S(1)}, u32[]{:S(2)}, u32[]{:S(2)}) collective-permute-start(f32[8,256,128]{2,1,0:T(8,128)S(1)} %get-tuple-element.19), channel_id=1, source_target_pairs={{1,0},{3,2},{5,4},{7,6},{9,8},{11,10},{13,12},{15,14},{17,16},{19,... | collective-permute-start | bytes 3145736 | tf_op jit(solution)/shard_map/ppermute | solution.py:438
  24.6 7.4 %collective-permute-start.3 = (f32[8,256]{1,0:T(8,128)S(1)}, f32[8,256]{1,0:T(8,128)S(1)}, u32[]{:S(2)}, u32[]{:S(2)}) collective-permute-start(f32[8,256]{1,0:T(8,128)S(1)} %get-tuple-element.29), channel_id=1, source_target_pairs={{0,1},{2,3},{4,5},{6,7},{8,9},{10,11},{12,13},{14,15},{16,17},{18,... | collective-permute-start | bytes 24584 | tf_op jit(solution)/shard_map/ppermute | solution.py:442
  28.7 5.0 %collective-permute-start.4 = (f32[8,256]{1,0:T(8,128)S(1)}, f32[8,256]{1,0:T(8,128)S(1)}, u32[]{:S(2)}, u32[]{:S(2)}) collective-permute-start(f32[8,256]{1,0:T(8,128)S(1)} %get-tuple-element.30), channel_id=1, source_target_pairs={{1,4},{4,1},{5,8},{8,5},{9,12},{12,9},{3,6},{6,3},{7,10},{10,7},{1... | collective-permute-start | bytes 24584 | tf_op jit(solution)/shard_map/ppermute | solution.py:448
  33.7 2.5 %collective-permute-start.5 = (f32[3,256]{1,0:T(4,128)S(1)}, f32[3,256]{1,0:T(4,128)S(1)}, u32[]{:S(2)}, u32[]{:S(2)}) collective-permute-start(f32[3,256]{1,0:T(4,128)S(1)} %slice_add_fusion), channel_id=1, source_target_pairs={{0,2},{2,0},{1,3},{3,1},{4,6},{6,4},{5,7},{7,5},{8,10},{10,8},{9,1... | collective-permute-start | bytes 9224 | tf_op jit(solution)/shard_map/ppermute | solution.py:547

commit v9 on v7

--- a/solution.py
+++ b/solution.py
@@ -9,7 +9,7 @@
 
 LANES = 128
 BLOCK = 64
-UPPER = 48
+UPPER = 52
 SHARD = ("atoms", "sub")
 
 
@@ -90,13 +90,13 @@
     return [jnp.sum(pair[k][0] + pair[k][1], axis=0, keepdims=True) for k in range(3)]
 
 
-def slot_map(index_ref, r):
-    target = lax.broadcasted_iota(jnp.int32, (8, LANES), 0) + 8 * r
+def slot_map(index_ref, base, first=0):
+    target = lax.broadcasted_iota(jnp.int32, (8, LANES), 0) + base
     slot = jnp.full((8, LANES), 16, jnp.int32)
     for n in range(16):
         hit = jnp.broadcast_to(index_ref[n : n + 1, :], (8, LANES)) == target
         slot = jnp.where(hit, n, slot)
-    return slot
+    return jnp.where(target < first, 16, slot) if first else slot
 
 
 def spread(slot, pair, spread_ref, rows):
@@ -175,9 +175,11 @@
                             at = deriv_at(k, x, b, g, half)
                             deriv_ref[h, at] = side_by_side(parts[0], parts[1], h % 2)
     for r in range(32):
-        slot_ref[r] = slot_map(index_ref.at[0], r)
-    for r in range(32 - UPPER // 8):
-        slot_ref[32 + r] = slot_map(index_ref.at[1], r)
+        slot_ref[r] = slot_map(index_ref.at[0], 8 * r)
+    lower = LANES - UPPER
+    for r in range(16 + lower // 8):
+        slot_ref[32 + r] = slot_map(index_ref.at[1], 8 * r)
+    slot_ref[48 + lower // 8] = slot_map(index_ref.at[1], LANES + lower - 8, LANES + lower // 8 * 8)
     for c, copy in enumerate(copies):
         copy.wait()
         lanes = slice(c * LANES, (c + 1) * LANES)
@@ -225,8 +227,13 @@
 
 
 def payload_rows(atoms, states):
-    planes = -(-48 // (states // LANES))
-    return max(4 * (atoms // 2 - UPPER), 4 * UPPER + 16 * planes + 16)
+    groups = -(-48 // (states // LANES))
+    return max(4 * (atoms // 2 - UPPER), 4 * BLOCK + 16 * (groups - 3))
+
+
+def plane_row(plane, count):
+    group = plane // count
+    return 16 * group if group < 3 else 4 * BLOCK + 16 * (group - 3)
 
 
 def pack_kernel(
@@ -247,26 +254,33 @@
 
     def fill(up_ref, up_sem, down_ref, down_sem):
         copies = []
+        skip = 4 * (BLOCK - UPPER)
         for c in range(count):
             lanes = slice(c * LANES, (c + 1) * LANES)
             up_rows = coeffs_ref.at[4 * (atoms - UPPER) :, lanes]
-            copies.append(pltpu.make_async_copy(up_rows, up_ref.at[c, : 4 * UPPER, :], up_sem.at[c]))
+            copies.append(pltpu.make_async_copy(up_rows, up_ref.at[c, skip : 4 * BLOCK, :], up_sem.at[c]))
             down_rows = coeffs_ref.at[:lower, lanes]
             copies.append(pltpu.make_async_copy(down_rows, down_ref.at[c, :lower, :], down_sem.at[c]))
         for copy in fetched + copies:
             copy.start()
         if rows > lower:
             down_ref[:, lower:, :] = jnp.zeros((count, rows - lower, LANES), jnp.float32)
-        up_ref[:, 4 * UPPER :, :] = jnp.zeros((count, rows - 4 * UPPER, LANES), jnp.float32)
-        planes = -(-48 // count)
+        for plane in range(48, -(-48 // count) * count):
+            up_ref[plane % count, plane_row(plane, count) : plane_row(plane, count) + 16, :] = jnp.zeros(
+                (16, LANES), jnp.float32
+            )
         for copy in fetched:
             copy.wait()
         last = last_ref[...]
         target = jnp.where(last >= 0, last - (start_ref[0] + atoms), -1).astype(jnp.float32)
-        at = 4 * UPPER + 16 * planes
-        for half in range(2):
-            part = target[8 * half : 8 * half + 8]
-            up_ref[0, at + 8 * half : at + 8 * half + 8, :] = side_by_side(part, part, 1)
+        free = BLOCK - UPPER
+        pieces = [
+            [
+                pltpu.roll(target[8 * half : 8 * half + 8], LANES - BLOCK - (piece + 1) * free, 1)
+                for half in range(2)
+            ]
+            for piece in range(-(-UPPER // free))
+        ]
         for x, ref in enumerate((ham_ref, ovl_ref)):
             for k in range(3):
                 for g in range(2):
@@ -277,8 +291,11 @@
                                 ref[k * 16 + (2 * g + parity) * 4 + b, 8 * half : 8 * half + 8, :]
                                 for parity in range(2)
                             ]
-                            at = 4 * UPPER + 16 * (plane // count) + 8 * half
-                            up_ref[plane % count, at : at + 8, :] = side_by_side(parts[0], parts[1], 1)
+                            both = side_by_side(parts[0], parts[1], 1)
+                            if plane < len(pieces):
+                                both = jnp.where(lane_numbers() < free, pieces[plane][half], both)
+                            at = plane_row(plane, count) + 8 * half
+                            up_ref[plane % count, at : at + 8, :] = both
         for copy in copies:
             copy.wait()
 
@@ -309,35 +326,30 @@
     def above():
         occup = occup_ref[...]
         weights = [occup, occup * energies_ref[...]]
-        extra = lower - BLOCK
+        size = cut_high_ref.shape[0] // 8
+        even = lower // 8 * 8
         for c in range(count):
             lanes = slice(c * LANES, (c + 1) * LANES)
             for b in range(4):
-                rows = payload_ref[c, pl.ds(b, BLOCK, stride=4), :]
+                rows = jnp.concatenate(
+                    [
+                        payload_ref[c, pl.ds(b, even, stride=4), :],
+                        payload_ref[c, pl.ds(4 * (lower - 8) + b, 8, stride=4), :],
+                    ],
+                    0,
+                )
                 for x in range(2):
-                    at = slice((x * 4 + b) * BLOCK, (x * 4 + b + 1) * BLOCK)
+                    at = slice((x * 4 + b) * size, (x * 4 + b + 1) * size)
                     cut_high_ref[at, lanes], cut_low_ref[at, lanes] = split(rows * weights[x][:, lanes])
-                rows = payload_ref[c, pl.ds(4 * BLOCK + b, extra, stride=4), :]
-                for x in range(2):
-                    at = slice(512 + (x * 4 + b) * extra, 512 + (x * 4 + b + 1) * extra)
-                    cut_high_ref[at, lanes], cut_low_ref[at, lanes] = split(rows * weights[x][:, lanes])
-        gram_ref[:512, :] = gram(
-            cut_high_ref[:512, :], cut_low_ref[:512, :], own_high_ref[512:, :], own_low_ref[512:, :]
+        gram_ref[...] = gram(
+            cut_high_ref[...], cut_low_ref[...], own_high_ref[512:, :], own_low_ref[512:, :]
         )
-        gram_ref[512:, 256:] = gram(
-            cut_high_ref[512:, :], cut_low_ref[512:, :], own_high_ref[768:, :], own_low_ref[768:, :]
-        )
-        index_ref[...] = nbr_ref[:, LANES:] - (start_ref[0] + atoms)
-        near_tile = tiles(gram_ref, 256, BLOCK)
-        extra_tile = tiles(gram_ref.at[512:, :], 256, extra)
-
-        def odd_tile(r, *key):
-            return near_tile(r, *key) if r < BLOCK // 8 else extra_tile(r - BLOCK // 8, *key)
-
+        target = nbr_ref[:, LANES:] - (start_ref[0] + atoms)
+        index_ref[...] = jnp.where(target >= even, target + (size - lower), target)
         pairs = [
             pick_pairs(
-                (tiles(gram_ref, 0, BLOCK), odd_tile)[h],
-                (BLOCK, lower)[h] // 8,
+                tiles(gram_ref, 256 * h, size),
+                (BLOCK, size)[h] // 8,
                 block_index(index_ref, h),
                 lambda *key: deriv_ref[2 + h, deriv_at(*key)],
             )
@@ -345,39 +357,44 @@
         ]
         pair = merge(fold(pairs[0]), fold(pairs[1]))
         mine = slot_sum(pair)
-        theirs = spread(lambda r: slot_ref[48 + r], pair, spread_ref, lower)
+        theirs = spread(lambda r: slot_ref[48 + r], pair, spread_ref, size)
         for k in range(3):
             force_ref[k : k + 1, LANES:] += -2.0 * mine[k]
-            sent_ref[k : k + 1, :lower] = 2.0 * theirs[k]
+            sent_ref[k : k + 1, :even] = 2.0 * theirs[k][:, :even]
+            sent_ref[k : k + 1, lower - 8 : lower] += 2.0 * theirs[k][:, even:]
 
     @pl.when(jnp.logical_not(first))
     def below():
-        skip = BLOCK - UPPER
         for c in range(count):
             lanes = slice(c * LANES, (c + 1) * LANES)
             for a in range(4):
-                rows = payload_ref[c, pl.ds(a, UPPER, stride=4), :]
-                at = slice(a * BLOCK + skip, (a + 1) * BLOCK)
-                cut_high_ref[at, lanes], cut_low_ref[at, lanes] = split(rows)
-                at = slice(a * BLOCK, a * BLOCK + skip)
-                cut_high_ref[at, lanes] = jnp.zeros((skip, LANES), jnp.bfloat16)
-                cut_low_ref[at, lanes] = jnp.zeros((skip, LANES), jnp.bfloat16)
+                at = slice(a * BLOCK, (a + 1) * BLOCK)
+                cut_high_ref[at, lanes], cut_low_ref[at, lanes] = split(
+                    payload_ref[c, pl.ds(a, BLOCK, stride=4), :]
+                )
         gram_ref[:512, :256] = gram(
             near_high_ref[...], near_low_ref[...], cut_high_ref[:256, :], cut_low_ref[:256, :]
         )
-        planes = -(-48 // count)
-        at = 4 * UPPER + 16 * planes
-        target = payload_ref[0, at : at + 16, :].astype(jnp.int32)
-        index_ref[...] = jnp.where(target >= lower, target - BLOCK, -1)
+        free = BLOCK - UPPER
+        lane = lane_numbers()
+        for half in range(2):
+            target = jnp.zeros((8, LANES), jnp.float32)
+            for piece in range(-(-UPPER // free)):
+                at = plane_row(piece, count) + 8 * half
+                first_lane = (piece + 1) * free
+                moved = pltpu.roll(payload_ref[piece % count, at : at + 8, :], first_lane, 1)
+                target = jnp.where((lane >= first_lane) & (lane < first_lane + free), moved, target)
+            target = side_by_side(target, target, 0).astype(jnp.int32)
+            index_ref[8 * half : 8 * half + 8, :] = jnp.where(target >= lower, target - BLOCK, -1)
         index = [index_ref[8 * half : 8 * half + 8, :] for half in range(2)]
 
         def deriv(k, x, b, g, half):
             plane = x * 24 + k * 8 + g * 4 + b
-            at = 4 * UPPER + 16 * (plane // count) + 8 * half
+            at = plane_row(plane, count) + 8 * half
             return payload_ref[plane % count, at : at + 8, :]
 
         pair = pick_pairs(tiles(gram_ref, 0, BLOCK), BLOCK // 8, index, deriv)
-        theirs = spread(functools.partial(slot_map, index_ref), pair, spread_ref, BLOCK)
+        theirs = spread(lambda r: slot_map(index_ref, 8 * r), pair, spread_ref, BLOCK)
         mine = slot_sum(fold(pair))
         for k in range(3):
             force_ref[k : k + 1, BLOCK:LANES] += 2.0 * theirs[k]
@@ -413,7 +430,7 @@
     whole = jax.ShapeDtypeStruct((4 * atoms, states), jnp.bfloat16)
     force = jax.ShapeDtypeStruct((8, atoms), jnp.float32)
     prepared = pltpu.VMEM((512, states), jnp.bfloat16)
-    lower = atoms // 2 - UPPER
+    padded = -(-(atoms // 2 - UPPER) // 16) * 16
     payload = jax.ShapeDtypeStruct((count, payload_rows(atoms, states), LANES), jnp.float32)
     core_payload, far_payload = pl.pallas_call(
         pack_kernel,
@@ -458,7 +475,7 @@
     )(start, in_hbm(coeffs), occup, energies, nbr, dham, dovl)
 
     def cross(parity, payload, before, name):
-        cut = pltpu.VMEM((8 * lower, states), jnp.bfloat16)
+        cut = pltpu.VMEM((8 * padded, states), jnp.bfloat16)
         return pl.pallas_call(
             functools.partial(cross_kernel, parity),
             out_shape=(force, force),
@@ -467,9 +484,9 @@
             scratch_shapes=[
                 cut,
                 cut,
-                pltpu.VMEM((8 * lower, 512), jnp.float32),
+                pltpu.VMEM((8 * padded, 512), jnp.float32),
                 pltpu.VMEM((slots, LANES), jnp.int32),
-                pltpu.VMEM((3, lower, LANES), jnp.float32),
+                pltpu.VMEM((3, padded, LANES), jnp.float32),
             ],
             compiler_params=pltpu.CompilerParams(vmem_limit_bytes=20 * 1024 * 1024),
             cost_estimate=pl.CostEstimate(

time: 33.9 us -> 33.7 us (level)
  no operation moved by 1% of the time
where the time goes in v9:
time: 33.7 us; the launch traced here: 33.5 us
  Pallas kernels  20.7 us (61%)
  starting transfers between devices  7.86 us (23%)
  waiting for transfers between devices  4.24 us (13%)
  other arithmetic  0.6 us (2%)
    pallas_call x1, Pallas kernels, local(): pl.pallas_call(inner_kernel, out_shape=(whole, whole, half, half, force,...  13.6 us
    ppermute x2, starting transfers between devices, shard_swap(): return lax.ppermute(value, SHARD, pairs)  6.49 us
    pallas_call x2, Pallas kernels, cross(): pl.pallas_call(functools.partial(cross_kernel, parity), out_shape=(force,...  4.88 us
    ppermute x2, waiting for transfers between devices, shard_swap(): return lax.ppermute(value, SHARD, pairs)  2.97 us
    pallas_call x1, Pallas kernels, local(): pl.pallas_call(pack_kernel, out_shape=(payload, payload), in_specs=[smem]...  2.21 us
    ppermute x1, waiting for transfers between devices, local(): return total + lax.ppermute(total, 'states', [(0, 1), (1, 0)])  1.27 us
    ppermute x1, starting transfers between devices, local(): return total + lax.ppermute(total, 'states', [(0, 1), (1, 0)])  1.19 us
  transfers between devices with their start and end apart: 5, of which 2 were waited for; matrix products, arithmetic and copies ran while one was open for 0% of the time, Pallas kernels for 46%

profile of v9, /device:TPU:1, one launch (start us, length us, event | category | flops | bytes accessed | tf_op | source)
XLA Modules:
  0.0 33.5 jit_solution(16665636861122718450)
XLA Ops:
  0.0 0.0 copy-start
  0.0 0.0 copy-start.1
  0.0 0.0 copy-start.2
  0.0 0.0 copy-start.3
  0.0 0.0 copy-start.4
  0.0 2.2 %pack.1 = (f32[8,304,128]{2,1,0:T(8,128)S(1)}, f32[8,304,128]{2,1,0:T(8,128)S(1)}) custom-call(s32[1]{0:T(128)} %bitcast.start_ref, f32[1024,1024]{1,0:T(8,128)} %coeffs_ref.3, s32[16,256]{1,0:T(8,128)} %nbr_ref.7, f32[48,16,256]{2,1,0:T(8,128)} %dham_ref.3, f32[48,16,256]{2,1,0:T(8,128)} %dovl_ref.3), custom_call_target="tpu_custom_call" | custom-call | tf_op jit(solution)/shard_map/pack/pallas_call | solution.py:435
  2.2 0.1 collective-permute-start.1
  2.4 4.6 %collective-permute-start = (f32[8,304,128]{2,1,0:T(8,128)S(1)}, f32[8,304,128]{2,1,0:T(8,128)S(1)}, u32[]{:S(2)}, u32[]{:S(2)}) collective-permute-start(f32[8,304,128]{2,1,0:T(8,128)S(1)} %get-tuple-element.18), channel_id=1, source_target_pairs={{1,4},{4,1},{5,8},{8,5},{9,12},{12,9},{3,6},{6,3},{7,10},{10,7},{1... | collective-permute-start | bytes 3735560 | tf_op jit(solution)/shard_map/ppermute | solution.py:415
  6.9 0.0 copy-done
  6.9 0.0 copy-done.1
  6.9 0.0 copy-done.2
  7.0 0.0 copy-done.3
  7.0 0.0 copy-done.4
  7.0 13.6 %inner_pairs.1 = (bf16[1024,1024]{1,0:T(8,128)(2,1)S(1)}, bf16[1024,1024]{1,0:T(8,128)(2,1)S(1)}, bf16[512,1024]{1,0:T(8,128)(2,1)S(1)}, bf16[512,1024]{1,0:T(8,...) custom-call(s32[1]{0:T(128)} %bitcast.start_ref, ...), custom_call_target="tpu_custom_call" | custom-call | flops 7247757312 | bytes 16777216 | tf_op jit(solution)/shard_map/inner_pairs/pallas_call | solution.py:453
  20.6 0.0 collective-permute-done.1.payload_ref
  20.6 2.0 %core_pairs.1 = (f32[8,256]{1,0:T(8,128)S(1)}, f32[8,256]{1,0:T(8,128)S(1)}) custom-call(s32[1]{0:T(128)} %bitcast.start_ref, f32[8,304,128]{2,1,0:T(8,128)S(1)} %collective-permute-done.1.payload_ref, f32[8,256]{1,0:T(8,128)S(1)} %get-tuple-element.20.before_ref, f32[1,1024]{1,0:T(1,128)S(1)} %bitcast.4, f32[1,1024]{1,0:T(1,128)S(1)} %bitcast.7, ...), custom_call_target="tpu_custom_call" | custom-call | flops 1610612736 | bytes 6291456 | tf_op jit(solution)/shard_map/core_pairs/pallas_call | solution.py:479
  22.5 0.0 collective-permute-done.payload_ref
  22.5 2.9 %far_pairs.1 = (f32[8,256]{1,0:T(8,128)S(1)}, f32[8,256]{1,0:T(8,128)S(1)}) custom-call(s32[1]{0:T(128)} %bitcast.start_ref, f32[8,304,128]{2,1,0:T(8,128)S(1)} %collective-permute-done.payload_ref, f32[8,256]{1,0:T(8,128)S(1)} %get-tuple-element.27.before_ref, f32[1,1024]{1,0:T(1,128)S(1)} %bitcast.5, f32[1,1024]{1,0:T(1,128)S(1)} %bitcast.8, ...), custom_call_target="tpu_custom_call" | custom-call | flops 1610612736 | bytes 6291456 | tf_op jit(solution)/shard_map/far_pairs/pallas_call | solution.py:479
  25.5 1.9 %collective-permute-start.3 = (f32[8,256]{1,0:T(8,128)S(1)}, f32[8,256]{1,0:T(8,128)S(1)}, u32[]{:S(2)}, u32[]{:S(2)}) collective-permute-start(f32[8,256]{1,0:T(8,128)S(1)} %get-tuple-element.30), channel_id=1, source_target_pairs={{1,4},{4,1},{5,8},{8,5},{9,12},{12,9},{3,6},{6,3},{7,10},{10,7},{1... | collective-permute-start | bytes 24584 | tf_op jit(solution)/shard_map/ppermute | solution.py:415
  27.4 0.1 collective-permute-start.2
  27.5 3.0 %collective-permute-done.3 = f32[8,256]{1,0:T(8,128)S(1)} collective-permute-done((f32[8,256]{1,0:T(8,128)S(1)}, f32[8,256]{1,0:T(8,128)S(1)}, u32[]{:S(2)}, u32[]{:S(2)}) %collective-permute-start.3) | collective-permute-done | bytes 8224 | tf_op jit(solution)/shard_map/ppermute | solution.py:415
  30.4 0.0 collective-permute-done.2
  30.4 1.2 %collective-permute-start.4 = (f32[3,256]{1,0:T(4,128)S(1)}, f32[3,256]{1,0:T(4,128)S(1)}, u32[]{:S(2)}, u32[]{:S(2)}) collective-permute-start(f32[3,256]{1,0:T(4,128)S(1)} %slice_add_fusion), channel_id=1, source_target_pairs={{0,2},{2,0},{1,3},{3,1},{4,6},{6,4},{5,7},{7,5},{8,10},{10,8},{9,1... | collective-permute-start | bytes 9224 | tf_op jit(solution)/shard_map/ppermute | solution.py:503
  31.6 1.3 %collective-permute-done.4 = f32[3,256]{1,0:T(4,128)S(1)} collective-permute-done((f32[3,256]{1,0:T(4,128)S(1)}, f32[3,256]{1,0:T(4,128)S(1)}, u32[]{:S(2)}, u32[]{:S(2)}) %collective-permute-start.4) | collective-permute-done | bytes 3104 | tf_op jit(solution)/shard_map/ppermute | solution.py:503
  32.9 0.6 %add.15 = f32[3,256]{1,0:T(4,128)} add(f32[3,256]{1,0:T(4,128)S(1)} %slice_add_fusion, f32[3,256]{1,0:T(4,128)S(1)} %collective-permute-done.4) | non-fusion elementwise | flops 768 | bytes 9216 | tf_op jit(solution)/shard_map/add | solution.py:503
  (1 shorter events, 0.0 us)
Async XLA Ops:
  0.0 6.9 %copy-start = (f32[48,16,256]{2,1,0:T(8,128)S(1)}, f32[48,16,256]{2,1,0:T(8,128)}, u32[]{:S(2)}) copy-start(f32[48,16,256]{2,1,0:T(8,128)} %dham_ref.3) | copy-start | bytes 2359300
  0.0 6.9 %copy-start.1 = (f32[48,16,256]{2,1,0:T(8,128)S(1)}, f32[48,16,256]{2,1,0:T(8,128)}, u32[]{:S(2)}) copy-start(f32[48,16,256]{2,1,0:T(8,128)} %dovl_ref.3) | copy-start | bytes 2359300
  0.0 6.9 %copy-start.2 = (s32[16,256]{1,0:T(8,128)S(1)}, s32[16,256]{1,0:T(8,128)}, u32[]{:S(2)}) copy-start(s32[16,256]{1,0:T(8,128)} %nbr_ref.7) | copy-start | bytes 49156
  0.0 7.0 %copy-start.3 = (f32[1024]{0:T(1024)S(1)}, f32[1024]{0:T(1024)}, u32[]{:S(2)}) copy-start(f32[1024]{0:T(1024)} %param.7) | copy-start | bytes 12292
  0.0 7.0 %copy-start.4 = (f32[1024]{0:T(1024)S(1)}, f32[1024]{0:T(1024)}, u32[]{:S(2)}) copy-start(f32[1024]{0:T(1024)} %param.8) | copy-start | bytes 12292
  2.2 18.3 %collective-permute-start.1 = (f32[8,304,128]{2,1,0:T(8,128)S(1)}, f32[8,304,128]{2,1,0:T(8,128)S(1)}, u32[]{:S(2)}, u32[]{:S(2)}) collective-permute-start(f32[8,304,128]{2,1,0:T(8,128)S(1)} %get-tuple-element.19), channel_id=1, source_target_pairs={{0,1},{1,0},{2,3},{3,2},{4,5},{5,4},{6,7},{7,6},{8,9},{9,8},{10,11... | collective-permute-start | bytes 3735560 | tf_op jit(solution)/shard_map/ppermute | solution.py:409
  2.4 20.2 %collective-permute-start = (f32[8,304,128]{2,1,0:T(8,128)S(1)}, f32[8,304,128]{2,1,0:T(8,128)S(1)}, u32[]{:S(2)}, u32[]{:S(2)}) collective-permute-start(f32[8,304,128]{2,1,0:T(8,128)S(1)} %get-tuple-element.18), channel_id=1, source_target_pairs={{1,4},{4,1},{5,8},{8,5},{9,12},{12,9},{3,6},{6,3},{7,10},{10,7},{1... | collective-permute-start | bytes 3735560 | tf_op jit(solution)/shard_map/ppermute | solution.py:415
  25.5 5.0 %collective-permute-start.3 = (f32[8,256]{1,0:T(8,128)S(1)}, f32[8,256]{1,0:T(8,128)S(1)}, u32[]{:S(2)}, u32[]{:S(2)}) collective-permute-start(f32[8,256]{1,0:T(8,128)S(1)} %get-tuple-element.30), channel_id=1, source_target_pairs={{1,4},{4,1},{5,8},{8,5},{9,12},{12,9},{3,6},{6,3},{7,10},{10,7},{1... | collective-permute-start | bytes 24584 | tf_op jit(solution)/shard_map/ppermute | solution.py:415
  27.4 3.0 %collective-permute-start.2 = (f32[8,256]{1,0:T(8,128)S(1)}, f32[8,256]{1,0:T(8,128)S(1)}, u32[]{:S(2)}, u32[]{:S(2)}) collective-permute-start(f32[8,256]{1,0:T(8,128)S(1)} %get-tuple-element.29), channel_id=1, source_target_pairs={{0,1},{1,0},{2,3},{3,2},{4,5},{5,4},{6,7},{7,6},{8,9},{9,8},{10,11... | collective-permute-start | bytes 24584 | tf_op jit(solution)/shard_map/ppermute | solution.py:409
  30.4 2.5 %collective-permute-start.4 = (f32[3,256]{1,0:T(4,128)S(1)}, f32[3,256]{1,0:T(4,128)S(1)}, u32[]{:S(2)}, u32[]{:S(2)}) collective-permute-start(f32[3,256]{1,0:T(4,128)S(1)} %slice_add_fusion), channel_id=1, source_target_pairs={{0,2},{2,0},{1,3},{3,1},{4,6},{6,4},{5,7},{7,5},{8,10},{10,8},{9,1... | collective-permute-start | bytes 9224 | tf_op jit(solution)/shard_map/ppermute | solution.py:503

commit v10 on v9

--- a/solution.py
+++ b/solution.py
@@ -135,9 +135,10 @@
 
 def inner_kernel(
     start_ref, coeffs_ref, occup_ref, energies_ref, nbr_ref, dham_ref, dovl_ref,
-    own_high_ref, own_low_ref, near1_high_ref, near1_low_ref, force_ref, deriv_ref, slot_ref,
-    near0_high_ref, near0_low_ref, near2_high_ref, near2_low_ref, near3_high_ref, near3_low_ref,
-    gram0_ref, gram1_ref, gram2_ref, gram3_ref, index_ref, spread_ref, columns_ref, copy_sem,
+    own_high_ref, own_low_ref, near1_high_ref, near1_low_ref, near3_high_ref, near3_low_ref,
+    force_ref, deriv_ref, slot_ref,
+    near0_high_ref, near0_low_ref, near2_high_ref, near2_low_ref,
+    gram0_ref, gram1_ref, gram2_ref, index_ref, spread_ref, columns_ref, copy_sem,
 ):
     states = coeffs_ref.shape[1]
     count = states // LANES
@@ -147,7 +148,7 @@
         (near2_high_ref, near2_low_ref),
         (near3_high_ref, near3_low_ref),
     ]
-    grams = [gram0_ref, gram1_ref, gram2_ref, gram3_ref]
+    grams = [gram0_ref, gram1_ref, gram2_ref]
     copies = [
         pltpu.make_async_copy(
             coeffs_ref.at[:, c * LANES : (c + 1) * LANES], columns_ref.at[c], copy_sem.at[c]
@@ -212,11 +213,10 @@
         theirs = spread(lambda r: slot_ref[32 * tile + r], pair, spread_ref, 256 - tile * LANES)
         return mine, theirs
 
-    for h in (3, 2, 1, 0):
+    for h in (2, 1, 0):
         multiply(h)
-    pair3 = pick(3)
-    pair2 = pick(2)
-    mine1, theirs1 = finish(1, pair2, pair3)
+    nothing = [[jnp.zeros((8, LANES), jnp.float32)] * 2] * 3
+    mine1, theirs1 = finish(1, pick(2), nothing)
     pair1 = pick(1)
     pair0 = pick(0)
     mine0, theirs0 = finish(0, pair0, pair1)
@@ -401,6 +401,28 @@
             sent_ref[k : k + 1, atoms - BLOCK :] = -2.0 * mine[k][:, BLOCK:]
 
 
+def last_kernel(
+    start_ref, before_ref, nbr_ref, deriv_ref, slot_ref, own_high_ref, own_low_ref, near_high_ref, near_low_ref,
+    force_ref, gram_ref, index_ref, spread_ref,
+):
+    gram_ref[...] = gram(
+        near_high_ref[...], near_low_ref[...], own_high_ref[768:, :], own_low_ref[768:, :]
+    )
+    index_ref[...] = nbr_ref[:, LANES:] - (start_ref[0] + LANES)
+    index = [part - BLOCK for part in block_index(index_ref, 1)]
+    pair = fold(
+        pick_pairs(tiles(gram_ref, 0, BLOCK), BLOCK // 8, index, lambda *key: deriv_ref[3, deriv_at(*key)])
+    )
+    nothing = [[jnp.zeros((8, LANES), jnp.float32)] * 2] * 3
+    pair = merge(nothing, pair)
+    mine = slot_sum(pair)
+    theirs = spread(lambda r: slot_ref[40 + r], pair, spread_ref, BLOCK)
+    force_ref[...] = before_ref[...]
+    for k in range(3):
+        force_ref[k : k + 1, LANES:] += -2.0 * mine[k]
+        force_ref[k : k + 1, LANES + BLOCK :] += 2.0 * theirs[k]
+
+
 def in_hbm(value):
     return pltpu.with_memory_space_constraint(value, pltpu.HBM)
 
@@ -450,17 +472,17 @@
     )(start, *(in_hbm(value) for value in (coeffs, nbr, dham, dovl)))
     far_payload = shard_swap(far_payload)
     core_payload = core_swap(core_payload)
-    own_high, own_low, near_high, near_low, inner, derivs, slot_maps = pl.pallas_call(
+    own_high, own_low, near_high, near_low, last_high, last_low, inner, derivs, slot_maps = pl.pallas_call(
         inner_kernel,
         out_shape=(
-            whole, whole, half, half, force,
+            whole, whole, half, half, half, half, force,
             jax.ShapeDtypeStruct((4, 96, 8, LANES), jnp.float32),
             jax.ShapeDtypeStruct((64 - UPPER // 8, 8, LANES), jnp.int32),
         ),
         in_specs=[smem, hbm] + [vmem] * 5,
-        out_specs=(vmem,) * 7,
-        scratch_shapes=[prepared] * 6
-        + [pltpu.VMEM((512 * n, 256), jnp.float32) for n in (3, 3, 2, 1)]
+        out_specs=(vmem,) * 9,
+        scratch_shapes=[prepared] * 4
+        + [pltpu.VMEM((512 * n, 256), jnp.float32) for n in (3, 3, 2)]
         + [
             pltpu.VMEM((2, slots, LANES), jnp.int32),
             pltpu.VMEM((3, atoms, LANES), jnp.float32),
@@ -469,7 +491,7 @@
         ],
         compiler_params=pltpu.CompilerParams(vmem_limit_bytes=32 * 1024 * 1024),
         cost_estimate=pl.CostEstimate(
-            flops=3 * 2 * 9 * 512 * 256 * states, bytes_accessed=16 * 1024 * 1024, transcendentals=0
+            flops=3 * 2 * 8 * 512 * 256 * states, bytes_accessed=16 * 1024 * 1024, transcendentals=0
         ),
         name="inner_pairs",
     )(start, in_hbm(coeffs), occup, energies, nbr, dham, dovl)
@@ -498,7 +520,24 @@
     total, core_sent = cross(0, core_payload, inner, "core_pairs")
     core_back = core_swap(core_sent)
     total, far_sent = cross(1, far_payload, total, "far_pairs")
-    total = (total + core_back + shard_swap(far_sent))[:3]
+    far_back = shard_swap(far_sent)
+    total = pl.pallas_call(
+        last_kernel,
+        out_shape=force,
+        in_specs=[smem] + [vmem] * 8,
+        out_specs=vmem,
+        scratch_shapes=[
+            pltpu.VMEM((512, 256), jnp.float32),
+            pltpu.VMEM((slots, LANES), jnp.int32),
+            pltpu.VMEM((3, BLOCK, LANES), jnp.float32),
+        ],
+        compiler_params=pltpu.CompilerParams(vmem_limit_bytes=12 * 1024 * 1024),
+        cost_estimate=pl.CostEstimate(
+            flops=3 * 2 * 512 * 256 * states, bytes_accessed=0, transcendentals=0
+        ),
+        name="last_pairs",
+    )(start, total, nbr, derivs, slot_maps, own_high, own_low, last_high, last_low)
+    total = (total + core_back + far_back)[:3]
     if lax.axis_size("states") == 2:
         return total + lax.ppermute(total, "states", [(0, 1), (1, 0)])
     return lax.psum(total, "states")

time: 33.7 us -> 33.7 us (level)
  the two profiles are of different devices: /device:TPU:1 before, /device:TPU:0 now
where the time goes in v10:
time: 33.7 us; the launch traced here: 33.5 us
  Pallas kernels  20.9 us (62%)
  starting transfers between devices  9.76 us (29%)
  waiting for transfers between devices  2.13 us (6%)
  other arithmetic  0.62 us (2%)
    pallas_call x1, Pallas kernels, local(): pl.pallas_call(inner_kernel, out_shape=(whole, whole, half, half, half, h...  12.2 us
    ppermute x2, starting transfers between devices, core_swap(): return lax.ppermute(value, 'sub', [(0, 1), (1, 0)])  6.8 us
    pallas_call x2, Pallas kernels, cross(): pl.pallas_call(functools.partial(cross_kernel, parity), out_shape=(force,...  4.7 us
    pallas_call x1, Pallas kernels, local(): pl.pallas_call(pack_kernel, out_shape=(payload, payload), in_specs=[smem]...  2.21 us
    ppermute x1, waiting for transfers between devices, local(): return total + lax.ppermute(total, 'states', [(0, 1), (1, 0)])  2.12 us
    pallas_call x1, Pallas kernels, local(): pl.pallas_call(last_kernel, out_shape=force, in_specs=[smem] + [vmem] * 8...  1.73 us
    ppermute x1, starting transfers between devices, local(): return total + lax.ppermute(total, 'states', [(0, 1), (1, 0)])  1.55 us
    ppermute x2, starting transfers between devices, shard_swap(): return lax.ppermute(value, SHARD, pairs)  1.41 us
  transfers between devices with their start and end apart: 5, of which 1 were waited for; matrix products, arithmetic and copies ran while one was open for 0% of the time, Pallas kernels for 50%

profile of v10, /device:TPU:0, one launch (start us, length us, event | category | flops | bytes accessed | tf_op | source)
XLA Modules:
  0.0 33.5 jit_solution(10000099881402572204)
XLA Ops:
  0.0 0.0 copy-start
  0.0 0.0 copy-start.1
  0.0 0.0 copy-start.2
  0.0 0.0 copy-start.3
  0.0 0.0 copy-start.4
  0.0 2.2 %pack.1 = (f32[8,304,128]{2,1,0:T(8,128)S(1)}, f32[8,304,128]{2,1,0:T(8,128)S(1)}) custom-call(s32[1]{0:T(128)} %bitcast.start_ref, f32[1024,1024]{1,0:T(8,128)} %coeffs_ref.3, s32[16,256]{1,0:T(8,128)} %nbr_ref.9, f32[48,16,256]{2,1,0:T(8,128)} %dham_ref.3, f32[48,16,256]{2,1,0:T(8,128)} %dovl_ref.3), custom_call_target="tpu_custom_call" | custom-call | tf_op jit(solution)/shard_map/pack/pallas_call | solution.py:457
  2.2 0.5 %collective-permute-start.1 = (f32[8,304,128]{2,1,0:T(8,128)S(1)}, f32[8,304,128]{2,1,0:T(8,128)S(1)}, u32[]{:S(2)}, u32[]{:S(2)}) collective-permute-start(f32[8,304,128]{2,1,0:T(8,128)S(1)} %get-tuple-element.21), channel_id=1, source_target_pairs={{0,1},{1,0},{2,3},{3,2},{4,5},{5,4},{6,7},{7,6},{8,9},{9,8},{10,11... | collective-permute-start | bytes 3735560 | tf_op jit(solution)/shard_map/ppermute | solution.py:431
  2.8 0.7 %collective-permute-start = (f32[8,304,128]{2,1,0:T(8,128)S(1)}, f32[8,304,128]{2,1,0:T(8,128)S(1)}, u32[]{:S(2)}, u32[]{:S(2)}) collective-permute-start(f32[8,304,128]{2,1,0:T(8,128)S(1)} %get-tuple-element.20), channel_id=1, source_target_pairs={{1,4},{4,1},{5,8},{8,5},{9,12},{12,9},{3,6},{6,3},{7,10},{10,7},{1... | collective-permute-start | bytes 3735560 | tf_op jit(solution)/shard_map/ppermute | solution.py:437
  3.5 0.0 copy-done
  3.5 0.0 copy-done.1
  3.5 0.0 copy-done.2
  3.5 0.0 copy-done.3
  3.5 0.0 copy-done.4
  3.6 12.2 %inner_pairs.1 = (bf16[1024,1024]{1,0:T(8,128)(2,1)S(1)}, bf16[1024,1024]{1,0:T(8,128)(2,1)S(1)}, bf16[512,1024]{1,0:T(8,128)(2,1)S(1)}, bf16[512,1024]{1,0:T(8,...) custom-call(s32[1]{0:T(128)} %bitcast.start_ref, ...), custom_call_target="tpu_custom_call" | custom-call | flops 6442450944 | bytes 16777216 | tf_op jit(solution)/shard_map/inner_pairs/pallas_call | solution.py:475
  15.8 0.0 collective-permute-done.1.payload_ref
  15.8 2.9 %core_pairs.1 = (f32[8,256]{1,0:T(8,128)S(1)}, f32[8,256]{1,0:T(8,128)S(1)}) custom-call(s32[1]{0:T(128)} %bitcast.start_ref, f32[8,304,128]{2,1,0:T(8,128)S(1)} %collective-permute-done.1.payload_ref, f32[8,256]{1,0:T(8,128)S(1)} %get-tuple-element.22.before_ref, f32[1,1024]{1,0:T(1,128)S(1)} %bitcast.4, f32[1,1024]{1,0:T(1,128)S(1)} %bitcast.7, ...), custom_call_target="tpu_custom_call" | custom-call | flops 1610612736 | bytes 6291456 | tf_op jit(solution)/shard_map/core_pairs/pallas_call | solution.py:501
  18.7 0.0 collective-permute-done.payload_ref
  18.7 1.8 %far_pairs.1 = (f32[8,256]{1,0:T(8,128)S(1)}, f32[8,256]{1,0:T(8,128)S(1)}) custom-call(s32[1]{0:T(128)} %bitcast.start_ref, f32[8,304,128]{2,1,0:T(8,128)S(1)} %collective-permute-done.payload_ref, f32[8,256]{1,0:T(8,128)S(1)} %get-tuple-element.29.before_ref, f32[1,1024]{1,0:T(1,128)S(1)} %bitcast.5, f32[1,1024]{1,0:T(1,128)S(1)} %bitcast.8, ...), custom_call_target="tpu_custom_call" | custom-call | flops 1610612736 | bytes 6291456 | tf_op jit(solution)/shard_map/far_pairs/pallas_call | solution.py:501
  20.5 0.7 %collective-permute-start.3 = (f32[8,256]{1,0:T(8,128)S(1)}, f32[8,256]{1,0:T(8,128)S(1)}, u32[]{:S(2)}, u32[]{:S(2)}) collective-permute-start(f32[8,256]{1,0:T(8,128)S(1)} %get-tuple-element.34), channel_id=1, source_target_pairs={{1,4},{4,1},{5,8},{8,5},{9,12},{12,9},{3,6},{6,3},{7,10},{10,7},{1... | collective-permute-start | bytes 24584 | tf_op jit(solution)/shard_map/ppermute | solution.py:437
  21.2 6.3 %collective-permute-start.2 = (f32[8,256]{1,0:T(8,128)S(1)}, f32[8,256]{1,0:T(8,128)S(1)}, u32[]{:S(2)}, u32[]{:S(2)}) collective-permute-start(f32[8,256]{1,0:T(8,128)S(1)} %get-tuple-element.33), channel_id=1, source_target_pairs={{0,1},{1,0},{2,3},{3,2},{4,5},{5,4},{6,7},{7,6},{8,9},{9,8},{10,11... | collective-permute-start | bytes 24584 | tf_op jit(solution)/shard_map/ppermute | solution.py:431
  27.5 1.7 %last_pairs.1 = f32[8,256]{1,0:T(8,128)S(1)} custom-call(s32[1]{0:T(128)} %bitcast.start_ref, f32[8,256]{1,0:T(8,128)S(1)} %get-tuple-element.30.before_ref, s32[16,256]{1,0:T(8,128)S(1)} %copy-done.2, f32[4,96,8,128]{3,2,1,0:T(8,128)S(1)} %get-tuple-element.23.deriv_ref, s32[58,8,128]{2,1,0:T(8,128)S(1)} %get-tuple-element.24.slot_ref, ...), custom_call_target="tpu_custom_call" | custom-call | flops 805306368 | tf_op jit(solution)/shard_map/last_pairs/pallas_call | solution.py:524
  29.2 0.0 collective-permute-done.3
  29.2 0.0 collective-permute-done.2
  29.2 1.6 %collective-permute-start.4 = (f32[3,256]{1,0:T(4,128)S(1)}, f32[3,256]{1,0:T(4,128)S(1)}, u32[]{:S(2)}, u32[]{:S(2)}) collective-permute-start(f32[3,256]{1,0:T(4,128)S(1)} %slice_add_fusion), channel_id=1, source_target_pairs={{0,2},{2,0},{1,3},{3,1},{4,6},{6,4},{5,7},{7,5},{8,10},{10,8},{9,1... | collective-permute-start | bytes 9224 | tf_op jit(solution)/shard_map/ppermute | solution.py:542
  30.8 2.1 %collective-permute-done.4 = f32[3,256]{1,0:T(4,128)S(1)} collective-permute-done((f32[3,256]{1,0:T(4,128)S(1)}, f32[3,256]{1,0:T(4,128)S(1)}, u32[]{:S(2)}, u32[]{:S(2)}) %collective-permute-start.4) | collective-permute-done | bytes 3104 | tf_op jit(solution)/shard_map/ppermute | solution.py:542
  32.9 0.6 %add.15 = f32[3,256]{1,0:T(4,128)} add(f32[3,256]{1,0:T(4,128)S(1)} %slice_add_fusion, f32[3,256]{1,0:T(4,128)S(1)} %collective-permute-done.4) | non-fusion elementwise | flops 768 | bytes 9216 | tf_op jit(solution)/shard_map/add | solution.py:542
  (1 shorter events, 0.0 us)
Async XLA Ops:
  0.0 3.5 %copy-start = (f32[48,16,256]{2,1,0:T(8,128)S(1)}, f32[48,16,256]{2,1,0:T(8,128)}, u32[]{:S(2)}) copy-start(f32[48,16,256]{2,1,0:T(8,128)} %dham_ref.3) | copy-start | bytes 2359300
  0.0 3.5 %copy-start.1 = (f32[48,16,256]{2,1,0:T(8,128)S(1)}, f32[48,16,256]{2,1,0:T(8,128)}, u32[]{:S(2)}) copy-start(f32[48,16,256]{2,1,0:T(8,128)} %dovl_ref.3) | copy-start | bytes 2359300
  0.0 3.5 %copy-start.2 = (s32[16,256]{1,0:T(8,128)S(1)}, s32[16,256]{1,0:T(8,128)}, u32[]{:S(2)}) copy-start(s32[16,256]{1,0:T(8,128)} %nbr_ref.9) | copy-start | bytes 49156
  0.0 3.5 %copy-start.3 = (f32[1024]{0:T(1024)S(1)}, f32[1024]{0:T(1024)}, u32[]{:S(2)}) copy-start(f32[1024]{0:T(1024)} %param.7) | copy-start | bytes 12292
  0.0 3.5 %copy-start.4 = (f32[1024]{0:T(1024)S(1)}, f32[1024]{0:T(1024)}, u32[]{:S(2)}) copy-start(f32[1024]{0:T(1024)} %param.8) | copy-start | bytes 12292
  2.2 13.5 %collective-permute-start.1 = (f32[8,304,128]{2,1,0:T(8,128)S(1)}, f32[8,304,128]{2,1,0:T(8,128)S(1)}, u32[]{:S(2)}, u32[]{:S(2)}) collective-permute-start(f32[8,304,128]{2,1,0:T(8,128)S(1)} %get-tuple-element.21), channel_id=1, source_target_pairs={{0,1},{1,0},{2,3},{3,2},{4,5},{5,4},{6,7},{7,6},{8,9},{9,8},{10,11... | collective-permute-start | bytes 3735560 | tf_op jit(solution)/shard_map/ppermute | solution.py:431
  2.8 15.9 %collective-permute-start = (f32[8,304,128]{2,1,0:T(8,128)S(1)}, f32[8,304,128]{2,1,0:T(8,128)S(1)}, u32[]{:S(2)}, u32[]{:S(2)}) collective-permute-start(f32[8,304,128]{2,1,0:T(8,128)S(1)} %get-tuple-element.20), channel_id=1, source_target_pairs={{1,4},{4,1},{5,8},{8,5},{9,12},{12,9},{3,6},{6,3},{7,10},{10,7},{1... | collective-permute-start | bytes 3735560 | tf_op jit(solution)/shard_map/ppermute | solution.py:437
  20.5 8.7 %collective-permute-start.3 = (f32[8,256]{1,0:T(8,128)S(1)}, f32[8,256]{1,0:T(8,128)S(1)}, u32[]{:S(2)}, u32[]{:S(2)}) collective-permute-start(f32[8,256]{1,0:T(8,128)S(1)} %get-tuple-element.34), channel_id=1, source_target_pairs={{1,4},{4,1},{5,8},{8,5},{9,12},{12,9},{3,6},{6,3},{7,10},{10,7},{1... | collective-permute-start | bytes 24584 | tf_op jit(solution)/shard_map/ppermute | solution.py:437
  21.2 8.0 %collective-permute-start.2 = (f32[8,256]{1,0:T(8,128)S(1)}, f32[8,256]{1,0:T(8,128)S(1)}, u32[]{:S(2)}, u32[]{:S(2)}) collective-permute-start(f32[8,256]{1,0:T(8,128)S(1)} %get-tuple-element.33), channel_id=1, source_target_pairs={{0,1},{1,0},{2,3},{3,2},{4,5},{5,4},{6,7},{7,6},{8,9},{9,8},{10,11... | collective-permute-start | bytes 24584 | tf_op jit(solution)/shard_map/ppermute | solution.py:431
  29.2 3.7 %collective-permute-start.4 = (f32[3,256]{1,0:T(4,128)S(1)}, f32[3,256]{1,0:T(4,128)S(1)}, u32[]{:S(2)}, u32[]{:S(2)}) collective-permute-start(f32[3,256]{1,0:T(4,128)S(1)} %slice_add_fusion), channel_id=1, source_target_pairs={{0,2},{2,0},{1,3},{3,1},{4,6},{6,4},{5,7},{7,5},{8,10},{10,8},{9,1... | collective-permute-start | bytes 9224 | tf_op jit(solution)/shard_map/ppermute | solution.py:542

commit v11 on v10

--- a/solution.py
+++ b/solution.py
@@ -402,7 +402,8 @@
 
 
 def last_kernel(
-    start_ref, before_ref, nbr_ref, deriv_ref, slot_ref, own_high_ref, own_low_ref, near_high_ref, near_low_ref,
+    start_ref, before_ref, back_ref, nbr_ref, deriv_ref, slot_ref,
+    own_high_ref, own_low_ref, near_high_ref, near_low_ref,
     force_ref, gram_ref, index_ref, spread_ref,
 ):
     gram_ref[...] = gram(
@@ -417,7 +418,7 @@
     pair = merge(nothing, pair)
     mine = slot_sum(pair)
     theirs = spread(lambda r: slot_ref[40 + r], pair, spread_ref, BLOCK)
-    force_ref[...] = before_ref[...]
+    force_ref[...] = before_ref[...] + back_ref[...]
     for k in range(3):
         force_ref[k : k + 1, LANES:] += -2.0 * mine[k]
         force_ref[k : k + 1, LANES + BLOCK :] += 2.0 * theirs[k]
@@ -524,7 +525,7 @@
     total = pl.pallas_call(
         last_kernel,
         out_shape=force,
-        in_specs=[smem] + [vmem] * 8,
+        in_specs=[smem] + [vmem] * 9,
         out_specs=vmem,
         scratch_shapes=[
             pltpu.VMEM((512, 256), jnp.float32),
@@ -536,8 +537,8 @@
             flops=3 * 2 * 512 * 256 * states, bytes_accessed=0, transcendentals=0
         ),
         name="last_pairs",
-    )(start, total, nbr, derivs, slot_maps, own_high, own_low, last_high, last_low)
-    total = (total + core_back + far_back)[:3]
+    )(start, total, core_back, nbr, derivs, slot_maps, own_high, own_low, last_high, last_low)
+    total = (total + far_back)[:3]
     if lax.axis_size("states") == 2:
         return total + lax.ppermute(total, "states", [(0, 1), (1, 0)])
     return lax.psum(total, "states")

time: 33.7 us -> 32.9 us (0.976)
  the two profiles are of different devices: /device:TPU:0 before, /device:TPU:1 now
where the time goes in v11:
time: 32.9 us; the launch traced here: 32.7 us
  Pallas kernels  21 us (64%)
  starting transfers between devices  8.95 us (27%)
  waiting for transfers between devices  2.03 us (6%)
  other arithmetic  0.6 us (2%)
    pallas_call x1, Pallas kernels, local(): pl.pallas_call(inner_kernel, out_shape=(whole, whole, half, half, half, h...  12.2 us
    ppermute x2, starting transfers between devices, shard_swap(): return lax.ppermute(value, SHARD, pairs)  7.1 us
    pallas_call x2, Pallas kernels, cross(): pl.pallas_call(functools.partial(cross_kernel, parity), out_shape=(force,...  4.85 us
    pallas_call x1, Pallas kernels, local(): pl.pallas_call(pack_kernel, out_shape=(payload, payload), in_specs=[smem]...  2.21 us
    ppermute x1, starting transfers between devices, local(): return total + lax.ppermute(total, 'states', [(0, 1), (1, 0)])  1.74 us
    pallas_call x1, Pallas kernels, local(): pl.pallas_call(last_kernel, out_shape=force, in_specs=[smem] + [vmem] * 9...  1.73 us
    ppermute x2, waiting for transfers between devices, shard_swap(): return lax.ppermute(value, SHARD, pairs)  1.03 us
    ppermute x1, waiting for transfers between devices, local(): return total + lax.ppermute(total, 'states', [(0, 1), (1, 0)])  0.99 us
  transfers between devices with their start and end apart: 5, of which 3 were waited for; matrix products, arithmetic and copies ran while one was open for 0% of the time, Pallas kernels for 57%

profile of v11, /device:TPU:1, one launch (start us, length us, event | category | flops | bytes accessed | tf_op | source)
XLA Modules:
  0.0 32.7 jit_solution(7148037830401445925)
XLA Ops:
  0.0 0.0 copy-start
  0.0 0.0 copy-start.1
  0.0 0.0 copy-start.2
  0.0 0.0 copy-start.3
  0.0 0.0 copy-start.4
  0.0 2.2 %pack.1 = (f32[8,304,128]{2,1,0:T(8,128)S(1)}, f32[8,304,128]{2,1,0:T(8,128)S(1)}) custom-call(s32[1]{0:T(128)} %bitcast.start_ref, f32[1024,1024]{1,0:T(8,128)} %coeffs_ref.3, s32[16,256]{1,0:T(8,128)} %nbr_ref.9, f32[48,16,256]{2,1,0:T(8,128)} %dham_ref.3, f32[48,16,256]{2,1,0:T(8,128)} %dovl_ref.3), custom_call_target="tpu_custom_call" | custom-call | tf_op jit(solution)/shard_map/pack/pallas_call | solution.py:458
  2.2 0.1 collective-permute-start.1
  2.4 4.6 %collective-permute-start = (f32[8,304,128]{2,1,0:T(8,128)S(1)}, f32[8,304,128]{2,1,0:T(8,128)S(1)}, u32[]{:S(2)}, u32[]{:S(2)}) collective-permute-start(f32[8,304,128]{2,1,0:T(8,128)S(1)} %get-tuple-element.20), channel_id=1, source_target_pairs={{1,4},{4,1},{5,8},{8,5},{9,12},{12,9},{3,6},{6,3},{7,10},{10,7},{1... | collective-permute-start | bytes 3735560 | tf_op jit(solution)/shard_map/ppermute | solution.py:438
  6.9 0.0 copy-done
  6.9 0.0 copy-done.1
  6.9 0.0 copy-done.2
  7.0 0.0 copy-done.3
  7.0 0.0 copy-done.4
  7.0 12.2 %inner_pairs.1 = (bf16[1024,1024]{1,0:T(8,128)(2,1)S(1)}, bf16[1024,1024]{1,0:T(8,128)(2,1)S(1)}, bf16[512,1024]{1,0:T(8,128)(2,1)S(1)}, bf16[512,1024]{1,0:T(8,...) custom-call(s32[1]{0:T(128)} %bitcast.start_ref, ...), custom_call_target="tpu_custom_call" | custom-call | flops 6442450944 | bytes 16777216 | tf_op jit(solution)/shard_map/inner_pairs/pallas_call | solution.py:476
  19.2 0.0 collective-permute-done.1.payload_ref
  19.2 2.0 %core_pairs.1 = (f32[8,256]{1,0:T(8,128)S(1)}, f32[8,256]{1,0:T(8,128)S(1)}) custom-call(s32[1]{0:T(128)} %bitcast.start_ref, f32[8,304,128]{2,1,0:T(8,128)S(1)} %collective-permute-done.1.payload_ref, f32[8,256]{1,0:T(8,128)S(1)} %get-tuple-element.22.before_ref, f32[1,1024]{1,0:T(1,128)S(1)} %bitcast.4, f32[1,1024]{1,0:T(1,128)S(1)} %bitcast.7, ...), custom_call_target="tpu_custom_call" | custom-call | flops 1610612736 | bytes 6291456 | tf_op jit(solution)/shard_map/core_pairs/pallas_call | solution.py:502
  21.2 0.0 collective-permute-start.2
  21.2 0.3 %collective-permute-done.payload_ref = f32[8,304,128]{2,1,0:T(8,128)S(1)} collective-permute-done((f32[8,304,128]{2,1,0:T(8,128)S(1)}, f32[8,304,128]{2,1,0:T(8,128)S(1)}, u32[]{:S(2)}, u32[]{:S(2)}) %collective-permute-start) | collective-permute-done | bytes 1245216 | tf_op jit(solution)/shard_map/ppermute | solution.py:438
  21.5 2.9 %far_pairs.1 = (f32[8,256]{1,0:T(8,128)S(1)}, f32[8,256]{1,0:T(8,128)S(1)}) custom-call(s32[1]{0:T(128)} %bitcast.start_ref, f32[8,304,128]{2,1,0:T(8,128)S(1)} %collective-permute-done.payload_ref, f32[8,256]{1,0:T(8,128)S(1)} %get-tuple-element.29.before_ref, f32[1,1024]{1,0:T(1,128)S(1)} %bitcast.5, f32[1,1024]{1,0:T(1,128)S(1)} %bitcast.8, ...), custom_call_target="tpu_custom_call" | custom-call | flops 1610612736 | bytes 6291456 | tf_op jit(solution)/shard_map/far_pairs/pallas_call | solution.py:502
  24.4 2.5 %collective-permute-start.3 = (f32[8,256]{1,0:T(8,128)S(1)}, f32[8,256]{1,0:T(8,128)S(1)}, u32[]{:S(2)}, u32[]{:S(2)}) collective-permute-start(f32[8,256]{1,0:T(8,128)S(1)} %get-tuple-element.34), channel_id=1, source_target_pairs={{1,4},{4,1},{5,8},{8,5},{9,12},{12,9},{3,6},{6,3},{7,10},{10,7},{1... | collective-permute-start | bytes 24584 | tf_op jit(solution)/shard_map/ppermute | solution.py:438
  26.9 0.0 collective-permute-done.2.back_ref
  26.9 1.7 %last_pairs.1 = f32[8,256]{1,0:T(8,128)S(1)} custom-call(s32[1]{0:T(128)} %bitcast.start_ref, f32[8,256]{1,0:T(8,128)S(1)} %get-tuple-element.30.before_ref, f32[8,256]{1,0:T(8,128)S(1)} %collective-permute-done.2.back_ref, s32[16,256]{1,0:T(8,128)S(1)} %copy-done.2, f32[4,96,8,128]{3,2,1,0:T(8,128)S(1)} %get-tuple-element.23.deriv_ref, ...), custom_call_target="tpu_custom_call" | custom-call | flops 805306368 | tf_op jit(solution)/shard_map/last_pairs/pallas_call | solution.py:525
  28.7 0.7 %collective-permute-done.3 = f32[8,256]{1,0:T(8,128)S(1)} collective-permute-done((f32[8,256]{1,0:T(8,128)S(1)}, f32[8,256]{1,0:T(8,128)S(1)}, u32[]{:S(2)}, u32[]{:S(2)}) %collective-permute-start.3) | collective-permute-done | bytes 8224 | tf_op jit(solution)/shard_map/ppermute | solution.py:438
  29.4 1.7 %collective-permute-start.4 = (f32[3,256]{1,0:T(4,128)S(1)}, f32[3,256]{1,0:T(4,128)S(1)}, u32[]{:S(2)}, u32[]{:S(2)}) collective-permute-start(f32[3,256]{1,0:T(4,128)S(1)} %slice_add_fusion), channel_id=1, source_target_pairs={{0,2},{2,0},{1,3},{3,1},{4,6},{6,4},{5,7},{7,5},{8,10},{10,8},{9,1... | collective-permute-start | bytes 9224 | tf_op jit(solution)/shard_map/ppermute | solution.py:543
  31.1 1.0 %collective-permute-done.4 = f32[3,256]{1,0:T(4,128)S(1)} collective-permute-done((f32[3,256]{1,0:T(4,128)S(1)}, f32[3,256]{1,0:T(4,128)S(1)}, u32[]{:S(2)}, u32[]{:S(2)}) %collective-permute-start.4) | collective-permute-done | bytes 3104 | tf_op jit(solution)/shard_map/ppermute | solution.py:543
  32.1 0.6 %add.11 = f32[3,256]{1,0:T(4,128)} add(f32[3,256]{1,0:T(4,128)S(1)} %slice_add_fusion, f32[3,256]{1,0:T(4,128)S(1)} %collective-permute-done.4) | non-fusion elementwise | flops 768 | bytes 9216 | tf_op jit(solution)/shard_map/add | solution.py:543
  (1 shorter events, 0.0 us)
Async XLA Ops:
  0.0 6.9 %copy-start = (f32[48,16,256]{2,1,0:T(8,128)S(1)}, f32[48,16,256]{2,1,0:T(8,128)}, u32[]{:S(2)}) copy-start(f32[48,16,256]{2,1,0:T(8,128)} %dham_ref.3) | copy-start | bytes 2359300
  0.0 6.9 %copy-start.1 = (f32[48,16,256]{2,1,0:T(8,128)S(1)}, f32[48,16,256]{2,1,0:T(8,128)}, u32[]{:S(2)}) copy-start(f32[48,16,256]{2,1,0:T(8,128)} %dovl_ref.3) | copy-start | bytes 2359300
  0.0 6.9 %copy-start.2 = (s32[16,256]{1,0:T(8,128)S(1)}, s32[16,256]{1,0:T(8,128)}, u32[]{:S(2)}) copy-start(s32[16,256]{1,0:T(8,128)} %nbr_ref.9) | copy-start | bytes 49156
  0.0 7.0 %copy-start.3 = (f32[1024]{0:T(1024)S(1)}, f32[1024]{0:T(1024)}, u32[]{:S(2)}) copy-start(f32[1024]{0:T(1024)} %param.7) | copy-start | bytes 12292
  0.0 7.0 %copy-start.4 = (f32[1024]{0:T(1024)S(1)}, f32[1024]{0:T(1024)}, u32[]{:S(2)}) copy-start(f32[1024]{0:T(1024)} %param.8) | copy-start | bytes 12292
  2.2 16.9 %collective-permute-start.1 = (f32[8,304,128]{2,1,0:T(8,128)S(1)}, f32[8,304,128]{2,1,0:T(8,128)S(1)}, u32[]{:S(2)}, u32[]{:S(2)}) collective-permute-start(f32[8,304,128]{2,1,0:T(8,128)S(1)} %get-tuple-element.21), channel_id=1, source_target_pairs={{0,1},{1,0},{2,3},{3,2},{4,5},{5,4},{6,7},{7,6},{8,9},{9,8},{10,11... | collective-permute-start | bytes 3735560 | tf_op jit(solution)/shard_map/ppermute | solution.py:432
  2.4 19.1 %collective-permute-start = (f32[8,304,128]{2,1,0:T(8,128)S(1)}, f32[8,304,128]{2,1,0:T(8,128)S(1)}, u32[]{:S(2)}, u32[]{:S(2)}) collective-permute-start(f32[8,304,128]{2,1,0:T(8,128)S(1)} %get-tuple-element.20), channel_id=1, source_target_pairs={{1,4},{4,1},{5,8},{8,5},{9,12},{12,9},{3,6},{6,3},{7,10},{10,7},{1... | collective-permute-start | bytes 3735560 | tf_op jit(solution)/shard_map/ppermute | solution.py:438
  21.2 5.8 %collective-permute-start.2 = (f32[8,256]{1,0:T(8,128)S(1)}, f32[8,256]{1,0:T(8,128)S(1)}, u32[]{:S(2)}, u32[]{:S(2)}) collective-permute-start(f32[8,256]{1,0:T(8,128)S(1)} %get-tuple-element.31), channel_id=1, source_target_pairs={{0,1},{1,0},{2,3},{3,2},{4,5},{5,4},{6,7},{7,6},{8,9},{9,8},{10,11... | collective-permute-start | bytes 24584 | tf_op jit(solution)/shard_map/ppermute | solution.py:432
  24.4 5.0 %collective-permute-start.3 = (f32[8,256]{1,0:T(8,128)S(1)}, f32[8,256]{1,0:T(8,128)S(1)}, u32[]{:S(2)}, u32[]{:S(2)}) collective-permute-start(f32[8,256]{1,0:T(8,128)S(1)} %get-tuple-element.34), channel_id=1, source_target_pairs={{1,4},{4,1},{5,8},{8,5},{9,12},{12,9},{3,6},{6,3},{7,10},{10,7},{1... | collective-permute-start | bytes 24584 | tf_op jit(solution)/shard_map/ppermute | solution.py:438
  29.4 2.7 %collective-permute-start.4 = (f32[3,256]{1,0:T(4,128)S(1)}, f32[3,256]{1,0:T(4,128)S(1)}, u32[]{:S(2)}, u32[]{:S(2)}) collective-permute-start(f32[3,256]{1,0:T(4,128)S(1)} %slice_add_fusion), channel_id=1, source_target_pairs={{0,2},{2,0},{1,3},{3,1},{4,6},{6,4},{5,7},{7,5},{8,10},{10,8},{9,1... | collective-permute-start | bytes 9224 | tf_op jit(solution)/shard_map/ppermute | solution.py:543

commit v12 on v11

--- a/solution.py
+++ b/solution.py
@@ -327,6 +327,7 @@
         occup = occup_ref[...]
         weights = [occup, occup * energies_ref[...]]
         size = cut_high_ref.shape[0] // 8
+        extra = size - BLOCK
         even = lower // 8 * 8
         for c in range(count):
             lanes = slice(c * LANES, (c + 1) * LANES)
@@ -339,16 +340,28 @@
                     0,
                 )
                 for x in range(2):
-                    at = slice((x * 4 + b) * size, (x * 4 + b + 1) * size)
-                    cut_high_ref[at, lanes], cut_low_ref[at, lanes] = split(rows * weights[x][:, lanes])
-        gram_ref[...] = gram(
-            cut_high_ref[...], cut_low_ref[...], own_high_ref[512:, :], own_low_ref[512:, :]
+                    high, low = split(rows * weights[x][:, lanes])
+                    at = slice((x * 4 + b) * BLOCK, (x * 4 + b + 1) * BLOCK)
+                    cut_high_ref[at, lanes], cut_low_ref[at, lanes] = high[:BLOCK], low[:BLOCK]
+                    at = slice(512 + (x * 4 + b) * extra, 512 + (x * 4 + b + 1) * extra)
+                    cut_high_ref[at, lanes], cut_low_ref[at, lanes] = high[BLOCK:], low[BLOCK:]
+        gram_ref[:, 256:] = gram(
+            cut_high_ref[...], cut_low_ref[...], own_high_ref[768:, :], own_low_ref[768:, :]
         )
+        gram_ref[:512, :256] = gram(
+            cut_high_ref[:512, :], cut_low_ref[:512, :], own_high_ref[512:768, :], own_low_ref[512:768, :]
+        )
+        first_tile = tiles(gram_ref, 256, BLOCK)
+        extra_tile = tiles(gram_ref.at[512:, :], 256, extra)
+
+        def odd_tile(r, *key):
+            return first_tile(r, *key) if r < BLOCK // 8 else extra_tile(r - BLOCK // 8, *key)
+
         target = nbr_ref[:, LANES:] - (start_ref[0] + atoms)
         index_ref[...] = jnp.where(target >= even, target + (size - lower), target)
         pairs = [
             pick_pairs(
-                tiles(gram_ref, 256 * h, size),
+                (tiles(gram_ref, 0, BLOCK), odd_tile)[h],
                 (BLOCK, size)[h] // 8,
                 block_index(index_ref, h),
                 lambda *key: deriv_ref[2 + h, deriv_at(*key)],

time: 32.9 us -> 32.9 us (level)
  transfers between devices with their start and end apart: 5 -> 5, of which waited for: 3 -> 3; matrix products, arithmetic and copies ran while one was open for 0% -> 0% of each run, Pallas kernels for 57% -> 58%
where the time goes in v12:
time: 32.9 us; the launch traced here: 32.7 us
  Pallas kernels  21 us (64%)
  starting transfers between devices  8.92 us (27%)
  waiting for transfers between devices  2.07 us (6%)
  other arithmetic  0.6 us (2%)
    pallas_call x1, Pallas kernels, local(): pl.pallas_call(inner_kernel, out_shape=(whole, whole, half, half, half, h...  12.2 us
    ppermute x2, starting transfers between devices, shard_swap(): return lax.ppermute(value, SHARD, pairs)  7.07 us
    pallas_call x2, Pallas kernels, cross(): pl.pallas_call(functools.partial(cross_kernel, parity), out_shape=(force,...  4.89 us
    pallas_call x1, Pallas kernels, local(): pl.pallas_call(pack_kernel, out_shape=(payload, payload), in_specs=[smem]...  2.21 us
    ppermute x1, starting transfers between devices, local(): return total + lax.ppermute(total, 'states', [(0, 1), (1, 0)])  1.74 us
    pallas_call x1, Pallas kernels, local(): pl.pallas_call(last_kernel, out_shape=force, in_specs=[smem] + [vmem] * 9...  1.73 us
    ppermute x2, waiting for transfers between devices, shard_swap(): return lax.ppermute(value, SHARD, pairs)  1.07 us
    ppermute x1, waiting for transfers between devices, local(): return total + lax.ppermute(total, 'states', [(0, 1), (1, 0)])  0.99 us
  transfers between devices with their start and end apart: 5, of which 3 were waited for; matrix products, arithmetic and copies ran while one was open for 0% of the time, Pallas kernels for 58%

profile of v12, /device:TPU:1, one launch (start us, length us, event | category | flops | bytes accessed | tf_op | source)
XLA Modules:
  0.0 32.7 jit_solution(7389278964218396257)
XLA Ops:
  0.0 0.0 copy-start
  0.0 0.0 copy-start.1
  0.0 0.0 copy-start.2
  0.0 0.0 copy-start.3
  0.0 0.0 copy-start.4
  0.0 2.2 %pack.1 = (f32[8,304,128]{2,1,0:T(8,128)S(1)}, f32[8,304,128]{2,1,0:T(8,128)S(1)}) custom-call(s32[1]{0:T(128)} %bitcast.start_ref, f32[1024,1024]{1,0:T(8,128)} %coeffs_ref.3, s32[16,256]{1,0:T(8,128)} %nbr_ref.9, f32[48,16,256]{2,1,0:T(8,128)} %dham_ref.3, f32[48,16,256]{2,1,0:T(8,128)} %dovl_ref.3), custom_call_target="tpu_custom_call" | custom-call | tf_op jit(solution)/shard_map/pack/pallas_call | solution.py:471
  2.2 0.1 collective-permute-start.1
  2.4 4.6 %collective-permute-start = (f32[8,304,128]{2,1,0:T(8,128)S(1)}, f32[8,304,128]{2,1,0:T(8,128)S(1)}, u32[]{:S(2)}, u32[]{:S(2)}) collective-permute-start(f32[8,304,128]{2,1,0:T(8,128)S(1)} %get-tuple-element.20), channel_id=1, source_target_pairs={{1,4},{4,1},{5,8},{8,5},{9,12},{12,9},{3,6},{6,3},{7,10},{10,7},{1... | collective-permute-start | bytes 3735560 | tf_op jit(solution)/shard_map/ppermute | solution.py:451
  6.9 0.0 copy-done
  6.9 0.0 copy-done.1
  6.9 0.0 copy-done.2
  7.0 0.0 copy-done.3
  7.0 0.0 copy-done.4
  7.0 12.2 %inner_pairs.1 = (bf16[1024,1024]{1,0:T(8,128)(2,1)S(1)}, bf16[1024,1024]{1,0:T(8,128)(2,1)S(1)}, bf16[512,1024]{1,0:T(8,128)(2,1)S(1)}, bf16[512,1024]{1,0:T(8,...) custom-call(s32[1]{0:T(128)} %bitcast.start_ref, ...), custom_call_target="tpu_custom_call" | custom-call | flops 6442450944 | bytes 16777216 | tf_op jit(solution)/shard_map/inner_pairs/pallas_call | solution.py:489
  19.2 0.0 collective-permute-done.1.payload_ref
  19.2 2.0 %core_pairs.1 = (f32[8,256]{1,0:T(8,128)S(1)}, f32[8,256]{1,0:T(8,128)S(1)}) custom-call(s32[1]{0:T(128)} %bitcast.start_ref, f32[8,304,128]{2,1,0:T(8,128)S(1)} %collective-permute-done.1.payload_ref, f32[8,256]{1,0:T(8,128)S(1)} %get-tuple-element.22.before_ref, f32[1,1024]{1,0:T(1,128)S(1)} %bitcast.4, f32[1,1024]{1,0:T(1,128)S(1)} %bitcast.7, ...), custom_call_target="tpu_custom_call" | custom-call | flops 1610612736 | bytes 6291456 | tf_op jit(solution)/shard_map/core_pairs/pallas_call | solution.py:515
  21.2 0.0 collective-permute-start.2
  21.2 0.3 %collective-permute-done.payload_ref = f32[8,304,128]{2,1,0:T(8,128)S(1)} collective-permute-done((f32[8,304,128]{2,1,0:T(8,128)S(1)}, f32[8,304,128]{2,1,0:T(8,128)S(1)}, u32[]{:S(2)}, u32[]{:S(2)}) %collective-permute-start) | collective-permute-done | bytes 1245216 | tf_op jit(solution)/shard_map/ppermute | solution.py:451
  21.5 2.9 %far_pairs.1 = (f32[8,256]{1,0:T(8,128)S(1)}, f32[8,256]{1,0:T(8,128)S(1)}) custom-call(s32[1]{0:T(128)} %bitcast.start_ref, f32[8,304,128]{2,1,0:T(8,128)S(1)} %collective-permute-done.payload_ref, f32[8,256]{1,0:T(8,128)S(1)} %get-tuple-element.29.before_ref, f32[1,1024]{1,0:T(1,128)S(1)} %bitcast.5, f32[1,1024]{1,0:T(1,128)S(1)} %bitcast.8, ...), custom_call_target="tpu_custom_call" | custom-call | flops 1610612736 | bytes 6291456 | tf_op jit(solution)/shard_map/far_pairs/pallas_call | solution.py:515
  24.4 2.5 %collective-permute-start.3 = (f32[8,256]{1,0:T(8,128)S(1)}, f32[8,256]{1,0:T(8,128)S(1)}, u32[]{:S(2)}, u32[]{:S(2)}) collective-permute-start(f32[8,256]{1,0:T(8,128)S(1)} %get-tuple-element.34), channel_id=1, source_target_pairs={{1,4},{4,1},{5,8},{8,5},{9,12},{12,9},{3,6},{6,3},{7,10},{10,7},{1... | collective-permute-start | bytes 24584 | tf_op jit(solution)/shard_map/ppermute | solution.py:451
  26.9 0.0 collective-permute-done.2.back_ref
  26.9 1.7 %last_pairs.1 = f32[8,256]{1,0:T(8,128)S(1)} custom-call(s32[1]{0:T(128)} %bitcast.start_ref, f32[8,256]{1,0:T(8,128)S(1)} %get-tuple-element.30.before_ref, f32[8,256]{1,0:T(8,128)S(1)} %collective-permute-done.2.back_ref, s32[16,256]{1,0:T(8,128)S(1)} %copy-done.2, f32[4,96,8,128]{3,2,1,0:T(8,128)S(1)} %get-tuple-element.23.deriv_ref, ...), custom_call_target="tpu_custom_call" | custom-call | flops 805306368 | tf_op jit(solution)/shard_map/last_pairs/pallas_call | solution.py:538
  28.7 0.7 %collective-permute-done.3 = f32[8,256]{1,0:T(8,128)S(1)} collective-permute-done((f32[8,256]{1,0:T(8,128)S(1)}, f32[8,256]{1,0:T(8,128)S(1)}, u32[]{:S(2)}, u32[]{:S(2)}) %collective-permute-start.3) | collective-permute-done | bytes 8224 | tf_op jit(solution)/shard_map/ppermute | solution.py:451
  29.4 1.7 %collective-permute-start.4 = (f32[3,256]{1,0:T(4,128)S(1)}, f32[3,256]{1,0:T(4,128)S(1)}, u32[]{:S(2)}, u32[]{:S(2)}) collective-permute-start(f32[3,256]{1,0:T(4,128)S(1)} %slice_add_fusion), channel_id=1, source_target_pairs={{0,2},{2,0},{1,3},{3,1},{4,6},{6,4},{5,7},{7,5},{8,10},{10,8},{9,1... | collective-permute-start | bytes 9224 | tf_op jit(solution)/shard_map/ppermute | solution.py:556
  31.2 1.0 %collective-permute-done.4 = f32[3,256]{1,0:T(4,128)S(1)} collective-permute-done((f32[3,256]{1,0:T(4,128)S(1)}, f32[3,256]{1,0:T(4,128)S(1)}, u32[]{:S(2)}, u32[]{:S(2)}) %collective-permute-start.4) | collective-permute-done | bytes 3104 | tf_op jit(solution)/shard_map/ppermute | solution.py:556
  32.1 0.6 %add.11 = f32[3,256]{1,0:T(4,128)} add(f32[3,256]{1,0:T(4,128)S(1)} %slice_add_fusion, f32[3,256]{1,0:T(4,128)S(1)} %collective-permute-done.4) | non-fusion elementwise | flops 768 | bytes 9216 | tf_op jit(solution)/shard_map/add | solution.py:556
  (1 shorter events, 0.0 us)
Async XLA Ops:
  0.0 6.9 %copy-start = (f32[48,16,256]{2,1,0:T(8,128)S(1)}, f32[48,16,256]{2,1,0:T(8,128)}, u32[]{:S(2)}) copy-start(f32[48,16,256]{2,1,0:T(8,128)} %dham_ref.3) | copy-start | bytes 2359300
  0.0 6.9 %copy-start.1 = (f32[48,16,256]{2,1,0:T(8,128)S(1)}, f32[48,16,256]{2,1,0:T(8,128)}, u32[]{:S(2)}) copy-start(f32[48,16,256]{2,1,0:T(8,128)} %dovl_ref.3) | copy-start | bytes 2359300
  0.0 6.9 %copy-start.2 = (s32[16,256]{1,0:T(8,128)S(1)}, s32[16,256]{1,0:T(8,128)}, u32[]{:S(2)}) copy-start(s32[16,256]{1,0:T(8,128)} %nbr_ref.9) | copy-start | bytes 49156
  0.0 7.0 %copy-start.3 = (f32[1024]{0:T(1024)S(1)}, f32[1024]{0:T(1024)}, u32[]{:S(2)}) copy-start(f32[1024]{0:T(1024)} %param.7) | copy-start | bytes 12292
  0.0 7.0 %copy-start.4 = (f32[1024]{0:T(1024)S(1)}, f32[1024]{0:T(1024)}, u32[]{:S(2)}) copy-start(f32[1024]{0:T(1024)} %param.8) | copy-start | bytes 12292
  2.2 16.9 %collective-permute-start.1 = (f32[8,304,128]{2,1,0:T(8,128)S(1)}, f32[8,304,128]{2,1,0:T(8,128)S(1)}, u32[]{:S(2)}, u32[]{:S(2)}) collective-permute-start(f32[8,304,128]{2,1,0:T(8,128)S(1)} %get-tuple-element.21), channel_id=1, source_target_pairs={{0,1},{1,0},{2,3},{3,2},{4,5},{5,4},{6,7},{7,6},{8,9},{9,8},{10,11... | collective-permute-start | bytes 3735560 | tf_op jit(solution)/shard_map/ppermute | solution.py:445
  2.4 19.1 %collective-permute-start = (f32[8,304,128]{2,1,0:T(8,128)S(1)}, f32[8,304,128]{2,1,0:T(8,128)S(1)}, u32[]{:S(2)}, u32[]{:S(2)}) collective-permute-start(f32[8,304,128]{2,1,0:T(8,128)S(1)} %get-tuple-element.20), channel_id=1, source_target_pairs={{1,4},{4,1},{5,8},{8,5},{9,12},{12,9},{3,6},{6,3},{7,10},{10,7},{1... | collective-permute-start | bytes 3735560 | tf_op jit(solution)/shard_map/ppermute | solution.py:451
  21.2 5.8 %collective-permute-start.2 = (f32[8,256]{1,0:T(8,128)S(1)}, f32[8,256]{1,0:T(8,128)S(1)}, u32[]{:S(2)}, u32[]{:S(2)}) collective-permute-start(f32[8,256]{1,0:T(8,128)S(1)} %get-tuple-element.31), channel_id=1, source_target_pairs={{0,1},{1,0},{2,3},{3,2},{4,5},{5,4},{6,7},{7,6},{8,9},{9,8},{10,11... | collective-permute-start | bytes 24584 | tf_op jit(solution)/shard_map/ppermute | solution.py:445
  24.4 5.0 %collective-permute-start.3 = (f32[8,256]{1,0:T(8,128)S(1)}, f32[8,256]{1,0:T(8,128)S(1)}, u32[]{:S(2)}, u32[]{:S(2)}) collective-permute-start(f32[8,256]{1,0:T(8,128)S(1)} %get-tuple-element.34), channel_id=1, source_target_pairs={{1,4},{4,1},{5,8},{8,5},{9,12},{12,9},{3,6},{6,3},{7,10},{10,7},{1... | collective-permute-start | bytes 24584 | tf_op jit(solution)/shard_map/ppermute | solution.py:451
  29.4 2.7 %collective-permute-start.4 = (f32[3,256]{1,0:T(4,128)S(1)}, f32[3,256]{1,0:T(4,128)S(1)}, u32[]{:S(2)}, u32[]{:S(2)}) collective-permute-start(f32[3,256]{1,0:T(4,128)S(1)} %slice_add_fusion), channel_id=1, source_target_pairs={{0,2},{2,0},{1,3},{3,1},{4,6},{6,4},{5,7},{7,5},{8,10},{10,8},{9,1... | collective-permute-start | bytes 9224 | tf_op jit(solution)/shard_map/ppermute | solution.py:556
